TPU v7x, 512 devices: a whole 4x4x16 slice. The times are simulated.
512 devices in a mesh: row: 4 (over x), col: 32 (over y, z_lo, core), layer: 4 (over z_hi).
Axes of the slice: x: 4, y: 4, z: 16 (z_hi: 4, z_lo: 4; z = z_hi * 4 + z_lo), core: 2. Of those that a mesh axis runs over, the one named last changes fastest.
Arguments:
- a_values: float32 [32, 4, 32, 128, 128], P('row', 'layer', 'col'), may hold values from 0 to 0.035
- a_index: int32 [32, 4, 32], P('row', 'layer', 'col'), may hold values from -1 to 1, as said below
- b_values: float32 [4, 32, 128, 128, 128], P('layer', 'row', 'col'), may hold values from 0 to 0.035
- b_index: int32 [4, 32, 128], P('layer', 'row', 'col'), may hold values from -1 to 15, as said below
- out_rows: int32 [4, 32, 16], P('row', 'col'), may hold values from 0 to 7, as said below
- out_cols: int32 [4, 32, 16], P('row', 'col'), may hold values from 0 to 3
Outputs:
- inflated: float32 [4, 32, 16, 128, 128], P('row', 'col', 'layer')
Inputs may be any that keep to these rules, and one draw needn't show every extreme that they name: `a_index`: in each draw the slots of one device are all live. `b_index`: in each draw the slots of one device are all live except in one block column of the slab, which has no live slot at all. The pairs (out_rows, out_cols) of one row stripe and column stripe are distinct.
All inputs are finite; a program needn't handle non-finite values.
Results may differ from a plain program's by a relative error of at most 0.0003.
Values sent between devices are 32-bit elements; how exact they have to be, the bound alone decides.
No kernel may reach another device: no remote copies, remote signals or barrier semaphores. Data moves between devices by JAX's collectives and lax.ppermute only.
A program may use at most 128 MiB of HBM per device.

v0:
```python
import jax
import jax.numpy as jnp
from jax import lax
from jax.sharding import PartitionSpec as P

KB_C = 2


def local(a_values, a_index, b_values, b_index, out_rows, out_cols):
    row_count = lax.axis_size("row")
    col_count = lax.axis_size("col")
    layer_count = lax.axis_size("layer")
    block_rows = a_values.shape[0]
    left_slots = a_values.shape[2]
    right_slots = b_values.shape[1]
    block_cols = b_values.shape[2]
    block_size = a_values.shape[3]
    inner_col = KB_C
    inner_row = col_count * inner_col // row_count
    out_total = out_rows.shape[2]
    out_share = out_total // layer_count
    right_full, right_index = (
        lax.all_gather(b_values, "row", axis=1, tiled=True),
        lax.all_gather(b_index, "row", axis=1, tiled=True),
    )
    right_panel = right_full[0]
    gathered_slots = right_index.shape[1]
    right_offset = jnp.arange(gathered_slots, dtype=jnp.int32) // right_slots * inner_row
    right_keys = jnp.where(right_index[0] >= 0, right_index[0] + right_offset[:, None], -2)
    rows_here = out_rows[0, 0]
    cols_here = out_cols[0, 0]
    left_local = a_values[:, 0]
    left_local_index = a_index[:, 0]
    empty = jnp.zeros((out_total, block_size, block_size), jnp.float32)
    left_panel, left_index = (
        lax.all_gather(left_local, "col", axis=1, tiled=True),
        lax.all_gather(left_local_index, "col", axis=1, tiled=True),
    )
    panel_slots = left_index.shape[1]
    left_offset = jnp.arange(panel_slots, dtype=jnp.int32) // left_slots * inner_col
    left_keys = jnp.where(left_index >= 0, left_index + left_offset[None, :], -1)

    def per_output(which, totals):
        left_row = lax.dynamic_index_in_dim(left_panel, rows_here[which], 0, False)
        left_row_keys = lax.dynamic_index_in_dim(left_keys, rows_here[which], 0, False)
        right_col = lax.dynamic_index_in_dim(right_panel, cols_here[which], 1, False)
        right_col_keys = lax.dynamic_index_in_dim(right_keys, cols_here[which], 1, False)
        match = (left_row_keys[:, None] == right_col_keys[None, :]).astype(jnp.float32)
        chosen = jnp.einsum("ab,axy->bxy", match, left_row, precision=lax.Precision.HIGHEST)
        term = jnp.einsum("bxy,byz->xz", chosen, right_col, precision=lax.Precision.HIGHEST)
        return totals.at[which].add(term)

    partial_value = lax.fori_loop(0, out_total, per_output, empty)
    mine = lax.psum_scatter(partial_value, "layer", scatter_dimension=0, tiled=True)
    squared = mine * mine
    offset = lax.axis_index("layer") * out_share
    cols_mine = lax.dynamic_slice_in_dim(cols_here, offset, out_share)
    column_hot = (cols_mine[:, None] == jnp.arange(block_cols, dtype=jnp.int32)[None, :]).astype(
        jnp.float32
    )
    local_sums = jnp.einsum(
        "oc,ox->cx", column_hot, jnp.sum(squared, axis=1), precision=lax.Precision.HIGHEST
    )
    layer_summed = lax.psum(local_sums, "layer")
    colsum = lax.psum(layer_summed, "row")
    denom = colsum + 1e-06
    picked_denom = jnp.einsum("oc,cx->ox", column_hot, denom, precision=lax.Precision.HIGHEST)
    scale_rows = float(row_count * block_rows * block_size)
    inflated = squared * (scale_rows / picked_denom[:, None, :])
    return inflated.reshape(1, 1, out_share, block_size, block_size)


def solution(mesh):
    in_specs = (
        P("row", "layer", "col", None, None),
        P("row", "layer", "col"),
        P("layer", "row", "col", None, None),
        P("layer", "row", "col"),
        P("row", "col", None),
        P("row", "col", None),
    )
    out_specs = P("row", "col", "layer", None, None)
    return jax.shard_map(local, mesh=mesh, in_specs=in_specs, out_specs=out_specs, check_vma=False)
```

profile of v0, /device:TPU:16, one launch (start us, length us, event | category | flops | bytes accessed | tf_op | source)
XLA Modules:
  0.0 558.4 jit_solution(4900487934249945048)
XLA Ops:
  6.5 3.2 copy.13
  10.6 37.0 %all-gather = s32[8,32,1]{0,2,1:T(1,128)S(1)} all-gather(s32[8,1,1]{0,2,1:T(1,128)S(1)} %copy-done.3), channel_id=2, replica_groups=mesh['row'=4,'col'=32,'layer'=4] {'col'}, dimensions={1}, use_global_device_ids=true | all-gather | bytes 1056 | tf_op jit(solution)/shard_map/all_gather | solution.py:37
  47.9 12.3 %all_gather.13 = s32[1,32,4]{2,0,1:T(1,128)S(1)} all-gather(s32[1,8,4]{2,0,1:T(1,128)S(1)} %copy.10), channel_id=1, replica_groups=mesh['row'=4,'col'=32,'layer'=4] {'row'}, dimensions={1}, use_global_device_ids=true | all-gather | bytes 640 | tf_op jit(solution)/shard_map/all_gather | solution.py:24
  60.2 44.9 %all-gather.5.cloned.1.call-done = f32[1,32,4,128,128]{4,3,1,2,0:T(8,128)} async-done(((f32[1,8,4,128,128]{4,3,1,2,0:T(8,128)}), f32[1,32,4,128,128]{4,3,1,2,0:T(8,128)}) %all-gather.5.cloned.1.call-update) | async-done | bytes 8388624 | tf_op jit(solution)/shard_map/all_gather | solution.py:23
  105.1 107.7 %all-gather.7.cloned.1.call-done = f32[8,32,1,128,128]{4,3,1,0,2:T(8,128)} async-done(((f32[8,1,1,128,128]{4,3,1,0,2:T(8,128)}), f32[8,32,1,128,128]{4,3,1,0,2:T(8,128)}) %all-gather.7.cloned.1.call-update) | async-done | bytes 16777232 | tf_op jit(solution)/shard_map/all_gather | solution.py:36
  212.9 249.1 %while.14 = (s32[]{:T(128)}, f32[16,128,128]{2,1,0:T(8,128)S(1)}, s32[16]{0:T(128)S(1)}, s32[8,32]{1,0:T(8,128)S(1)}, s32[16]{0:T(128)S(1)}, /*index=5*/s32[32,4...) while((s32[]{:T(128)}, f32[16,128,128]{2,1,0:T(8,128)S(1)}, ...), condition=%wide.region_2.3_spmd, body=%wide.region_0.2_spmd.sunk | while | flops 1006666752 | bytes 12716038 | solution.py:53
  215.5 1.7 dynamic-slice_bitcast_fusion.3
  219.8 2.5 fusion.56
  223.0 5.5 fusion.57
  231.0 1.7 dynamic-slice_bitcast_fusion.3
  235.3 2.5 fusion.56
  238.6 5.5 fusion.57
  246.6 1.7 dynamic-slice_bitcast_fusion.3
  250.9 2.5 fusion.56
  254.2 5.5 fusion.57
  262.2 1.7 dynamic-slice_bitcast_fusion.3
  266.5 2.5 fusion.56
  269.7 5.5 fusion.57
  277.7 1.7 dynamic-slice_bitcast_fusion.3
  282.0 2.5 fusion.56
  285.3 5.5 fusion.57
  293.3 1.7 dynamic-slice_bitcast_fusion.3
  297.6 2.5 fusion.56
  300.9 5.5 fusion.57
  313.2 2.5 fusion.56
  316.4 5.5 fusion.57
  328.7 2.5 fusion.56
  332.0 5.5 fusion.57
  344.3 2.5 fusion.56
  347.6 5.5 fusion.57
  355.6 1.7 dynamic-slice_bitcast_fusion.3
  359.9 2.5 fusion.56
  363.1 5.5 fusion.57
  375.4 2.5 fusion.56
  378.7 5.5 fusion.57
  391.0 2.5 fusion.56
  394.3 5.5 fusion.57
  406.6 2.5 fusion.56
  409.8 5.5 fusion.57
  422.2 2.5 fusion.56
  425.4 5.5 fusion.57
  437.7 2.5 fusion.56
  441.0 5.5 fusion.57
  453.3 2.5 fusion.56
  456.5 5.5 fusion.57
  463.1 63.5 %reduce-scatter.2.cloned.1.call-done = f32[4,128,128]{2,1,0:T(8,128)} async-done(((f32[16,128,128]{2,1,0:T(8,128)}), f32[4,128,128]{2,1,0:T(8,128)}) %reduce-scatter.2.cloned.1.call-update) | async-done | bytes 262160 | tf_op jit(solution)/shard_map/reduce_scatter | solution.py:54
  527.8 11.7 %psum.14 = f32[4,128]{1,0:T(4,128)S(1)} all-reduce(f32[4,128]{1,0:T(4,128)S(1)} %fusion.35), channel_id=1, replica_groups=mesh['row'=4,'col'=32,'layer'=4] {'layer'}, use_global_device_ids=true, to_apply=%region_5.6 | all-reduce | flops 512 | bytes 4096 | tf_op jit(solution)/shard_map/psum | solution.py:64
  539.6 10.4 %psum.15 = f32[4,128]{1,0:T(4,128)S(1)} all-reduce(f32[4,128]{1,0:T(4,128)S(1)} %psum.14), channel_id=1, replica_groups=mesh['row'=4,'col'=32,'layer'=4] {'row'}, use_global_device_ids=true, to_apply=%region_6.7 | all-reduce | flops 512 | bytes 4096 | tf_op jit(solution)/shard_map/psum | solution.py:65
  (120 shorter events, 52.6 us)
Async XLA Ops:
  6.5 98.6 %all-gather.5.cloned.1.call-start = ((), (), s32[]{:S(2)}) async-start(), calls=%async_computation.1 | async-start | bytes 10485760 | tf_op jit(solution)/shard_map/all_gather | solution.py:23
  9.7 0.8 copy-start.3
  9.7 38.0 %copy-start.2 = (s32[1,8,4]{1,2,0:T(4,128)S(1)}, s32[1,8,4]{1,2,0:T(4,128)}, u32[]{:S(2)}) copy-start(s32[1,8,4]{1,2,0:T(4,128)} %param.13) | copy-start | bytes 388
  9.7 203.2 %copy-start.1 = (s32[3]{0:T(128)S(1)}, s32[3]{0:T(128)}, u32[]{:S(2)}) copy-start(s32[3]{0:T(128)} %constant.125.clone.1) | copy-start | bytes 40
  9.7 203.2 %copy-start.4 = (s32[1,1,16]{2,1,0:T(1,128)S(1)}, s32[1,1,16]{2,1,0:T(1,128)}, u32[]{:S(2)}) copy-start(s32[1,1,16]{2,1,0:T(1,128)} %param.14) | copy-start | bytes 196
  9.7 203.2 %copy-start.5 = (s32[1,1,16]{2,1,0:T(1,128)S(1)}, s32[1,1,16]{2,1,0:T(1,128)}, u32[]{:S(2)}) copy-start(s32[1,1,16]{2,1,0:T(1,128)} %param.15) | copy-start | bytes 196
  9.8 203.0 %all-gather.7.cloned.1.call-start = ((), (), s32[]{:S(2)}) async-start(), calls=%async_computation.3 | async-start | bytes 17301504 | tf_op jit(solution)/shard_map/all_gather | solution.py:36
  10.5 516.1 %reduce-scatter.2.cloned.1.call-start = ((), (), s32[]{:S(2)}) async-start(), calls=%async_computation.2 | async-start | bytes 1310720 | tf_op jit(solution)/shard_map/reduce_scatter | solution.py:54
  462.1 1.0 copy-start
Sparse Core Ops, SparseCore 0:
  9.9 95.1 all-gather.4
  107.3 105.4 all-gather.6
  463.2 63.3 reduce-scatter.1
where the time goes:
time: 561 us; the launch traced here: 558 us
  waiting for transfers between devices  217 us (39%)
  matrix products  128 us (23%)
  blocking collectives  71.5 us (13%)
  loops' own time  61.7 us (11%)
  local copies, waits for them, and re-layouts  52.1 us (9%)
  other arithmetic  14.5 us (3%)
  between operations  13.2 us (2%)
    all_gather x1, waiting for transfers between devices, local(): lax.all_gather(left_local, 'col', axis=1, tiled=True)  108 us
    dot_general x16, matrix products, per_output(): jnp.einsum('bxy,byz->xz', chosen, right_col, precision=lax.Precision.HIGH...  87.9 us
    reduce_scatter x1, waiting for transfers between devices, local(): lax.psum_scatter(partial_value, 'layer', scatter_dimension=0, tiled=True)  63.5 us
    another operation x1, loops' own time, local(): partial_value = lax.fori_loop(0, out_total, per_output, empty)  61.7 us
    all_gather x1, waiting for transfers between devices, local(): lax.all_gather(b_values, 'row', axis=1, tiled=True)  44.9 us
    dot_general x16, matrix products, per_output(): jnp.einsum('ab,axy->bxy', match, left_row, precision=lax.Precision.HIGHEST)  40.1 us
    all_gather x1, blocking collectives, local(): lax.all_gather(left_local_index, 'col', axis=1, tiled=True)  37 us
    squeeze x16, local copies, waits for them, and re-layouts, per_output(): left_row = lax.dynamic_index_in_dim(left_panel, rows_here[which], 0, False)  27.7 us
  transfers between devices with their start and end apart: 3, of which 3 were waited for; matrix products, arithmetic and copies ran while one was open for 0% of the time, Pallas kernels for 0%

commit v1 on v0

v1 whole, which is shorter than its diff:
```python
import functools

import jax
import jax.numpy as jnp
from jax import lax
from jax.experimental import pallas as pl
from jax.experimental.pallas import tpu as pltpu
from jax.sharding import PartitionSpec as P

KB_C = 2
CHUNK = 4


def dot_split(left, right):
    left_high = left.astype(jnp.bfloat16)
    left_low = (left - left_high.astype(jnp.float32)).astype(jnp.bfloat16)
    right_high = right.astype(jnp.bfloat16)
    right_low = (right - right_high.astype(jnp.float32)).astype(jnp.bfloat16)
    rows, cols = left.shape[0], right.shape[1]
    full = jnp.dot(
        jnp.concatenate([left_high, left_low], axis=0),
        jnp.concatenate([right_high, right_low], axis=1),
        preferred_element_type=jnp.float32,
    )
    return full[:rows, :cols] + full[:rows, cols:] + full[rows:, :cols]


def product_kernel(outputs, pieces, slots, block_cols, size, rows_ref, cols_ref, left_keys,
                   right_keys, right_base, left_ref, *rest):
    piece_refs = rest[:pieces]
    out_refs = rest[pieces:-6]
    left_buf, right_buf, left_list, right_list, left_sem, right_sem = rest[-6:]
    block_rows = (left_ref.shape[1] - 8) // size
    piece_slots = slots // pieces

    def build(which, buf):
        row, col = rows_ref[which], cols_ref[which]

        def one(slot, count):
            key = right_keys[slot * block_cols + col]
            shard = right_base[slot] + jnp.maximum(key, 0) // KB_C
            held = left_keys[shard * block_rows + row]
            live = (key >= 0) & (held == lax.rem(jnp.maximum(key, 0), KB_C))
            left_list[buf, count] = shard
            right_list[buf, count] = slot
            return count + live.astype(jnp.int32)

        return lax.fori_loop(0, slots, one, jnp.int32(0), unroll=4)

    def issue(which, buf, count):
        row, col = rows_ref[which], cols_ref[which]

        def one(spot, carry):
            shard, slot = left_list[buf, spot], right_list[buf, spot]
            left_rows = pl.ds(pl.multiple_of(row * size, size), size)
            pltpu.make_async_copy(
                left_ref.at[shard, left_rows], left_buf.at[buf, spot], left_sem.at[buf, spot]
            ).start()
            piece = slot // piece_slots
            start = (lax.rem(slot, piece_slots) * block_cols + col) * size
            right_rows = pl.ds(pl.multiple_of(start, size), size)
            for number, ref in enumerate(piece_refs):
                @pl.when(piece == number)
                def _():
                    pltpu.make_async_copy(
                        ref.at[right_rows], right_buf.at[buf, spot], right_sem.at[buf, spot]
                    ).start()
            return carry

        lax.fori_loop(0, count, one, 0)

    def arrive(buf, count):
        def one(spot, carry):
            pltpu.make_async_copy(
                left_ref.at[0, pl.ds(0, size)], left_buf.at[buf, spot], left_sem.at[buf, spot]
            ).wait()
            pltpu.make_async_copy(
                piece_refs[0].at[pl.ds(0, size)], right_buf.at[buf, spot], right_sem.at[buf, spot]
            ).wait()
            return carry

        lax.fori_loop(0, count, one, 0)

    def multiply(buf, count):
        chunks = (count + CHUNK - 1) // CHUNK
        zero = jnp.zeros((size, size), jnp.float32)

        def clear(spot, carry):
            left_buf[buf, spot] = zero
            right_buf[buf, spot] = zero
            return carry

        lax.fori_loop(count, chunks * CHUNK, clear, 0)

        def one(chunk, total):
            left = jnp.concatenate(
                [left_buf[buf, chunk * CHUNK + part] for part in range(CHUNK)], axis=1
            )
            right = jnp.concatenate(
                [right_buf[buf, chunk * CHUNK + part] for part in range(CHUNK)], axis=0
            )
            return total + dot_split(left, right)

        return lax.fori_loop(0, chunks, one, zero)

    share = outputs // len(out_refs)
    first = build(0, 0)
    issue(0, 0, first)

    count = first
    for which in range(outputs):
        buf = which % 2
        later = jnp.int32(0)
        if which + 1 < outputs:
            later = build(which + 1, 1 - buf)
            issue(which + 1, 1 - buf, later)
        arrive(buf, count)
        out_refs[which // share][which % share] = multiply(buf, count)
        count = later


def products(name, parts, rows, cols, left_keys, right_keys, right_base, left, right_pieces):
    outputs = rows.shape[0]
    pieces = len(right_pieces)
    slots = right_base.shape[0]
    block_cols = right_keys.shape[0] // slots
    size = left.shape[2]
    smem = pl.BlockSpec(memory_space=pltpu.SMEM)
    hbm = pl.BlockSpec(memory_space=pl.ANY)
    vmem = pl.BlockSpec(memory_space=pltpu.VMEM)
    shape = jax.ShapeDtypeStruct((outputs // parts, size, size), jnp.float32)
    return pl.pallas_call(
        functools.partial(product_kernel, outputs, pieces, slots, block_cols, size),
        out_shape=[shape] * parts,
        in_specs=[smem] * 5 + [hbm] * (1 + pieces),
        out_specs=[vmem] * parts,
        scratch_shapes=[
            pltpu.VMEM((2, slots, size, size), jnp.float32),
            pltpu.VMEM((2, slots, size, size), jnp.float32),
            pltpu.SMEM((2, slots + 1), jnp.int32),
            pltpu.SMEM((2, slots + 1), jnp.int32),
            pltpu.SemaphoreType.DMA((2, slots)),
            pltpu.SemaphoreType.DMA((2, slots)),
        ],
        compiler_params=pltpu.CompilerParams(vmem_limit_bytes=24 * 1024 * 1024),
        cost_estimate=pl.CostEstimate(
            flops=outputs * 16 * 8 * size**3, bytes_accessed=outputs * 16 * 8 * size**2,
            transcendentals=0,
        ),
        name=name,
    )(rows, cols, left_keys, right_keys, right_base, left, *right_pieces)


def with_index(values, index):
    lanes = values.shape[1]
    line = jnp.zeros((lanes,), jnp.float32).at[: index.shape[0]].set(index.astype(jnp.float32))
    return jnp.concatenate([values, jnp.broadcast_to(line[None], (8, lanes))], axis=0)


def shift(value, axis, by):
    count = lax.axis_size(axis)
    return lax.ppermute(value, axis, [(i, (i + by) % count) for i in range(count)])


def local(a_values, a_index, b_values, b_index, out_rows, out_cols):
    row_count = lax.axis_size("row")
    layer_count = lax.axis_size("layer")
    block_rows = a_values.shape[0]
    right_slots = b_values.shape[1]
    block_cols = b_values.shape[2]
    size = a_values.shape[3]
    lanes = a_values.shape[4]
    out_total = out_rows.shape[2]
    share = out_total // layer_count
    half = right_slots // 2

    left_here = with_index(a_values.reshape(-1, lanes), a_index.reshape(-1))
    left = lax.all_gather(left_here, "col", axis=0, tiled=False)
    low = with_index(b_values[0, :half].reshape(-1, lanes), b_index[0, :half].reshape(-1))
    high = with_index(b_values[0, half:].reshape(-1, lanes), b_index[0, half:].reshape(-1))
    low_next, high_next = shift(low, "row", 1), shift(high, "row", 1)
    low_last, high_last = shift(low, "row", -1), shift(high, "row", -1)
    low_far, high_far = shift(low_next, "row", 1), shift(high_last, "row", -1)
    pieces = [low, high, low_next, high_next, low_last, high_last, low_far, high_far]
    away = jnp.repeat(jnp.array([0, 0, -1, -1, 1, 1, 2, 2], jnp.int32), half)

    left_keys = left[:, -1, :block_rows].astype(jnp.int32).reshape(-1)
    right_keys = jnp.concatenate([p[-1, : half * block_cols] for p in pieces]).astype(jnp.int32)
    origin = lax.rem(lax.axis_index("row") + away + row_count, row_count)
    right_base = origin * (left.shape[0] // row_count)

    me = lax.axis_index("layer")
    rows_here, cols_here = out_rows[0, 0], out_cols[0, 0]

    def quarter(array, away):
        start = lax.rem(me + away, layer_count) * share
        return lax.dynamic_slice_in_dim(array, start, share)

    def blocks(name, parts, aways):
        rows = jnp.concatenate([quarter(rows_here, away) for away in aways])
        cols = jnp.concatenate([quarter(cols_here, away) for away in aways])
        return products(
            name, parts, rows, cols, left_keys, right_keys, right_base, left, pieces
        )

    far_low, far_high = blocks("far_blocks", 2, [2])
    from_last = shift(far_low, "layer", 1)
    from_next = shift(far_high, "layer", -1)
    up, down = blocks("near_blocks", 2, [1, 3])
    up = jnp.concatenate([up[: share // 2] + from_last, up[share // 2 :]])
    down = jnp.concatenate([down[: share // 2], down[share // 2 :] + from_next])
    up_in, down_in = shift(up, "layer", 1), shift(down, "layer", -1)
    (own,) = blocks("own_blocks", 1, [0])
    mine = own + up_in + down_in

    squared = mine * mine
    cols_mine = quarter(cols_here, 0)
    column_hot = (cols_mine[:, None] == jnp.arange(block_cols, dtype=jnp.int32)[None, :]).astype(
        jnp.float32
    )
    local_sums = jnp.einsum(
        "oc,ox->cx", column_hot, jnp.sum(squared, axis=1), precision=lax.Precision.HIGHEST
    )
    colsum = lax.psum(lax.psum(local_sums, "layer"), "row")
    denom = colsum + 1e-06
    picked_denom = jnp.einsum("oc,cx->ox", column_hot, denom, precision=lax.Precision.HIGHEST)
    scale_rows = float(row_count * block_rows * size)
    inflated = squared * (scale_rows / picked_denom[:, None, :])
    return inflated.reshape(1, 1, share, size, lanes)


def solution(mesh):
    in_specs = (
        P("row", "layer", "col", None, None),
        P("row", "layer", "col"),
        P("layer", "row", "col", None, None),
        P("layer", "row", "col"),
        P("row", "col", None),
        P("row", "col", None),
    )
    out_specs = P("row", "col", "layer", None, None)
    return jax.shard_map(local, mesh=mesh, in_specs=in_specs, out_specs=out_specs, check_vma=False)
```

time: 561 us -> 247 us (0.44)
  the two profiles are of different devices: /device:TPU:16 before, /device:TPU:8 now
where the time goes in v1:
time: 247 us; the launch traced here: 246 us
  waiting for transfers between devices  87.4 us (35%)
  starting transfers between devices  50.8 us (21%)
  blocking collectives  36.7 us (15%)
  Pallas kernels  32.5 us (13%)
  local copies, waits for them, and re-layouts  17.2 us (7%)
  between operations  13.7 us (6%)
  other arithmetic  7.04 us (3%)
    ppermute x10, waiting for transfers between devices, shift(): lax.ppermute(value, axis, [(i, (i + by) % count) for i in range(count)])  60.4 us
    ppermute x10, starting transfers between devices, shift(): lax.ppermute(value, axis, [(i, (i + by) % count) for i in range(count)])  50.8 us
    psum x2, blocking collectives, local(): colsum = lax.psum(lax.psum(local_sums, 'layer'), 'row')  36.7 us
    pallas_call x3, Pallas kernels, products(): pl.pallas_call(functools.partial(product_kernel, outputs, pieces, slots,...  32.5 us
    all_gather x1, waiting for transfers between devices, local(): left = lax.all_gather(left_here, 'col', axis=0, tiled=False)  26.9 us
    unnamed x22, local copies, waits for them, and re-layouts  11.6 us
  transfers between devices with their start and end apart: 11, of which 8 were waited for; matrix products, arithmetic and copies ran while one was open for 3% of the time, Pallas kernels for 10%

profile of v1, /device:TPU:8, one launch (start us, length us, event | category | flops | bytes accessed | tf_op | source)
XLA Modules:
  0.0 245.7 jit_solution(4279838410444988767)
XLA Ops:
  6.5 0.7 convert_bitcast_fusion
  7.2 1.9 pad_maximum_fusion.2
  9.2 0.1 copy.11
  9.3 0.1 convert_element_type.37
  9.4 2.7 %fusion.18 = (f32[1,4,4,128,128]{4,3,2,1,0:T(8,128)S(1)}, f32[1,4,4,128,128]{4,3,2,1,0:T(8,128)}) fusion(f32[1,8,4,128,128]{4,3,2,1,0:T(8,128)} %param.15), kind=kLoop, calls=%fused_computation.52 | loop fusion | bytes 4194304 | tf_op jit(solution)/shard_map/slice | solution.py:180
  12.2 4.7 %collective-permute-start.3 = (f32[2056,128]{1,0:T(8,128)S(1)}, f32[2056,128]{1,0:T(8,128)S(1)}, u32[]{:S(2)}, u32[]{:S(2)}) collective-permute-start(f32[2056,128]{1,0:T(8,128)S(1)} %pad_maximum_fusion.1.rest_1_), channel_id=1, source_target_pairs={{0,384},{128,0},{256,128},{384,256},{1,385},{129,1},{257,129},{385... | collective-permute-start | bytes 3158024 | tf_op jit(solution)/shard_map/ppermute | solution.py:162
  16.9 0.1 copy.10
  17.0 0.1 convert_element_type.35
  17.1 1.3 pad_maximum_fusion.rest_0_
  18.4 1.9 collective-permute-start
  20.3 5.1 %collective-permute-start.2 = (f32[2056,128]{1,0:T(8,128)S(1)}, f32[2056,128]{1,0:T(8,128)}, u32[]{:S(2)}, u32[]{:S(2)}) collective-permute-start(f32[2056,128]{1,0:T(8,128)S(1)} %pad_maximum_fusion.rest_0_), channel_id=1, source_target_pairs={{0,384},{128,0},{256,128},{384,256},{1,385},{129,1},{257,129},{385... | collective-permute-start | bytes 3158024 | tf_op jit(solution)/shard_map/ppermute | solution.py:162
  25.5 1.9 collective-permute-start.1
  27.5 0.1 add.82
  27.7 12.8 %collective-permute-done.3.rest_5_ = f32[2056,128]{1,0:T(8,128)S(1)} collective-permute-done((f32[2056,128]{1,0:T(8,128)S(1)}, f32[2056,128]{1,0:T(8,128)S(1)}, u32[]{:S(2)}, u32[]{:S(2)}) %collective-permute-start.3) | collective-permute-done | bytes 1052704 | tf_op jit(solution)/shard_map/ppermute | solution.py:162
  40.5 5.6 %collective-permute-start.5 = (f32[2056,128]{1,0:T(8,128)S(1)}, f32[2056,128]{1,0:T(8,128)S(1)}, u32[]{:S(2)}, u32[]{:S(2)}) collective-permute-start(f32[2056,128]{1,0:T(8,128)S(1)} %collective-permute-done.3.rest_5_), channel_id=1, source_target_pairs={{0,384},{128,0},{256,128},{384,256},{1,385},{129,1},{257,129},{385... | collective-permute-start | bytes 3158024 | tf_op jit(solution)/shard_map/ppermute | solution.py:162
  46.1 0.1 fusion.6
  46.3 1.5 collective-permute-done.rest_2_
  47.8 1.9 collective-permute-start.4
  49.7 0.7 slice_bitcast_fusion.5
  50.4 12.7 %collective-permute-done.2.rest_4_ = f32[2056,128]{1,0:T(8,128)} collective-permute-done((f32[2056,128]{1,0:T(8,128)S(1)}, f32[2056,128]{1,0:T(8,128)}, u32[]{:S(2)}, u32[]{:S(2)}) %collective-permute-start.2) | collective-permute-done | bytes 1052704 | tf_op jit(solution)/shard_map/ppermute | solution.py:162
  63.0 0.7 slice_bitcast_fusion.3
  63.7 6.6 %collective-permute-done.1.rest_3_ = f32[2056,128]{1,0:T(8,128)} collective-permute-done((f32[2056,128]{1,0:T(8,128)S(1)}, f32[2056,128]{1,0:T(8,128)}, u32[]{:S(2)}, u32[]{:S(2)}) %collective-permute-start.1) | collective-permute-done | bytes 1052704 | tf_op jit(solution)/shard_map/ppermute | solution.py:162
  70.3 0.7 slice_bitcast_fusion.4
  71.0 13.5 %collective-permute-done.5.rest_7_ = f32[2056,128]{1,0:T(8,128)S(1)} collective-permute-done((f32[2056,128]{1,0:T(8,128)S(1)}, f32[2056,128]{1,0:T(8,128)S(1)}, u32[]{:S(2)}, u32[]{:S(2)}) %collective-permute-start.5) | collective-permute-done | bytes 1052704 | tf_op jit(solution)/shard_map/ppermute | solution.py:162
  84.5 1.0 copy-done.1
  85.5 5.8 %collective-permute-done.4.rest_6_ = f32[2056,128]{1,0:T(8,128)S(1)} collective-permute-done((f32[2056,128]{1,0:T(8,128)}, f32[2056,128]{1,0:T(8,128)S(1)}, u32[]{:S(2)}, u32[]{:S(2)}) %collective-permute-start.4) | collective-permute-done | bytes 1052704 | tf_op jit(solution)/shard_map/ppermute | solution.py:162
  91.3 1.0 copy-done.3
  92.4 26.9 %all-gather.3.cloned.1.call-done = f32[33024,128]{1,0:T(8,128)} async-done(((f32[1032,128]{1,0:T(8,128)}), f32[33024,128]{1,0:T(8,128)}) %all-gather.3.cloned.1.call-update) | async-done | bytes 16908304 | tf_op jit(solution)/shard_map/all_gather | solution.py:178
  119.3 1.0 fusion
  120.3 0.1 convert_element_type.33.left_keys
  120.4 5.8 %copy-done = f32[33024,128]{1,0:T(8,128)S(1)} copy-done((f32[33024,128]{1,0:T(8,128)S(1)}, f32[33024,128]{1,0:T(8,128)}, u32[]{:S(2)}) %copy-start) | copy-done | bytes 16908312
  126.2 1.2 copy-done.2
  127.4 1.2 copy-done.4
  128.6 7.8 %far_blocks.1 = (f32[2,128,128]{2,1,0:T(8,128)S(1)}, f32[2,128,128]{2,1,0:T(8,128)S(1)}) custom-call(s32[4]{0:T(128)S(1)} %get-tuple-element.63.rows_ref, s32[4]{0:T(128)S(1)} %get-tuple-element.59.cols_ref, s32[256]{0:T(256)S(1)} %convert_element_type.33.left_keys, s32[128]{0:T(128)S(1)} %convert_element_type.38.right_keys, s32[32]{0:T(128)S(1)} %fusion.15.right_base, ...), custom_call_target="tpu_custom_call" | custom-call | flops 1073741824 | bytes 8388608 | tf_op jit(solution)/shard_map/far_blocks/pallas_call | solution.py:132
  136.5 10.5 %collective-permute-start.6 = (f32[2,128,128]{2,1,0:T(8,128)S(1)}, f32[2,128,128]{2,1,0:T(8,128)S(1)}, u32[]{:S(2)}, u32[]{:S(2)}) collective-permute-start(f32[2,128,128]{2,1,0:T(8,128)S(1)} %get-tuple-element.46), channel_id=1, source_target_pairs={{0,1},{1,2},{2,3},{3,0},{4,5},{5,6},{6,7},{7,4},{8,9},{9,10},{10,1... | collective-permute-start | bytes 393224 | tf_op jit(solution)/shard_map/ppermute | solution.py:162
  147.0 1.9 collective-permute-start.8
  148.9 14.8 %near_blocks.1 = (f32[4,128,128]{2,1,0:T(8,128)S(1)}, f32[4,128,128]{2,1,0:T(8,128)S(1)}) custom-call(s32[8]{0:T(128)S(1)} %get-tuple-element.65.rows_ref, s32[8]{0:T(128)S(1)} %get-tuple-element.66.cols_ref, s32[256]{0:T(256)S(1)} %convert_element_type.33.left_keys, s32[128]{0:T(128)S(1)} %convert_element_type.38.right_keys, s32[32]{0:T(128)S(1)} %fusion.15.right_base, ...), custom_call_target="tpu_custom_call" | custom-call | flops 2147483648 | bytes 16777216 | tf_op jit(solution)/shard_map/near_blocks/pallas_call | solution.py:132
  163.9 15.3 %collective-permute-start.7 = (f32[4,128,128]{2,1,0:T(8,128)S(1)}, f32[4,128,128]{2,1,0:T(8,128)S(1)}, u32[]{:S(2)}, u32[]{:S(2)}) collective-permute-start(f32[4,128,128]{2,1,0:T(8,128)S(1)} %pad_maximum_fusion.3), channel_id=1, source_target_pairs={{0,1},{1,2},{2,3},{3,0},{4,5},{5,6},{6,7},{7,4},{8,9},{9,10},{10,1... | collective-permute-start | bytes 786440 | tf_op jit(solution)/shard_map/ppermute | solution.py:162
  179.2 1.9 collective-permute-start.9
  181.1 9.9 %own_blocks.1 = f32[4,128,128]{2,1,0:T(8,128)S(1)} custom-call(s32[4]{0:T(128)S(1)} %get-tuple-element.61.rows_ref, s32[4]{0:T(128)S(1)} %get-tuple-element.57.cols_ref, s32[256]{0:T(256)S(1)} %convert_element_type.33.left_keys, s32[128]{0:T(128)S(1)} %convert_element_type.38.right_keys, s32[32]{0:T(128)S(1)} %fusion.15.right_base, ...), custom_call_target="tpu_custom_call" | custom-call | flops 1073741824 | bytes 8388608 | tf_op jit(solution)/shard_map/own_blocks/pallas_call | solution.py:132
  191.0 7.6 %collective-permute-done.7 = f32[4,128,128]{2,1,0:T(8,128)S(1)} collective-permute-done((f32[4,128,128]{2,1,0:T(8,128)S(1)}, f32[4,128,128]{2,1,0:T(8,128)S(1)}, u32[]{:S(2)}, u32[]{:S(2)}) %collective-permute-start.7) | collective-permute-done | bytes 262176 | tf_op jit(solution)/shard_map/ppermute | solution.py:162
  198.6 0.7 copy-done.5
  199.3 0.6 copy-done.6
  200.0 0.3 fusion.2
  200.2 16.8 %psum.14 = f32[4,128]{1,0:T(4,128)S(1)} all-reduce(f32[4,128]{1,0:T(4,128)S(1)} %fusion.2), channel_id=1, replica_groups=mesh['row'=4,'col'=32,'layer'=4] {'layer'}, use_global_device_ids=true, to_apply=%region_1.0 | all-reduce | flops 512 | bytes 4096 | tf_op jit(solution)/shard_map/psum | solution.py:224
  217.0 19.9 %psum.15 = f32[4,128]{1,0:T(4,128)S(1)} all-reduce(f32[4,128]{1,0:T(4,128)S(1)} %psum.14), channel_id=1, replica_groups=mesh['row'=4,'col'=32,'layer'=4] {'row'}, use_global_device_ids=true, to_apply=%region_2.0 | all-reduce | flops 512 | bytes 4096 | tf_op jit(solution)/shard_map/psum | solution.py:224
  236.9 0.2 convolution_divide_fusion
  237.1 1.8 multiply_bitcast_fusion
  (43 shorter events, 0.7 us)
Async XLA Ops:
  6.5 2.6 %copy-start.9 = (s32[1,8,4]{1,2,0:T(4,128)S(1)}, s32[1,8,4]{1,2,0:T(4,128)}, u32[]{:S(2)}) copy-start(s32[1,8,4]{1,2,0:T(4,128)} %param.16) | copy-start | bytes 388
  6.5 112.8 %all-gather.3.cloned.1.call-start = ((), (), s32[]{:S(2)}) async-start(), calls=%async_computation | async-start | bytes 17436672 | tf_op jit(solution)/shard_map/all_gather | solution.py:178
  12.2 28.3 %collective-permute-start.3 = (f32[2056,128]{1,0:T(8,128)S(1)}, f32[2056,128]{1,0:T(8,128)S(1)}, u32[]{:S(2)}, u32[]{:S(2)}) collective-permute-start(f32[2056,128]{1,0:T(8,128)S(1)} %pad_maximum_fusion.1.rest_1_), channel_id=1, source_target_pairs={{0,384},{128,0},{256,128},{384,256},{1,385},{129,1},{257,129},{385... | collective-permute-start | bytes 3158024 | tf_op jit(solution)/shard_map/ppermute | solution.py:162
  17.0 10.4 %copy-start.10 = (s32[8]{0:T(128)S(1)}, s32[8]{0:T(128)}, u32[]{:S(2)}) copy-start(s32[8]{0:T(128)} %constant.115.clone) | copy-start | bytes 100
  17.1 10.6 %copy-start.7 = (s32[1,1,16]{2,1,0:T(1,128)S(1)}, s32[1,1,16]{2,1,0:T(1,128)}, u32[]{:S(2)}) copy-start(s32[1,1,16]{2,1,0:T(1,128)} %param.18) | copy-start | bytes 196
  17.1 29.0 %copy-start.8 = (s32[1,1,16]{2,1,0:T(1,128)S(1)}, s32[1,1,16]{2,1,0:T(1,128)}, u32[]{:S(2)}) copy-start(s32[1,1,16]{2,1,0:T(1,128)} %param.17) | copy-start | bytes 196
  18.4 29.4 %collective-permute-start = (f32[2056,128]{1,0:T(8,128)S(1)}, f32[2056,128]{1,0:T(8,128)}, u32[]{:S(2)}, u32[]{:S(2)}) collective-permute-start(f32[2056,128]{1,0:T(8,128)S(1)} %pad_maximum_fusion.rest_0_), channel_id=1, source_target_pairs={{0,128},{128,256},{256,384},{384,0},{1,129},{129,257},{257,385},{3... | collective-permute-start | bytes 3158024 | tf_op jit(solution)/shard_map/ppermute | solution.py:162
  20.3 42.7 %collective-permute-start.2 = (f32[2056,128]{1,0:T(8,128)S(1)}, f32[2056,128]{1,0:T(8,128)}, u32[]{:S(2)}, u32[]{:S(2)}) collective-permute-start(f32[2056,128]{1,0:T(8,128)S(1)} %pad_maximum_fusion.rest_0_), channel_id=1, source_target_pairs={{0,384},{128,0},{256,128},{384,256},{1,385},{129,1},{257,129},{385... | collective-permute-start | bytes 3158024 | tf_op jit(solution)/shard_map/ppermute | solution.py:162
  25.5 44.9 %collective-permute-start.1 = (f32[2056,128]{1,0:T(8,128)S(1)}, f32[2056,128]{1,0:T(8,128)}, u32[]{:S(2)}, u32[]{:S(2)}) collective-permute-start(f32[2056,128]{1,0:T(8,128)S(1)} %pad_maximum_fusion.1.rest_1_), channel_id=1, source_target_pairs={{0,128},{128,256},{256,384},{384,0},{1,129},{129,257},{257,385},{3... | collective-permute-start | bytes 3158024 | tf_op jit(solution)/shard_map/ppermute | solution.py:162
  40.5 44.0 %collective-permute-start.5 = (f32[2056,128]{1,0:T(8,128)S(1)}, f32[2056,128]{1,0:T(8,128)S(1)}, u32[]{:S(2)}, u32[]{:S(2)}) collective-permute-start(f32[2056,128]{1,0:T(8,128)S(1)} %collective-permute-done.3.rest_5_), channel_id=1, source_target_pairs={{0,384},{128,0},{256,128},{384,256},{1,385},{129,1},{257,129},{385... | collective-permute-start | bytes 3158024 | tf_op jit(solution)/shard_map/ppermute | solution.py:162
  47.8 43.5 %collective-permute-start.4 = (f32[2056,128]{1,0:T(8,128)}, f32[2056,128]{1,0:T(8,128)S(1)}, u32[]{:S(2)}, u32[]{:S(2)}) collective-permute-start(f32[2056,128]{1,0:T(8,128)} %collective-permute-done.rest_2_), channel_id=1, source_target_pairs={{0,128},{128,256},{256,384},{384,0},{1,129},{129,257},{257,385},{3... | collective-permute-start | bytes 3158024 | tf_op jit(solution)/shard_map/ppermute | solution.py:162
  84.5 1.0 copy-start.1
  91.3 1.0 copy-start.3
  120.4 5.8 %copy-start = (f32[33024,128]{1,0:T(8,128)S(1)}, f32[33024,128]{1,0:T(8,128)}, u32[]{:S(2)}) copy-start(f32[33024,128]{1,0:T(8,128)} %all-gather.3.cloned.1.call-done) | copy-start | bytes 50724868
  126.2 1.2 copy-start.2
  127.4 1.2 copy-start.4
  136.5 27.3 %collective-permute-start.6 = (f32[2,128,128]{2,1,0:T(8,128)S(1)}, f32[2,128,128]{2,1,0:T(8,128)S(1)}, u32[]{:S(2)}, u32[]{:S(2)}) collective-permute-start(f32[2,128,128]{2,1,0:T(8,128)S(1)} %get-tuple-element.46), channel_id=1, source_target_pairs={{0,1},{1,2},{2,3},{3,0},{4,5},{5,6},{6,7},{7,4},{8,9},{9,10},{10,1... | collective-permute-start | bytes 393224 | tf_op jit(solution)/shard_map/ppermute | solution.py:162
  147.0 32.1 %collective-permute-start.8 = (f32[2,128,128]{2,1,0:T(8,128)S(1)}, f32[2,128,128]{2,1,0:T(8,128)S(1)}, u32[]{:S(2)}, u32[]{:S(2)}) collective-permute-start(f32[2,128,128]{2,1,0:T(8,128)S(1)} %get-tuple-element.48), channel_id=1, source_target_pairs={{0,3},{1,0},{2,1},{3,2},{4,7},{5,4},{6,5},{7,6},{8,11},{9,8},{10,9... | collective-permute-start | bytes 393224 | tf_op jit(solution)/shard_map/ppermute | solution.py:162
  163.9 34.7 %collective-permute-start.7 = (f32[4,128,128]{2,1,0:T(8,128)S(1)}, f32[4,128,128]{2,1,0:T(8,128)S(1)}, u32[]{:S(2)}, u32[]{:S(2)}) collective-permute-start(f32[4,128,128]{2,1,0:T(8,128)S(1)} %pad_maximum_fusion.3), channel_id=1, source_target_pairs={{0,1},{1,2},{2,3},{3,0},{4,5},{5,6},{6,7},{7,4},{8,9},{9,10},{10,1... | collective-permute-start | bytes 786440 | tf_op jit(solution)/shard_map/ppermute | solution.py:162
  179.2 19.4 %collective-permute-start.9 = (f32[4,128,128]{2,1,0:T(8,128)S(1)}, f32[4,128,128]{2,1,0:T(8,128)S(1)}, u32[]{:S(2)}, u32[]{:S(2)}) collective-permute-start(f32[4,128,128]{2,1,0:T(8,128)S(1)} %pad_maximum_fusion.4), channel_id=1, source_target_pairs={{0,3},{1,0},{2,1},{3,2},{4,7},{5,4},{6,5},{7,6},{8,11},{9,8},{10,9... | collective-permute-start | bytes 786440 | tf_op jit(solution)/shard_map/ppermute | solution.py:162
  198.6 0.7 copy-start.5
  199.3 0.7 copy-start.6
Sparse Core Ops, SparseCore 0:
  9.5 109.7 all-gather.2

commit v2 on v1

v2 whole, which is shorter than its diff:
```python
import functools

import jax
import jax.numpy as jnp
from jax import lax
from jax.experimental import pallas as pl
from jax.experimental.pallas import tpu as pltpu
from jax.sharding import PartitionSpec as P

KB_C = 2
CHUNK = 8


def halves(value):
    high = value.astype(jnp.bfloat16)
    return high, (value - high.astype(jnp.float32)).astype(jnp.bfloat16)


def list_kernel(outputs, slots, block_cols, block_rows, rows_ref, cols_ref, left_keys, right_keys,
                right_base, counts, left_list, right_list):
    def per_output(which, carry):
        row, col = rows_ref[which], cols_ref[which]

        def one(slot, count):
            key = right_keys[slot * block_cols + col]
            inner = jnp.maximum(key, 0)
            place = (right_base[slot] + inner // KB_C) * block_rows + row
            live = (key >= 0) & (left_keys[place] == lax.rem(inner, KB_C))
            spot = which * slots + count
            left_list[spot] = place
            right_list[spot] = slot * block_cols + col
            return count + live.astype(jnp.int32)

        counts[which] = lax.fori_loop(0, slots, one, jnp.int32(0), unroll=8)
        return carry

    lax.fori_loop(0, outputs, per_output, 0)


def match_lists(rows, cols, left_keys, right_keys, right_base, block_rows):
    outputs, slots = rows.shape[0], right_base.shape[0]
    smem = pl.BlockSpec(memory_space=pltpu.SMEM)
    lists = jax.ShapeDtypeStruct((outputs * slots,), jnp.int32)
    return pl.pallas_call(
        functools.partial(
            list_kernel, outputs, slots, right_keys.shape[0] // slots, block_rows
        ),
        out_shape=[jax.ShapeDtypeStruct((outputs,), jnp.int32), lists, lists],
        in_specs=[smem] * 5,
        out_specs=[smem] * 3,
        name="match_lists",
    )(rows, cols, left_keys, right_keys, right_base)


def split_kernel(*refs):
    pieces, panel = refs[:-1], refs[-1]
    size = panel.shape[1]
    blocks = panel.shape[0] // len(pieces)
    for number, piece in enumerate(pieces):
        def one(block, carry):
            start = pl.multiple_of(block * size, size)
            high, low = halves(piece[pl.ds(start, size), :])
            panel[number * blocks + block, :, :size] = high
            panel[number * blocks + block, :, size:] = low
            return carry

        lax.fori_loop(0, blocks, one, 0)


def split_panel(pieces, blocks, size):
    vmem = pl.BlockSpec(memory_space=pltpu.VMEM)
    return pl.pallas_call(
        split_kernel,
        out_shape=jax.ShapeDtypeStruct((blocks * len(pieces), size, 2 * size), jnp.bfloat16),
        in_specs=[vmem] * len(pieces),
        out_specs=vmem,
        compiler_params=pltpu.CompilerParams(vmem_limit_bytes=32 * 1024 * 1024),
        name="split_panel",
    )(*pieces)


def product_kernel(first, outputs, slots, counts, left_list, right_list, left_ref, panel, *rest):
    out_refs = rest[:-2]
    left_buf, left_sem = rest[-2:]
    size = left_ref.shape[1]

    def issue(which):
        buf = which % 2

        def one(spot, carry):
            place = left_list[(first + which) * slots + spot]
            pltpu.make_async_copy(
                left_ref.at[place], left_buf.at[buf, spot], left_sem.at[buf, spot]
            ).start()
            return carry

        lax.fori_loop(0, counts[first + which], one, 0)

    def multiply(which):
        buf, count = which % 2, counts[first + which]
        zero = jnp.zeros((size, size), jnp.float32)
        chunks = (count + CHUNK - 1) // CHUNK

        def arrive(spot, carry):
            pltpu.make_async_copy(
                left_ref.at[0], left_buf.at[buf, spot], left_sem.at[buf, spot]
            ).wait()
            return carry

        def clear(spot, carry):
            left_buf[buf, spot] = zero
            return carry

        def one(chunk, total):
            base = chunk * CHUNK
            left, right = [], []
            for part in range(CHUNK):
                spot = base + part
                block = right_list[(first + which) * slots + spot]
                right.append(panel[jnp.where(spot < count, block, 0)])
                left.append(left_buf[buf, spot])
            high, low = halves(jnp.concatenate(left, axis=1))
            both = jnp.dot(
                jnp.concatenate([high, low], axis=0), jnp.concatenate(right, axis=0),
                preferred_element_type=jnp.float32,
            )
            return total + (both[:size, :size] + both[:size, size:] + both[size:, :size])

        lax.fori_loop(0, count, arrive, 0)
        lax.fori_loop(count, chunks * CHUNK, clear, 0)
        return lax.fori_loop(0, chunks, one, zero)

    share = outputs // len(out_refs)
    issue(0)
    for which in range(outputs):
        if which + 1 < outputs:
            issue(which + 1)
        out_refs[which // share][which % share] = multiply(which)


def products(name, parts, first, outputs, lists, left, panel):
    size = left.shape[1]
    slots = lists[1].shape[0] // lists[0].shape[0]
    smem = pl.BlockSpec(memory_space=pltpu.SMEM)
    vmem = pl.BlockSpec(memory_space=pltpu.VMEM)
    shape = jax.ShapeDtypeStruct((outputs // parts, size, size), jnp.float32)
    return pl.pallas_call(
        functools.partial(product_kernel, first, outputs, slots),
        out_shape=[shape] * parts,
        in_specs=[smem] * 3 + [pl.BlockSpec(memory_space=pl.ANY), vmem],
        out_specs=[vmem] * parts,
        scratch_shapes=[
            pltpu.VMEM((2, slots, size, size), jnp.float32),
            pltpu.SemaphoreType.DMA((2, slots)),
        ],
        compiler_params=pltpu.CompilerParams(vmem_limit_bytes=42 * 1024 * 1024),
        cost_estimate=pl.CostEstimate(
            flops=outputs * 16 * 8 * size**3, bytes_accessed=outputs * 16 * 4 * size**2,
            transcendentals=0,
        ),
        name=name,
    )(*lists, left, panel)


def with_index(values, index):
    lanes = values.shape[1]
    line = jnp.zeros((lanes,), jnp.float32).at[: index.shape[0]].set(index.astype(jnp.float32))
    return jnp.concatenate([values, jnp.broadcast_to(line[None], (8, lanes))], axis=0)


def shift(value, axis, by):
    count = lax.axis_size(axis)
    return lax.ppermute(value, axis, [(i, (i + by) % count) for i in range(count)])


def local(a_values, a_index, b_values, b_index, out_rows, out_cols):
    row_count = lax.axis_size("row")
    layer_count = lax.axis_size("layer")
    block_rows = a_values.shape[0]
    right_slots = b_values.shape[1]
    block_cols = b_values.shape[2]
    size = a_values.shape[3]
    lanes = a_values.shape[4]
    out_total = out_rows.shape[2]
    share = out_total // layer_count
    half = right_slots // 2

    left = lax.all_gather(a_values.reshape(block_rows, size, lanes), "col", axis=0, tiled=True)
    low = with_index(b_values[0, :half].reshape(-1, lanes), b_index[0, :half].reshape(-1))
    high = with_index(b_values[0, half:].reshape(-1, lanes), b_index[0, half:].reshape(-1))
    low_next, high_next = shift(low, "row", 1), shift(high, "row", 1)
    low_last, high_last = shift(low, "row", -1), shift(high, "row", -1)
    low_far, high_far = shift(low_next, "row", 1), shift(high_last, "row", -1)
    pieces = [low, high, low_next, high_next, low_last, high_last, low_far, high_far]
    away = jnp.repeat(jnp.array([0, 0, -1, -1, 1, 1, 2, 2], jnp.int32), half)

    left_index = a_index.reshape(-1) + low_next[-1, -1].astype(jnp.int32)
    left_keys = lax.all_gather(left_index, "col", axis=0, tiled=True)
    right_keys = jnp.concatenate([p[-1, : half * block_cols] for p in pieces]).astype(jnp.int32)
    origin = lax.rem(lax.axis_index("row") + away + row_count, row_count)
    right_base = origin * (left_keys.shape[0] // block_rows // row_count)

    me = lax.axis_index("layer")
    rows_here, cols_here = out_rows[0, 0], out_cols[0, 0]

    def quarter(array, away):
        start = lax.rem(me + away, layer_count) * share
        return lax.dynamic_slice_in_dim(array, start, share)

    order = [2, 1, 3, 0]
    rows = jnp.concatenate([quarter(rows_here, away) for away in order])
    cols = jnp.concatenate([quarter(cols_here, away) for away in order])
    lists = match_lists(rows, cols, left_keys, right_keys, right_base, block_rows)
    panel = split_panel(pieces, half * block_cols, size)

    far_low, far_high = products("far_blocks", 2, 0, share, lists, left, panel)
    from_last = shift(far_low, "layer", 1)
    from_next = shift(far_high, "layer", -1)
    up, down = products("near_blocks", 2, share, 2 * share, lists, left, panel)
    up = jnp.concatenate([up[: share // 2] + from_last, up[share // 2 :]])
    down = jnp.concatenate([down[: share // 2], down[share // 2 :] + from_next])
    up_in, down_in = shift(up, "layer", 1), shift(down, "layer", -1)
    (own,) = products("own_blocks", 1, 3 * share, share, lists, left, panel)
    mine = own + up_in + down_in

    squared = mine * mine
    cols_mine = quarter(cols_here, 0)
    column_hot = (cols_mine[:, None] == jnp.arange(block_cols, dtype=jnp.int32)[None, :]).astype(
        jnp.float32
    )
    local_sums = jnp.einsum(
        "oc,ox->cx", column_hot, jnp.sum(squared, axis=1), precision=lax.Precision.HIGHEST
    )
    colsum = lax.psum(lax.psum(local_sums, "layer"), "row")
    denom = colsum + 1e-06
    picked_denom = jnp.einsum("oc,cx->ox", column_hot, denom, precision=lax.Precision.HIGHEST)
    scale_rows = float(row_count * block_rows * size)
    inflated = squared * (scale_rows / picked_denom[:, None, :])
    return inflated.reshape(1, 1, share, size, lanes)


def solution(mesh):
    in_specs = (
        P("row", "layer", "col", None, None),
        P("row", "layer", "col"),
        P("layer", "row", "col", None, None),
        P("layer", "row", "col"),
        P("row", "col", None),
        P("row", "col", None),
    )
    out_specs = P("row", "col", "layer", None, None)
    return jax.shard_map(local, mesh=mesh, in_specs=in_specs, out_specs=out_specs, check_vma=False)
```

time: 247 us -> 219 us (0.89)
  the two profiles are of different devices: /device:TPU:8 before, /device:TPU:16 now
where the time goes in v2:
time: 219 us; the launch traced here: 218 us
  waiting for transfers between devices  61.7 us (28%)
  blocking collectives  52 us (24%)
  starting transfers between devices  39.1 us (18%)
  Pallas kernels  29.1 us (13%)
  local copies, waits for them, and re-layouts  15.4 us (7%)
  between operations  15 us (7%)
  other arithmetic  4.98 us (2%)
    ppermute x10, waiting for transfers between devices, shift(): lax.ppermute(value, axis, [(i, (i + by) % count) for i in range(count)])  45.5 us
    ppermute x10, starting transfers between devices, shift(): lax.ppermute(value, axis, [(i, (i + by) % count) for i in range(count)])  39.1 us
    psum x2, blocking collectives, local(): colsum = lax.psum(lax.psum(local_sums, 'layer'), 'row')  35.8 us
    pallas_call x3, Pallas kernels, products(): pl.pallas_call(functools.partial(product_kernel, first, outputs, slots),...  18.5 us
    all_gather x1, blocking collectives, local(): left_keys = lax.all_gather(left_index, 'col', axis=0, tiled=True)  16.1 us
    all_gather x1, waiting for transfers between devices, local(): lax.all_gather(a_values.reshape(block_rows, size, lanes), 'col', axis=0,...  15.5 us
    unnamed x20, local copies, waits for them, and re-layouts  7.91 us
    pallas_call x1, Pallas kernels, match_lists(): pl.pallas_call(functools.partial(list_kernel, outputs, slots, right_keys....  6.1 us
  transfers between devices with their start and end apart: 11, of which 9 were waited for; matrix products, arithmetic and copies ran while one was open for 6% of the time, Pallas kernels for 11%

profile of v2, /device:TPU:16, one launch (start us, length us, event | category | flops | bytes accessed | tf_op | source)
XLA Modules:
  0.0 217.6 jit_solution(15487115057132144293)
XLA Ops:
  6.5 0.7 all-gather.4.cloned.1.call-update
  7.3 0.8 slice_convert_fusion
  8.3 2.7 %fusion.17 = (f32[1,4,4,128,128]{4,3,2,1,0:T(8,128)}, f32[1,4,4,128,128]{4,3,2,1,0:T(8,128)S(1)}) fusion(f32[1,8,4,128,128]{4,3,2,1,0:T(8,128)} %param.13), kind=kLoop, calls=%fused_computation.49 | loop fusion | bytes 4194304 | tf_op jit(solution)/shard_map/slice | solution.py:190
  11.0 3.4 %collective-permute-start = (f32[2056,128]{1,0:T(8,128)S(1)}, f32[2056,128]{1,0:T(8,128)S(1)}, u32[]{:S(2)}, u32[]{:S(2)}) collective-permute-start(f32[2056,128]{1,0:T(8,128)S(1)} %pad_maximum_fusion.refs_0_), channel_id=1, source_target_pairs={{0,128},{128,256},{256,384},{384,0},{1,129},{129,257},{257,385},{3... | collective-permute-start | bytes 3158024 | tf_op jit(solution)/shard_map/ppermute | solution.py:173
  14.5 0.1 copy.15
  14.7 1.3 pad_maximum_fusion.1.refs_1_
  16.0 3.7 %collective-permute-start.3 = (f32[2056,128]{1,0:T(8,128)S(1)}, f32[2056,128]{1,0:T(8,128)}, u32[]{:S(2)}, u32[]{:S(2)}) collective-permute-start(f32[2056,128]{1,0:T(8,128)S(1)} %pad_maximum_fusion.1.refs_1_), channel_id=1, source_target_pairs={{0,384},{128,0},{256,128},{384,256},{1,385},{129,1},{257,129},{385... | collective-permute-start | bytes 3158024 | tf_op jit(solution)/shard_map/ppermute | solution.py:173
  19.7 3.5 %collective-permute-start.2 = (f32[2056,128]{1,0:T(8,128)S(1)}, f32[2056,128]{1,0:T(8,128)}, u32[]{:S(2)}, u32[]{:S(2)}) collective-permute-start(f32[2056,128]{1,0:T(8,128)S(1)} %pad_maximum_fusion.refs_0_), channel_id=1, source_target_pairs={{0,384},{128,0},{256,128},{384,256},{1,385},{129,1},{257,129},{385... | collective-permute-start | bytes 3158024 | tf_op jit(solution)/shard_map/ppermute | solution.py:173
  23.1 2.4 %collective-permute-start.1 = (f32[2056,128]{1,0:T(8,128)S(1)}, f32[2056,128]{1,0:T(8,128)}, u32[]{:S(2)}, u32[]{:S(2)}) collective-permute-start(f32[2056,128]{1,0:T(8,128)S(1)} %pad_maximum_fusion.1.refs_1_), channel_id=1, source_target_pairs={{0,128},{128,256},{256,384},{384,0},{1,129},{129,257},{257,385},{3... | collective-permute-start | bytes 3158024 | tf_op jit(solution)/shard_map/ppermute | solution.py:173
  25.7 0.5 fusion.14.right_base
  26.4 1.3 dynamic-slice.22
  28.3 0.7 pad_add_fusion
  29.0 11.3 %collective-permute-done.refs_2_ = f32[2056,128]{1,0:T(8,128)S(1)} collective-permute-done((f32[2056,128]{1,0:T(8,128)S(1)}, f32[2056,128]{1,0:T(8,128)S(1)}, u32[]{:S(2)}, u32[]{:S(2)}) %collective-permute-start) | collective-permute-done | bytes 1052704 | tf_op jit(solution)/shard_map/ppermute | solution.py:173
  40.3 0.7 slice.86
  41.6 2.2 %collective-permute-start.4 = (f32[2056,128]{1,0:T(8,128)S(1)}, f32[2056,128]{1,0:T(8,128)}, u32[]{:S(2)}, u32[]{:S(2)}) collective-permute-start(f32[2056,128]{1,0:T(8,128)S(1)} %collective-permute-done.refs_2_), channel_id=1, source_target_pairs={{0,128},{128,256},{256,384},{384,0},{1,129},{129,257},{257,385},{3... | collective-permute-start | bytes 3158024 | tf_op jit(solution)/shard_map/ppermute | solution.py:173
  43.8 0.4 collective-permute-done.3.refs_5_
  44.2 4.9 %collective-permute-start.5 = (f32[2056,128]{1,0:T(8,128)}, f32[2056,128]{1,0:T(8,128)}, u32[]{:S(2)}, u32[]{:S(2)}) collective-permute-start(f32[2056,128]{1,0:T(8,128)} %collective-permute-done.3.refs_5_), channel_id=1, source_target_pairs={{0,384},{128,0},{256,128},{384,256},{1,385},{129,1},{257,129},{385... | collective-permute-start | bytes 3158024 | tf_op jit(solution)/shard_map/ppermute | solution.py:173
  49.1 0.1 bitcast_dynamic-update-slice_fusion
  49.2 16.1 %all-reduce.2.left_keys = s32[256]{0:T(256)} all-reduce(s32[256]{0:T(256)S(1)} %bitcast_dynamic-update-slice_fusion), channel_id=2, replica_groups=mesh['row'=4,'col'=32,'layer'=4] {'col'}, use_global_device_ids=true, to_apply=%add.2 | all-reduce | flops 256 | bytes 2048 | tf_op jit(solution)/shard_map/all_gather | solution.py:198
  65.3 0.7 slice_bitcast_fusion.2
  66.0 0.8 collective-permute-done.2.refs_4_
  66.7 0.7 slice_bitcast_fusion.3
  67.4 0.7 slice_bitcast_fusion.4
  68.1 16.3 %collective-permute-done.4.refs_6_ = f32[2056,128]{1,0:T(8,128)} collective-permute-done((f32[2056,128]{1,0:T(8,128)S(1)}, f32[2056,128]{1,0:T(8,128)}, u32[]{:S(2)}, u32[]{:S(2)}) %collective-permute-start.4) | collective-permute-done | bytes 1052704 | tf_op jit(solution)/shard_map/ppermute | solution.py:173
  84.4 0.7 slice_bitcast_fusion.1
  85.0 2.8 %collective-permute-done.5.refs_7_ = f32[2056,128]{1,0:T(8,128)} collective-permute-done((f32[2056,128]{1,0:T(8,128)}, f32[2056,128]{1,0:T(8,128)}, u32[]{:S(2)}, u32[]{:S(2)}) %collective-permute-start.5) | collective-permute-done | bytes 1052704 | tf_op jit(solution)/shard_map/ppermute | solution.py:173
  87.8 0.7 slice_bitcast_fusion
  88.6 0.6 convert_element_type.28.right_keys
  89.1 6.1 %match_lists.1 = (s32[16]{0:T(128)}, s32[512]{0:T(512)}, s32[512]{0:T(512)}) custom-call(s32[16]{0:T(128)} %get-tuple-element.59.rows_ref, s32[16]{0:T(128)} %get-tuple-element.60.cols_ref, s32[256]{0:T(256)} %all-reduce.2.left_keys, s32[128]{0:T(128)} %convert_element_type.28.right_keys, s32[32]{0:T(128)} %fusion.14.right_base), custom_call_target="tpu_custom_call" | custom-call | tf_op jit(solution)/shard_map/match_lists/pallas_call | solution.py:44
  95.3 4.5 %split_panel.1.panel = bf16[128,128,256]{2,1,0:T(8,128)(2,1)S(1)} custom-call(f32[2056,128]{1,0:T(8,128)S(1)} %pad_maximum_fusion.refs_0_, f32[2056,128]{1,0:T(8,128)S(1)} %pad_maximum_fusion.1.refs_1_, f32[2056,128]{1,0:T(8,128)S(1)} %collective-permute-done.refs_2_, f32[2056,128]{1,0:T(8,128)} %collective-permute-done.1.refs_3_, ...), custom_call_target="tpu_custom_call" | custom-call | tf_op jit(solution)/shard_map/split_panel/pallas_call | solution.py:72
  99.8 3.2 %copy-done = bf16[128,128,256]{2,1,0:T(8,128)(2,1)} copy-done((bf16[128,128,256]{2,1,0:T(8,128)(2,1)}, bf16[128,128,256]{2,1,0:T(8,128)(2,1)S(1)}, u32[]{:S(2)}) %copy-start) | copy-done | bytes 8388632
  103.0 15.5 %all-gather.4.cloned.1.call-done = f32[256,1,1,128,128]{4,3,2,1,0:T(8,128)} async-done(((f32[8,1,1,128,128]{4,3,2,1,0:T(8,128)}), f32[256,1,1,128,128]{4,3,2,1,0:T(8,128)}) %all-gather.4.cloned.1.call-update) | async-done | bytes 16777232 | tf_op jit(solution)/shard_map/all_gather | solution.py:188
  118.5 3.4 %copy-done.1 = bf16[128,128,256]{2,1,0:T(8,128)(2,1)S(1)} copy-done((bf16[128,128,256]{2,1,0:T(8,128)(2,1)S(1)}, bf16[128,128,256]{2,1,0:T(8,128)(2,1)}, u32[]{:S(2)}) %copy-start.1) | copy-done | bytes 8388632
  121.8 5.1 %far_blocks.1 = (f32[2,128,128]{2,1,0:T(8,128)S(1)}, f32[2,128,128]{2,1,0:T(8,128)S(1)}) custom-call(s32[16]{0:T(128)S(1)} %copy-done.4, s32[512]{0:T(512)S(1)} %copy-done.2, s32[512]{0:T(512)S(1)} %copy-done.3, f32[256,128,128]{2,1,0:T(8,128)} %bitcast.38, bf16[128,128,256]{2,1,0:T(8,128)(2,1)S(1)} %copy-done.1), custom_call_target="tpu_custom_call" | custom-call | flops 1073741824 | bytes 4194304 | tf_op jit(solution)/shard_map/far_blocks/pallas_call | solution.py:147
  126.9 7.6 %collective-permute-start.6 = (f32[2,128,128]{2,1,0:T(8,128)S(1)}, f32[2,128,128]{2,1,0:T(8,128)S(1)}, u32[]{:S(2)}, u32[]{:S(2)}) collective-permute-start(f32[2,128,128]{2,1,0:T(8,128)S(1)} %get-tuple-element.40), channel_id=1, source_target_pairs={{0,1},{1,2},{2,3},{3,0},{4,5},{5,6},{6,7},{7,4},{8,9},{9,10},{10,1... | collective-permute-start | bytes 393224 | tf_op jit(solution)/shard_map/ppermute | solution.py:173
  134.5 2.8 %collective-permute-start.8 = (f32[2,128,128]{2,1,0:T(8,128)S(1)}, f32[2,128,128]{2,1,0:T(8,128)S(1)}, u32[]{:S(2)}, u32[]{:S(2)}) collective-permute-start(f32[2,128,128]{2,1,0:T(8,128)S(1)} %get-tuple-element.42), channel_id=1, source_target_pairs={{0,3},{1,0},{2,1},{3,2},{4,7},{5,4},{6,5},{7,6},{8,11},{9,8},{10,9... | collective-permute-start | bytes 393224 | tf_op jit(solution)/shard_map/ppermute | solution.py:173
  137.4 8.3 %near_blocks.1 = (f32[4,128,128]{2,1,0:T(8,128)S(1)}, f32[4,128,128]{2,1,0:T(8,128)S(1)}) custom-call(s32[16]{0:T(128)S(1)} %copy-done.4, s32[512]{0:T(512)S(1)} %copy-done.2, s32[512]{0:T(512)S(1)} %copy-done.3, f32[256,128,128]{2,1,0:T(8,128)} %bitcast.39, bf16[128,128,256]{2,1,0:T(8,128)(2,1)S(1)} %copy-done.1), custom_call_target="tpu_custom_call" | custom-call | flops 2147483648 | bytes 8388608 | tf_op jit(solution)/shard_map/near_blocks/pallas_call | solution.py:147
  145.8 5.5 %collective-permute-start.7 = (f32[4,128,128]{2,1,0:T(8,128)S(1)}, f32[4,128,128]{2,1,0:T(8,128)S(1)}, u32[]{:S(2)}, u32[]{:S(2)}) collective-permute-start(f32[4,128,128]{2,1,0:T(8,128)S(1)} %pad_maximum_fusion.2), channel_id=1, source_target_pairs={{0,1},{1,2},{2,3},{3,0},{4,5},{5,6},{6,7},{7,4},{8,9},{9,10},{10,1... | collective-permute-start | bytes 786440 | tf_op jit(solution)/shard_map/ppermute | solution.py:173
  151.3 2.7 %collective-permute-done.8 = f32[2,128,128]{2,1,0:T(8,128)S(1)} collective-permute-done((f32[2,128,128]{2,1,0:T(8,128)S(1)}, f32[2,128,128]{2,1,0:T(8,128)S(1)}, u32[]{:S(2)}, u32[]{:S(2)}) %collective-permute-start.8) | collective-permute-done | bytes 131104 | tf_op jit(solution)/shard_map/ppermute | solution.py:173
  154.0 3.2 %collective-permute-start.9 = (f32[4,128,128]{2,1,0:T(8,128)S(1)}, f32[4,128,128]{2,1,0:T(8,128)S(1)}, u32[]{:S(2)}, u32[]{:S(2)}) collective-permute-start(f32[4,128,128]{2,1,0:T(8,128)S(1)} %pad_maximum_fusion.3), channel_id=1, source_target_pairs={{0,3},{1,0},{2,1},{3,2},{4,7},{5,4},{6,5},{7,6},{8,11},{9,8},{10,9... | collective-permute-start | bytes 786440 | tf_op jit(solution)/shard_map/ppermute | solution.py:173
  157.2 5.1 %own_blocks.1 = f32[4,128,128]{2,1,0:T(8,128)S(1)} custom-call(s32[16]{0:T(128)S(1)} %copy-done.4, s32[512]{0:T(512)S(1)} %copy-done.2, s32[512]{0:T(512)S(1)} %copy-done.3, f32[256,128,128]{2,1,0:T(8,128)} %bitcast.40, bf16[128,128,256]{2,1,0:T(8,128)(2,1)S(1)} %copy-done.1), custom_call_target="tpu_custom_call" | custom-call | flops 1073741824 | bytes 4194304 | tf_op jit(solution)/shard_map/own_blocks/pallas_call | solution.py:147
  162.4 4.0 %collective-permute-done.7 = f32[4,128,128]{2,1,0:T(8,128)S(1)} collective-permute-done((f32[4,128,128]{2,1,0:T(8,128)S(1)}, f32[4,128,128]{2,1,0:T(8,128)S(1)}, u32[]{:S(2)}, u32[]{:S(2)}) %collective-permute-start.7) | collective-permute-done | bytes 262176 | tf_op jit(solution)/shard_map/ppermute | solution.py:173
  166.3 7.4 %collective-permute-done.9 = f32[4,128,128]{2,1,0:T(8,128)S(1)} collective-permute-done((f32[4,128,128]{2,1,0:T(8,128)S(1)}, f32[4,128,128]{2,1,0:T(8,128)S(1)}, u32[]{:S(2)}, u32[]{:S(2)}) %collective-permute-start.9) | collective-permute-done | bytes 262176 | tf_op jit(solution)/shard_map/ppermute | solution.py:173
  173.8 0.3 fusion.1
  174.0 14.5 %psum.14 = f32[4,128]{1,0:T(4,128)S(1)} all-reduce(f32[4,128]{1,0:T(4,128)S(1)} %fusion.1), channel_id=1, replica_groups=mesh['row'=4,'col'=32,'layer'=4] {'layer'}, use_global_device_ids=true, to_apply=%region_1.0 | all-reduce | flops 512 | bytes 4096 | tf_op jit(solution)/shard_map/psum | solution.py:234
  188.6 21.3 %psum.15 = f32[4,128]{1,0:T(4,128)S(1)} all-reduce(f32[4,128]{1,0:T(4,128)S(1)} %psum.14), channel_id=1, replica_groups=mesh['row'=4,'col'=32,'layer'=4] {'row'}, use_global_device_ids=true, to_apply=%region_2.0 | all-reduce | flops 512 | bytes 4096 | tf_op jit(solution)/shard_map/psum | solution.py:234
  209.9 0.2 convolution_divide_fusion
  210.0 0.8 multiply_bitcast_fusion
  (40 shorter events, 0.9 us)
Async XLA Ops:
  6.5 111.9 %all-gather.4.cloned.1.call-start = ((), (), s32[]{:S(2)}) async-start(), calls=%async_computation | async-start | bytes 17301504 | tf_op jit(solution)/shard_map/all_gather | solution.py:188
  11.0 29.2 %collective-permute-start = (f32[2056,128]{1,0:T(8,128)S(1)}, f32[2056,128]{1,0:T(8,128)S(1)}, u32[]{:S(2)}, u32[]{:S(2)}) collective-permute-start(f32[2056,128]{1,0:T(8,128)S(1)} %pad_maximum_fusion.refs_0_), channel_id=1, source_target_pairs={{0,128},{128,256},{256,384},{384,0},{1,129},{129,257},{257,385},{3... | collective-permute-start | bytes 3158024 | tf_op jit(solution)/shard_map/ppermute | solution.py:173
  14.6 10.9 %copy-start.8 = (s32[8]{0:T(128)S(1)}, s32[8]{0:T(128)}, u32[]{:S(2)}) copy-start(s32[8]{0:T(128)} %constant.94.clone) | copy-start | bytes 100
  14.6 11.6 %copy-start.5 = (s32[1,1,16]{2,1,0:T(1,128)S(1)}, s32[1,1,16]{2,1,0:T(1,128)}, u32[]{:S(2)}) copy-start(s32[1,1,16]{2,1,0:T(1,128)} %param.16) | copy-start | bytes 196
  14.7 11.7 %copy-start.6 = (s32[1,1,16]{2,1,0:T(1,128)S(1)}, s32[1,1,16]{2,1,0:T(1,128)}, u32[]{:S(2)}) copy-start(s32[1,1,16]{2,1,0:T(1,128)} %param.15) | copy-start | bytes 196
  14.7 34.4 %copy-start.7 = (s32[8,1,1]{0,2,1:T(1,128)S(1)}, s32[8,1,1]{0,2,1:T(1,128)}, u32[]{:S(2)}) copy-start(s32[8,1,1]{0,2,1:T(1,128)} %param.12) | copy-start | bytes 100
  16.0 28.2 %collective-permute-start.3 = (f32[2056,128]{1,0:T(8,128)S(1)}, f32[2056,128]{1,0:T(8,128)}, u32[]{:S(2)}, u32[]{:S(2)}) collective-permute-start(f32[2056,128]{1,0:T(8,128)S(1)} %pad_maximum_fusion.1.refs_1_), channel_id=1, source_target_pairs={{0,384},{128,0},{256,128},{384,256},{1,385},{129,1},{257,129},{385... | collective-permute-start | bytes 3158024 | tf_op jit(solution)/shard_map/ppermute | solution.py:173
  19.7 47.1 %collective-permute-start.2 = (f32[2056,128]{1,0:T(8,128)S(1)}, f32[2056,128]{1,0:T(8,128)}, u32[]{:S(2)}, u32[]{:S(2)}) collective-permute-start(f32[2056,128]{1,0:T(8,128)S(1)} %pad_maximum_fusion.refs_0_), channel_id=1, source_target_pairs={{0,384},{128,0},{256,128},{384,256},{1,385},{129,1},{257,129},{385... | collective-permute-start | bytes 3158024 | tf_op jit(solution)/shard_map/ppermute | solution.py:173
  23.1 44.3 %collective-permute-start.1 = (f32[2056,128]{1,0:T(8,128)S(1)}, f32[2056,128]{1,0:T(8,128)}, u32[]{:S(2)}, u32[]{:S(2)}) collective-permute-start(f32[2056,128]{1,0:T(8,128)S(1)} %pad_maximum_fusion.1.refs_1_), channel_id=1, source_target_pairs={{0,128},{128,256},{256,384},{384,0},{1,129},{129,257},{257,385},{3... | collective-permute-start | bytes 3158024 | tf_op jit(solution)/shard_map/ppermute | solution.py:173
  41.6 42.7 %collective-permute-start.4 = (f32[2056,128]{1,0:T(8,128)S(1)}, f32[2056,128]{1,0:T(8,128)}, u32[]{:S(2)}, u32[]{:S(2)}) collective-permute-start(f32[2056,128]{1,0:T(8,128)S(1)} %collective-permute-done.refs_2_), channel_id=1, source_target_pairs={{0,128},{128,256},{256,384},{384,0},{1,129},{129,257},{257,385},{3... | collective-permute-start | bytes 3158024 | tf_op jit(solution)/shard_map/ppermute | solution.py:173
  44.2 43.7 %collective-permute-start.5 = (f32[2056,128]{1,0:T(8,128)}, f32[2056,128]{1,0:T(8,128)}, u32[]{:S(2)}, u32[]{:S(2)}) collective-permute-start(f32[2056,128]{1,0:T(8,128)} %collective-permute-done.3.refs_5_), channel_id=1, source_target_pairs={{0,384},{128,0},{256,128},{384,256},{1,385},{129,1},{257,129},{385... | collective-permute-start | bytes 3158024 | tf_op jit(solution)/shard_map/ppermute | solution.py:173
  95.2 23.2 %copy-start.2 = (s32[512]{0:T(512)S(1)}, s32[512]{0:T(512)}, u32[]{:S(2)}) copy-start(s32[512]{0:T(512)} %get-tuple-element.37.left_list) | copy-start | bytes 6148
  95.3 23.2 %copy-start.3 = (s32[512]{0:T(512)S(1)}, s32[512]{0:T(512)}, u32[]{:S(2)}) copy-start(s32[512]{0:T(512)} %get-tuple-element.38.right_list) | copy-start | bytes 6148
  95.3 23.2 %copy-start.4 = (s32[16]{0:T(128)S(1)}, s32[16]{0:T(128)}, u32[]{:S(2)}) copy-start(s32[16]{0:T(128)} %get-tuple-element.36.counts) | copy-start | bytes 196
  99.8 3.2 %copy-start = (bf16[128,128,256]{2,1,0:T(8,128)(2,1)}, bf16[128,128,256]{2,1,0:T(8,128)(2,1)S(1)}, u32[]{:S(2)}) copy-start(bf16[128,128,256]{2,1,0:T(8,128)(2,1)S(1)} %split_panel.1.panel) | copy-start | bytes 25165828
  118.5 3.4 %copy-start.1 = (bf16[128,128,256]{2,1,0:T(8,128)(2,1)S(1)}, bf16[128,128,256]{2,1,0:T(8,128)(2,1)}, u32[]{:S(2)}) copy-start(bf16[128,128,256]{2,1,0:T(8,128)(2,1)} %copy-done) | copy-start | bytes 25165828
  126.9 18.8 %collective-permute-start.6 = (f32[2,128,128]{2,1,0:T(8,128)S(1)}, f32[2,128,128]{2,1,0:T(8,128)S(1)}, u32[]{:S(2)}, u32[]{:S(2)}) collective-permute-start(f32[2,128,128]{2,1,0:T(8,128)S(1)} %get-tuple-element.40), channel_id=1, source_target_pairs={{0,1},{1,2},{2,3},{3,0},{4,5},{5,6},{6,7},{7,4},{8,9},{9,10},{10,1... | collective-permute-start | bytes 393224 | tf_op jit(solution)/shard_map/ppermute | solution.py:173
  134.5 19.4 %collective-permute-start.8 = (f32[2,128,128]{2,1,0:T(8,128)S(1)}, f32[2,128,128]{2,1,0:T(8,128)S(1)}, u32[]{:S(2)}, u32[]{:S(2)}) collective-permute-start(f32[2,128,128]{2,1,0:T(8,128)S(1)} %get-tuple-element.42), channel_id=1, source_target_pairs={{0,3},{1,0},{2,1},{3,2},{4,7},{5,4},{6,5},{7,6},{8,11},{9,8},{10,9... | collective-permute-start | bytes 393224 | tf_op jit(solution)/shard_map/ppermute | solution.py:173
  145.8 20.5 %collective-permute-start.7 = (f32[4,128,128]{2,1,0:T(8,128)S(1)}, f32[4,128,128]{2,1,0:T(8,128)S(1)}, u32[]{:S(2)}, u32[]{:S(2)}) collective-permute-start(f32[4,128,128]{2,1,0:T(8,128)S(1)} %pad_maximum_fusion.2), channel_id=1, source_target_pairs={{0,1},{1,2},{2,3},{3,0},{4,5},{5,6},{6,7},{7,4},{8,9},{9,10},{10,1... | collective-permute-start | bytes 786440 | tf_op jit(solution)/shard_map/ppermute | solution.py:173
  154.0 19.7 %collective-permute-start.9 = (f32[4,128,128]{2,1,0:T(8,128)S(1)}, f32[4,128,128]{2,1,0:T(8,128)S(1)}, u32[]{:S(2)}, u32[]{:S(2)}) collective-permute-start(f32[4,128,128]{2,1,0:T(8,128)S(1)} %pad_maximum_fusion.3), channel_id=1, source_target_pairs={{0,3},{1,0},{2,1},{3,2},{4,7},{5,4},{6,5},{7,6},{8,11},{9,8},{10,9... | collective-permute-start | bytes 786440 | tf_op jit(solution)/shard_map/ppermute | solution.py:173
Sparse Core Ops, SparseCore 0:
  9.5 108.8 all-gather.3

commit v3 on v2

--- a/solution.py
+++ b/solution.py
@@ -80,18 +80,26 @@
 
 
 def product_kernel(first, outputs, slots, counts, left_list, right_list, left_ref, panel, *rest):
-    out_refs = rest[:-2]
-    left_buf, left_sem = rest[-2:]
+    out_refs = rest[:-4]
+    left_buf, right_buf, left_sem, right_sem = rest[-4:]
     size = left_ref.shape[1]
 
+    def copies(which, spot, left_place, right_place):
+        buf = which % 2
+        return (
+            pltpu.make_async_copy(
+                left_ref.at[left_place], left_buf.at[buf, spot], left_sem.at[buf, spot]
+            ),
+            pltpu.make_async_copy(
+                panel.at[right_place], right_buf.at[buf, spot], right_sem.at[buf, spot]
+            ),
+        )
+
     def issue(which):
-        buf = which % 2
-
         def one(spot, carry):
-            place = left_list[(first + which) * slots + spot]
-            pltpu.make_async_copy(
-                left_ref.at[place], left_buf.at[buf, spot], left_sem.at[buf, spot]
-            ).start()
+            at = (first + which) * slots + spot
+            for copy in copies(which, spot, left_list[at], right_list[at]):
+                copy.start()
             return carry
 
         lax.fori_loop(0, counts[first + which], one, 0)
@@ -102,23 +110,19 @@
         chunks = (count + CHUNK - 1) // CHUNK
 
         def arrive(spot, carry):
-            pltpu.make_async_copy(
-                left_ref.at[0], left_buf.at[buf, spot], left_sem.at[buf, spot]
-            ).wait()
+            for copy in copies(which, spot, 0, 0):
+                copy.wait()
             return carry
 
         def clear(spot, carry):
             left_buf[buf, spot] = zero
+            right_buf[buf, spot] = jnp.zeros((size, 2 * size), jnp.bfloat16)
             return carry
 
         def one(chunk, total):
             base = chunk * CHUNK
-            left, right = [], []
-            for part in range(CHUNK):
-                spot = base + part
-                block = right_list[(first + which) * slots + spot]
-                right.append(panel[jnp.where(spot < count, block, 0)])
-                left.append(left_buf[buf, spot])
+            left = [left_buf[buf, base + part] for part in range(CHUNK)]
+            right = [right_buf[buf, base + part] for part in range(CHUNK)]
             high, low = halves(jnp.concatenate(left, axis=1))
             both = jnp.dot(
                 jnp.concatenate([high, low], axis=0), jnp.concatenate(right, axis=0),
@@ -147,13 +151,15 @@
     return pl.pallas_call(
         functools.partial(product_kernel, first, outputs, slots),
         out_shape=[shape] * parts,
-        in_specs=[smem] * 3 + [pl.BlockSpec(memory_space=pl.ANY), vmem],
+        in_specs=[smem] * 3 + [pl.BlockSpec(memory_space=pl.ANY)] * 2,
         out_specs=[vmem] * parts,
         scratch_shapes=[
             pltpu.VMEM((2, slots, size, size), jnp.float32),
+            pltpu.VMEM((2, slots, size, 2 * size), jnp.bfloat16),
+            pltpu.SemaphoreType.DMA((2, slots)),
             pltpu.SemaphoreType.DMA((2, slots)),
         ],
-        compiler_params=pltpu.CompilerParams(vmem_limit_bytes=42 * 1024 * 1024),
+        compiler_params=pltpu.CompilerParams(vmem_limit_bytes=52 * 1024 * 1024),
         cost_estimate=pl.CostEstimate(
             flops=outputs * 16 * 8 * size**3, bytes_accessed=outputs * 16 * 4 * size**2,
             transcendentals=0,
@@ -216,12 +222,14 @@
     far_low, far_high = products("far_blocks", 2, 0, share, lists, left, panel)
     from_last = shift(far_low, "layer", 1)
     from_next = shift(far_high, "layer", -1)
-    up, down = products("near_blocks", 2, share, 2 * share, lists, left, panel)
-    up = jnp.concatenate([up[: share // 2] + from_last, up[share // 2 :]])
-    down = jnp.concatenate([down[: share // 2], down[share // 2 :] + from_next])
-    up_in, down_in = shift(up, "layer", 1), shift(down, "layer", -1)
+    up_low, up_high, down_low, down_high = products(
+        "near_blocks", 4, share, 2 * share, lists, left, panel
+    )
+    up_high_in, down_low_in = shift(up_high, "layer", 1), shift(down_low, "layer", -1)
+    up_low_in = shift(up_low + from_last, "layer", 1)
+    down_high_in = shift(down_high + from_next, "layer", -1)
     (own,) = products("own_blocks", 1, 3 * share, share, lists, left, panel)
-    mine = own + up_in + down_in
+    mine = own + jnp.concatenate([up_low_in + down_low_in, up_high_in + down_high_in])
 
     squared = mine * mine
     cols_mine = quarter(cols_here, 0)

time: 219 us -> 216 us (0.986)
  the two profiles are of different devices: /device:TPU:16 before, /device:TPU:64 now
where the time goes in v3:
time: 216 us; the launch traced here: 214 us
  waiting for transfers between devices  58.2 us (27%)
  starting transfers between devices  49.2 us (23%)
  blocking collectives  42.6 us (20%)
  Pallas kernels  32.1 us (15%)
  between operations  15 us (7%)
  local copies, waits for them, and re-layouts  12 us (6%)
  other arithmetic  4.98 us (2%)
    ppermute x12, starting transfers between devices, shift(): lax.ppermute(value, axis, [(i, (i + by) % count) for i in range(count)])  49.2 us
    ppermute x12, waiting for transfers between devices, shift(): lax.ppermute(value, axis, [(i, (i + by) % count) for i in range(count)])  42.1 us
    psum x2, blocking collectives, local(): colsum = lax.psum(lax.psum(local_sums, 'layer'), 'row')  27.5 us
    pallas_call x3, Pallas kernels, products(): pl.pallas_call(functools.partial(product_kernel, first, outputs, slots),...  21.5 us
    all_gather x1, waiting for transfers between devices, local(): lax.all_gather(a_values.reshape(block_rows, size, lanes), 'col', axis=0,...  15.4 us
    all_gather x1, blocking collectives, local(): left_keys = lax.all_gather(left_index, 'col', axis=0, tiled=True)  15.1 us
    pallas_call x1, Pallas kernels, match_lists(): pl.pallas_call(functools.partial(list_kernel, outputs, slots, right_keys....  6.1 us
    unnamed x18, local copies, waits for them, and re-layouts  4.53 us
  transfers between devices with their start and end apart: 13, of which 7 were waited for; matrix products, arithmetic and copies ran while one was open for 6% of the time, Pallas kernels for 12%

profile of v3, /device:TPU:64, one launch (start us, length us, event | category | flops | bytes accessed | tf_op | source)
XLA Modules:
  0.0 214.5 jit_solution(5722445519011162635)
XLA Ops:
  6.5 0.7 all-gather.4.cloned.1.call-update
  7.3 0.8 slice_convert_fusion
  8.1 0.1 copy.14
  8.3 2.7 %fusion.18 = (f32[1,4,4,128,128]{4,3,2,1,0:T(8,128)}, f32[1,4,4,128,128]{4,3,2,1,0:T(8,128)S(1)}) fusion(f32[1,8,4,128,128]{4,3,2,1,0:T(8,128)} %param.13), kind=kLoop, calls=%fused_computation.46 | loop fusion | bytes 4194304 | tf_op jit(solution)/shard_map/slice | solution.py:196
  11.0 3.4 %collective-permute-start = (f32[2056,128]{1,0:T(8,128)S(1)}, f32[2056,128]{1,0:T(8,128)S(1)}, u32[]{:S(2)}, u32[]{:S(2)}) collective-permute-start(f32[2056,128]{1,0:T(8,128)S(1)} %pad_maximum_fusion.refs_0_), channel_id=1, source_target_pairs={{0,128},{128,256},{256,384},{384,0},{1,129},{129,257},{257,385},{3... | collective-permute-start | bytes 3158024 | tf_op jit(solution)/shard_map/ppermute | solution.py:179
  14.4 0.1 copy.15
  14.7 1.3 pad_maximum_fusion.1.refs_1_
  16.0 3.7 %collective-permute-start.3 = (f32[2056,128]{1,0:T(8,128)S(1)}, f32[2056,128]{1,0:T(8,128)}, u32[]{:S(2)}, u32[]{:S(2)}) collective-permute-start(f32[2056,128]{1,0:T(8,128)S(1)} %pad_maximum_fusion.1.refs_1_), channel_id=1, source_target_pairs={{0,384},{128,0},{256,128},{384,256},{1,385},{129,1},{257,129},{385... | collective-permute-start | bytes 3158024 | tf_op jit(solution)/shard_map/ppermute | solution.py:179
  19.7 3.5 %collective-permute-start.2 = (f32[2056,128]{1,0:T(8,128)S(1)}, f32[2056,128]{1,0:T(8,128)}, u32[]{:S(2)}, u32[]{:S(2)}) collective-permute-start(f32[2056,128]{1,0:T(8,128)S(1)} %pad_maximum_fusion.refs_0_), channel_id=1, source_target_pairs={{0,384},{128,0},{256,128},{384,256},{1,385},{129,1},{257,129},{385... | collective-permute-start | bytes 3158024 | tf_op jit(solution)/shard_map/ppermute | solution.py:179
  23.1 2.4 %collective-permute-start.1 = (f32[2056,128]{1,0:T(8,128)S(1)}, f32[2056,128]{1,0:T(8,128)}, u32[]{:S(2)}, u32[]{:S(2)}) collective-permute-start(f32[2056,128]{1,0:T(8,128)S(1)} %pad_maximum_fusion.1.refs_1_), channel_id=1, source_target_pairs={{0,128},{128,256},{256,384},{384,0},{1,129},{129,257},{257,385},{3... | collective-permute-start | bytes 3158024 | tf_op jit(solution)/shard_map/ppermute | solution.py:179
  25.7 0.6 fusion.16.right_base
  26.5 1.3 dynamic-slice.22
  28.4 0.7 pad_add_fusion
  29.0 11.2 %collective-permute-done.refs_2_ = f32[2056,128]{1,0:T(8,128)S(1)} collective-permute-done((f32[2056,128]{1,0:T(8,128)S(1)}, f32[2056,128]{1,0:T(8,128)S(1)}, u32[]{:S(2)}, u32[]{:S(2)}) %collective-permute-start) | collective-permute-done | bytes 1052704 | tf_op jit(solution)/shard_map/ppermute | solution.py:179
  40.3 0.6 slice.70
  41.5 2.2 %collective-permute-start.4 = (f32[2056,128]{1,0:T(8,128)S(1)}, f32[2056,128]{1,0:T(8,128)}, u32[]{:S(2)}, u32[]{:S(2)}) collective-permute-start(f32[2056,128]{1,0:T(8,128)S(1)} %collective-permute-done.refs_2_), channel_id=1, source_target_pairs={{0,128},{128,256},{256,384},{384,0},{1,129},{129,257},{257,385},{3... | collective-permute-start | bytes 3158024 | tf_op jit(solution)/shard_map/ppermute | solution.py:179
  43.7 0.4 collective-permute-done.3.refs_5_
  44.2 4.9 %collective-permute-start.5 = (f32[2056,128]{1,0:T(8,128)}, f32[2056,128]{1,0:T(8,128)}, u32[]{:S(2)}, u32[]{:S(2)}) collective-permute-start(f32[2056,128]{1,0:T(8,128)} %collective-permute-done.3.refs_5_), channel_id=1, source_target_pairs={{0,384},{128,0},{256,128},{384,256},{1,385},{129,1},{257,129},{385... | collective-permute-start | bytes 3158024 | tf_op jit(solution)/shard_map/ppermute | solution.py:179
  49.0 0.1 bitcast_dynamic-update-slice_fusion
  49.1 15.1 %all-reduce.2.left_keys = s32[256]{0:T(256)} all-reduce(s32[256]{0:T(256)S(1)} %bitcast_dynamic-update-slice_fusion), channel_id=2, replica_groups=mesh['row'=4,'col'=32,'layer'=4] {'col'}, use_global_device_ids=true, to_apply=%add.2 | all-reduce | flops 256 | bytes 2048 | tf_op jit(solution)/shard_map/all_gather | solution.py:204
  64.2 0.7 slice_bitcast_fusion.2
  64.9 1.8 collective-permute-done.2.refs_4_
  66.7 0.7 slice_bitcast_fusion.3
  67.4 0.7 slice_bitcast_fusion.4
  68.1 16.3 %collective-permute-done.4.refs_6_ = f32[2056,128]{1,0:T(8,128)} collective-permute-done((f32[2056,128]{1,0:T(8,128)S(1)}, f32[2056,128]{1,0:T(8,128)}, u32[]{:S(2)}, u32[]{:S(2)}) %collective-permute-start.4) | collective-permute-done | bytes 1052704 | tf_op jit(solution)/shard_map/ppermute | solution.py:179
  84.3 0.7 slice_bitcast_fusion.1
  85.0 2.8 %collective-permute-done.5.refs_7_ = f32[2056,128]{1,0:T(8,128)} collective-permute-done((f32[2056,128]{1,0:T(8,128)}, f32[2056,128]{1,0:T(8,128)}, u32[]{:S(2)}, u32[]{:S(2)}) %collective-permute-start.5) | collective-permute-done | bytes 1052704 | tf_op jit(solution)/shard_map/ppermute | solution.py:179
  87.8 0.7 slice_bitcast_fusion
  88.6 0.5 convert_element_type.28.right_keys
  89.1 6.1 %match_lists.1 = (s32[16]{0:T(128)}, s32[512]{0:T(512)}, s32[512]{0:T(512)}) custom-call(s32[16]{0:T(128)} %get-tuple-element.59.rows_ref, s32[16]{0:T(128)} %get-tuple-element.60.cols_ref, s32[256]{0:T(256)} %all-reduce.2.left_keys, s32[128]{0:T(128)} %convert_element_type.28.right_keys, s32[32]{0:T(128)} %fusion.16.right_base), custom_call_target="tpu_custom_call" | custom-call | tf_op jit(solution)/shard_map/match_lists/pallas_call | solution.py:44
  95.2 4.5 %split_panel.1.panel = bf16[128,128,256]{2,1,0:T(8,128)(2,1)S(1)} custom-call(f32[2056,128]{1,0:T(8,128)S(1)} %pad_maximum_fusion.refs_0_, f32[2056,128]{1,0:T(8,128)S(1)} %pad_maximum_fusion.1.refs_1_, f32[2056,128]{1,0:T(8,128)S(1)} %collective-permute-done.refs_2_, f32[2056,128]{1,0:T(8,128)} %collective-permute-done.1.refs_3_, ...), custom_call_target="tpu_custom_call" | custom-call | tf_op jit(solution)/shard_map/split_panel/pallas_call | solution.py:72
  99.7 3.2 %copy-done = bf16[128,128,256]{2,1,0:T(8,128)(2,1)} copy-done((bf16[128,128,256]{2,1,0:T(8,128)(2,1)}, bf16[128,128,256]{2,1,0:T(8,128)(2,1)S(1)}, u32[]{:S(2)}) %copy-start) | copy-done | bytes 8388632
  102.9 15.4 %all-gather.4.cloned.1.call-done = f32[256,1,1,128,128]{4,3,2,1,0:T(8,128)} async-done(((f32[8,1,1,128,128]{4,3,2,1,0:T(8,128)}), f32[256,1,1,128,128]{4,3,2,1,0:T(8,128)}) %all-gather.4.cloned.1.call-update) | async-done | bytes 16777232 | tf_op jit(solution)/shard_map/all_gather | solution.py:194
  118.3 6.2 %far_blocks.1 = (f32[2,128,128]{2,1,0:T(8,128)S(1)}, f32[2,128,128]{2,1,0:T(8,128)S(1)}) custom-call(s32[16]{0:T(128)S(1)} %copy-done.3, s32[512]{0:T(512)S(1)} %copy-done.1, s32[512]{0:T(512)S(1)} %copy-done.2, f32[256,128,128]{2,1,0:T(8,128)} %bitcast.38, bf16[128,128,256]{2,1,0:T(8,128)(2,1)} %copy-done), custom_call_target="tpu_custom_call" | custom-call | flops 1073741824 | bytes 4194304 | tf_op jit(solution)/shard_map/far_blocks/pallas_call | solution.py:151
  124.5 7.2 %collective-permute-start.6 = (f32[2,128,128]{2,1,0:T(8,128)S(1)}, f32[2,128,128]{2,1,0:T(8,128)S(1)}, u32[]{:S(2)}, u32[]{:S(2)}) collective-permute-start(f32[2,128,128]{2,1,0:T(8,128)S(1)} %get-tuple-element.42), channel_id=1, source_target_pairs={{0,1},{1,2},{2,3},{3,0},{4,5},{5,6},{6,7},{7,4},{8,9},{9,10},{10,1... | collective-permute-start | bytes 393224 | tf_op jit(solution)/shard_map/ppermute | solution.py:179
  131.7 2.6 %collective-permute-start.10 = (f32[2,128,128]{2,1,0:T(8,128)S(1)}, f32[2,128,128]{2,1,0:T(8,128)S(1)}, u32[]{:S(2)}, u32[]{:S(2)}) collective-permute-start(f32[2,128,128]{2,1,0:T(8,128)S(1)} %get-tuple-element.46), channel_id=1, source_target_pairs={{0,3},{1,0},{2,1},{3,2},{4,7},{5,4},{6,5},{7,6},{8,11},{9,8},{10,9... | collective-permute-start | bytes 393224 | tf_op jit(solution)/shard_map/ppermute | solution.py:179
  134.3 9.2 %near_blocks.1 = (f32[2,128,128]{2,1,0:T(8,128)S(1)}, f32[2,128,128]{2,1,0:T(8,128)S(1)}, f32[2,128,128]{2,1,0:T(8,128)S(1)}, f32[2,128,128]{2,1,0:T(8,128)S(1)}) custom-call(s32[16]{0:T(128)S(1)} %copy-done.3, s32[512]{0:T(512)S(1)} %copy-done.1, s32[512]{0:T(512)S(1)} %copy-done.2, f32[256,128,128]{2,1,0:T(8,128)} %bitcast.39, bf16[128,128,256]{2,1,0:T(8,128)(2,1)} %copy-done), custom_call_target="tpu_custom_call" | custom-call | flops 2147483648 | bytes 8388608 | tf_op jit(solution)/shard_map/near_blocks/pallas_call | solution.py:151
  143.4 5.9 %collective-permute-start.8 = (f32[2,128,128]{2,1,0:T(8,128)S(1)}, f32[2,128,128]{2,1,0:T(8,128)S(1)}, u32[]{:S(2)}, u32[]{:S(2)}) collective-permute-start(f32[2,128,128]{2,1,0:T(8,128)S(1)} %get-tuple-element.43), channel_id=1, source_target_pairs={{0,3},{1,0},{2,1},{3,2},{4,7},{5,4},{6,5},{7,6},{8,11},{9,8},{10,9... | collective-permute-start | bytes 393224 | tf_op jit(solution)/shard_map/ppermute | solution.py:179
  149.4 3.8 %collective-permute-start.9 = (f32[2,128,128]{2,1,0:T(8,128)S(1)}, f32[2,128,128]{2,1,0:T(8,128)S(1)}, u32[]{:S(2)}, u32[]{:S(2)}) collective-permute-start(f32[2,128,128]{2,1,0:T(8,128)S(1)} %get-tuple-element.44), channel_id=1, source_target_pairs={{0,1},{1,2},{2,3},{3,0},{4,5},{5,6},{6,7},{7,4},{8,9},{9,10},{10,1... | collective-permute-start | bytes 393224 | tf_op jit(solution)/shard_map/ppermute | solution.py:179
  153.2 6.8 %collective-permute-start.7 = (f32[2,128,128]{2,1,0:T(8,128)S(1)}, f32[2,128,128]{2,1,0:T(8,128)S(1)}, u32[]{:S(2)}, u32[]{:S(2)}) collective-permute-start(f32[2,128,128]{2,1,0:T(8,128)S(1)} %add.100), channel_id=1, source_target_pairs={{0,1},{1,2},{2,3},{3,0},{4,5},{5,6},{6,7},{7,4},{8,9},{9,10},{10,1... | collective-permute-start | bytes 393224 | tf_op jit(solution)/shard_map/ppermute | solution.py:179
  160.1 3.0 %collective-permute-start.11 = (f32[2,128,128]{2,1,0:T(8,128)S(1)}, f32[2,128,128]{2,1,0:T(8,128)S(1)}, u32[]{:S(2)}, u32[]{:S(2)}) collective-permute-start(f32[2,128,128]{2,1,0:T(8,128)S(1)} %add.102), channel_id=1, source_target_pairs={{0,3},{1,0},{2,1},{3,2},{4,7},{5,4},{6,5},{7,6},{8,11},{9,8},{10,9... | collective-permute-start | bytes 393224 | tf_op jit(solution)/shard_map/ppermute | solution.py:179
  163.0 6.2 %own_blocks.1 = f32[4,128,128]{2,1,0:T(8,128)S(1)} custom-call(s32[16]{0:T(128)S(1)} %copy-done.3, s32[512]{0:T(512)S(1)} %copy-done.1, s32[512]{0:T(512)S(1)} %copy-done.2, f32[256,128,128]{2,1,0:T(8,128)} %bitcast.40, bf16[128,128,256]{2,1,0:T(8,128)(2,1)} %copy-done), custom_call_target="tpu_custom_call" | custom-call | flops 1073741824 | bytes 4194304 | tf_op jit(solution)/shard_map/own_blocks/pallas_call | solution.py:151
  169.3 9.5 %collective-permute-done.7 = f32[2,128,128]{2,1,0:T(8,128)S(1)} collective-permute-done((f32[2,128,128]{2,1,0:T(8,128)S(1)}, f32[2,128,128]{2,1,0:T(8,128)S(1)}, u32[]{:S(2)}, u32[]{:S(2)}) %collective-permute-start.7) | collective-permute-done | bytes 131104 | tf_op jit(solution)/shard_map/ppermute | solution.py:179
  178.9 0.3 fusion.3
  179.2 16.1 %psum.14 = f32[4,128]{1,0:T(4,128)S(1)} all-reduce(f32[4,128]{1,0:T(4,128)S(1)} %fusion.3), channel_id=1, replica_groups=mesh['row'=4,'col'=32,'layer'=4] {'layer'}, use_global_device_ids=true, to_apply=%region_1.0 | all-reduce | flops 512 | bytes 4096 | tf_op jit(solution)/shard_map/psum | solution.py:242
  195.3 11.3 %psum.15 = f32[4,128]{1,0:T(4,128)S(1)} all-reduce(f32[4,128]{1,0:T(4,128)S(1)} %psum.14), channel_id=1, replica_groups=mesh['row'=4,'col'=32,'layer'=4] {'row'}, use_global_device_ids=true, to_apply=%region_2.0 | all-reduce | flops 512 | bytes 4096 | tf_op jit(solution)/shard_map/psum | solution.py:242
  206.7 0.2 convolution_divide_fusion
  206.9 0.8 multiply_bitcast_fusion
  (42 shorter events, 0.8 us)
Async XLA Ops:
  6.5 111.8 %all-gather.4.cloned.1.call-start = ((), (), s32[]{:S(2)}) async-start(), calls=%async_computation | async-start | bytes 17301504 | tf_op jit(solution)/shard_map/all_gather | solution.py:194
  11.0 29.2 %collective-permute-start = (f32[2056,128]{1,0:T(8,128)S(1)}, f32[2056,128]{1,0:T(8,128)S(1)}, u32[]{:S(2)}, u32[]{:S(2)}) collective-permute-start(f32[2056,128]{1,0:T(8,128)S(1)} %pad_maximum_fusion.refs_0_), channel_id=1, source_target_pairs={{0,128},{128,256},{256,384},{384,0},{1,129},{129,257},{257,385},{3... | collective-permute-start | bytes 3158024 | tf_op jit(solution)/shard_map/ppermute | solution.py:179
  14.6 10.9 %copy-start.7 = (s32[8]{0:T(128)S(1)}, s32[8]{0:T(128)}, u32[]{:S(2)}) copy-start(s32[8]{0:T(128)} %constant.94.clone) | copy-start | bytes 100
  14.6 11.7 %copy-start.4 = (s32[1,1,16]{2,1,0:T(1,128)S(1)}, s32[1,1,16]{2,1,0:T(1,128)}, u32[]{:S(2)}) copy-start(s32[1,1,16]{2,1,0:T(1,128)} %param.16) | copy-start | bytes 196
  14.6 11.7 %copy-start.5 = (s32[1,1,16]{2,1,0:T(1,128)S(1)}, s32[1,1,16]{2,1,0:T(1,128)}, u32[]{:S(2)}) copy-start(s32[1,1,16]{2,1,0:T(1,128)} %param.15) | copy-start | bytes 196
  14.7 34.4 %copy-start.6 = (s32[8,1,1]{0,2,1:T(1,128)S(1)}, s32[8,1,1]{0,2,1:T(1,128)}, u32[]{:S(2)}) copy-start(s32[8,1,1]{0,2,1:T(1,128)} %param.12) | copy-start | bytes 100
  16.0 28.2 %collective-permute-start.3 = (f32[2056,128]{1,0:T(8,128)S(1)}, f32[2056,128]{1,0:T(8,128)}, u32[]{:S(2)}, u32[]{:S(2)}) collective-permute-start(f32[2056,128]{1,0:T(8,128)S(1)} %pad_maximum_fusion.1.refs_1_), channel_id=1, source_target_pairs={{0,384},{128,0},{256,128},{384,256},{1,385},{129,1},{257,129},{385... | collective-permute-start | bytes 3158024 | tf_op jit(solution)/shard_map/ppermute | solution.py:179
  19.7 47.1 %collective-permute-start.2 = (f32[2056,128]{1,0:T(8,128)S(1)}, f32[2056,128]{1,0:T(8,128)}, u32[]{:S(2)}, u32[]{:S(2)}) collective-permute-start(f32[2056,128]{1,0:T(8,128)S(1)} %pad_maximum_fusion.refs_0_), channel_id=1, source_target_pairs={{0,384},{128,0},{256,128},{384,256},{1,385},{129,1},{257,129},{385... | collective-permute-start | bytes 3158024 | tf_op jit(solution)/shard_map/ppermute | solution.py:179
  23.1 44.3 %collective-permute-start.1 = (f32[2056,128]{1,0:T(8,128)S(1)}, f32[2056,128]{1,0:T(8,128)}, u32[]{:S(2)}, u32[]{:S(2)}) collective-permute-start(f32[2056,128]{1,0:T(8,128)S(1)} %pad_maximum_fusion.1.refs_1_), channel_id=1, source_target_pairs={{0,128},{128,256},{256,384},{384,0},{1,129},{129,257},{257,385},{3... | collective-permute-start | bytes 3158024 | tf_op jit(solution)/shard_map/ppermute | solution.py:179
  41.5 42.8 %collective-permute-start.4 = (f32[2056,128]{1,0:T(8,128)S(1)}, f32[2056,128]{1,0:T(8,128)}, u32[]{:S(2)}, u32[]{:S(2)}) collective-permute-start(f32[2056,128]{1,0:T(8,128)S(1)} %collective-permute-done.refs_2_), channel_id=1, source_target_pairs={{0,128},{128,256},{256,384},{384,0},{1,129},{129,257},{257,385},{3... | collective-permute-start | bytes 3158024 | tf_op jit(solution)/shard_map/ppermute | solution.py:179
  44.2 43.7 %collective-permute-start.5 = (f32[2056,128]{1,0:T(8,128)}, f32[2056,128]{1,0:T(8,128)}, u32[]{:S(2)}, u32[]{:S(2)}) collective-permute-start(f32[2056,128]{1,0:T(8,128)} %collective-permute-done.3.refs_5_), channel_id=1, source_target_pairs={{0,384},{128,0},{256,128},{384,256},{1,385},{129,1},{257,129},{385... | collective-permute-start | bytes 3158024 | tf_op jit(solution)/shard_map/ppermute | solution.py:179
  95.2 23.1 %copy-start.1 = (s32[512]{0:T(512)S(1)}, s32[512]{0:T(512)}, u32[]{:S(2)}) copy-start(s32[512]{0:T(512)} %get-tuple-element.39.left_list) | copy-start | bytes 6148
  95.2 23.1 %copy-start.2 = (s32[512]{0:T(512)S(1)}, s32[512]{0:T(512)}, u32[]{:S(2)}) copy-start(s32[512]{0:T(512)} %get-tuple-element.40.right_list) | copy-start | bytes 6148
  95.2 23.1 %copy-start.3 = (s32[16]{0:T(128)S(1)}, s32[16]{0:T(128)}, u32[]{:S(2)}) copy-start(s32[16]{0:T(128)} %get-tuple-element.38.counts) | copy-start | bytes 196
  99.7 3.2 %copy-start = (bf16[128,128,256]{2,1,0:T(8,128)(2,1)}, bf16[128,128,256]{2,1,0:T(8,128)(2,1)S(1)}, u32[]{:S(2)}) copy-start(bf16[128,128,256]{2,1,0:T(8,128)(2,1)S(1)} %split_panel.1.panel) | copy-start | bytes 25165828
  124.5 28.7 %collective-permute-start.6 = (f32[2,128,128]{2,1,0:T(8,128)S(1)}, f32[2,128,128]{2,1,0:T(8,128)S(1)}, u32[]{:S(2)}, u32[]{:S(2)}) collective-permute-start(f32[2,128,128]{2,1,0:T(8,128)S(1)} %get-tuple-element.42), channel_id=1, source_target_pairs={{0,1},{1,2},{2,3},{3,0},{4,5},{5,6},{6,7},{7,4},{8,9},{9,10},{10,1... | collective-permute-start | bytes 393224 | tf_op jit(solution)/shard_map/ppermute | solution.py:179
  131.7 28.3 %collective-permute-start.10 = (f32[2,128,128]{2,1,0:T(8,128)S(1)}, f32[2,128,128]{2,1,0:T(8,128)S(1)}, u32[]{:S(2)}, u32[]{:S(2)}) collective-permute-start(f32[2,128,128]{2,1,0:T(8,128)S(1)} %get-tuple-element.46), channel_id=1, source_target_pairs={{0,3},{1,0},{2,1},{3,2},{4,7},{5,4},{6,5},{7,6},{8,11},{9,8},{10,9... | collective-permute-start | bytes 393224 | tf_op jit(solution)/shard_map/ppermute | solution.py:179
  143.4 25.8 %collective-permute-start.8 = (f32[2,128,128]{2,1,0:T(8,128)S(1)}, f32[2,128,128]{2,1,0:T(8,128)S(1)}, u32[]{:S(2)}, u32[]{:S(2)}) collective-permute-start(f32[2,128,128]{2,1,0:T(8,128)S(1)} %get-tuple-element.43), channel_id=1, source_target_pairs={{0,3},{1,0},{2,1},{3,2},{4,7},{5,4},{6,5},{7,6},{8,11},{9,8},{10,9... | collective-permute-start | bytes 393224 | tf_op jit(solution)/shard_map/ppermute | solution.py:179
  149.4 29.5 %collective-permute-start.9 = (f32[2,128,128]{2,1,0:T(8,128)S(1)}, f32[2,128,128]{2,1,0:T(8,128)S(1)}, u32[]{:S(2)}, u32[]{:S(2)}) collective-permute-start(f32[2,128,128]{2,1,0:T(8,128)S(1)} %get-tuple-element.44), channel_id=1, source_target_pairs={{0,1},{1,2},{2,3},{3,0},{4,5},{5,6},{6,7},{7,4},{8,9},{9,10},{10,1... | collective-permute-start | bytes 393224 | tf_op jit(solution)/shard_map/ppermute | solution.py:179
  153.2 25.6 %collective-permute-start.7 = (f32[2,128,128]{2,1,0:T(8,128)S(1)}, f32[2,128,128]{2,1,0:T(8,128)S(1)}, u32[]{:S(2)}, u32[]{:S(2)}) collective-permute-start(f32[2,128,128]{2,1,0:T(8,128)S(1)} %add.100), channel_id=1, source_target_pairs={{0,1},{1,2},{2,3},{3,0},{4,5},{5,6},{6,7},{7,4},{8,9},{9,10},{10,1... | collective-permute-start | bytes 393224 | tf_op jit(solution)/shard_map/ppermute | solution.py:179
  160.1 18.8 %collective-permute-start.11 = (f32[2,128,128]{2,1,0:T(8,128)S(1)}, f32[2,128,128]{2,1,0:T(8,128)S(1)}, u32[]{:S(2)}, u32[]{:S(2)}) collective-permute-start(f32[2,128,128]{2,1,0:T(8,128)S(1)} %add.102), channel_id=1, source_target_pairs={{0,3},{1,0},{2,1},{3,2},{4,7},{5,4},{6,5},{7,6},{8,11},{9,8},{10,9... | collective-permute-start | bytes 393224 | tf_op jit(solution)/shard_map/ppermute | solution.py:179
Sparse Core Ops, SparseCore 0:
  9.5 108.7 all-gather.3

commit v4 on v3

--- a/solution.py
+++ b/solution.py
@@ -17,7 +17,9 @@
 
 
 def list_kernel(outputs, slots, block_cols, block_rows, rows_ref, cols_ref, left_keys, right_keys,
-                right_base, counts, left_list, right_list):
+                right_base, matches):
+    blocks = slots * block_cols
+
     def per_output(which, carry):
         row, col = rows_ref[which], cols_ref[which]
 
@@ -26,12 +28,11 @@
             inner = jnp.maximum(key, 0)
             place = (right_base[slot] + inner // KB_C) * block_rows + row
             live = (key >= 0) & (left_keys[place] == lax.rem(inner, KB_C))
-            spot = which * slots + count
-            left_list[spot] = place
-            right_list[spot] = slot * block_cols + col
+            matches[which * slots + count] = place * blocks + slot * block_cols + col
             return count + live.astype(jnp.int32)
 
-        counts[which] = lax.fori_loop(0, slots, one, jnp.int32(0), unroll=8)
+        count = lax.fori_loop(0, slots, one, jnp.int32(0), unroll=8)
+        matches[outputs * slots + which] = count
         return carry
 
     lax.fori_loop(0, outputs, per_output, 0)
@@ -40,14 +41,13 @@
 def match_lists(rows, cols, left_keys, right_keys, right_base, block_rows):
     outputs, slots = rows.shape[0], right_base.shape[0]
     smem = pl.BlockSpec(memory_space=pltpu.SMEM)
-    lists = jax.ShapeDtypeStruct((outputs * slots,), jnp.int32)
     return pl.pallas_call(
         functools.partial(
             list_kernel, outputs, slots, right_keys.shape[0] // slots, block_rows
         ),
-        out_shape=[jax.ShapeDtypeStruct((outputs,), jnp.int32), lists, lists],
+        out_shape=jax.ShapeDtypeStruct((outputs * (slots + 1),), jnp.int32),
         in_specs=[smem] * 5,
-        out_specs=[smem] * 3,
+        out_specs=smem,
         name="match_lists",
     )(rows, cols, left_keys, right_keys, right_base)
 
@@ -79,10 +79,12 @@
     )(*pieces)
 
 
-def product_kernel(first, outputs, slots, counts, left_list, right_list, left_ref, panel, *rest):
-    out_refs = rest[:-4]
-    left_buf, right_buf, left_sem, right_sem = rest[-4:]
+def product_kernel(first, outputs, matches, left_ref, panel, out_ref, left_buf, right_buf,
+                   left_sem, right_sem):
     size = left_ref.shape[1]
+    blocks = panel.shape[0]
+    slots = left_buf.shape[1]
+    total_outputs = matches.shape[0] // (slots + 1)
 
     def copies(which, spot, left_place, right_place):
         buf = which % 2
@@ -97,15 +99,15 @@
 
     def issue(which):
         def one(spot, carry):
-            at = (first + which) * slots + spot
-            for copy in copies(which, spot, left_list[at], right_list[at]):
+            match = matches[(first + which) * slots + spot]
+            for copy in copies(which, spot, lax.div(match, blocks), lax.rem(match, blocks)):
                 copy.start()
             return carry
 
-        lax.fori_loop(0, counts[first + which], one, 0)
+        lax.fori_loop(0, matches[total_outputs * slots + first + which], one, 0)
 
     def multiply(which):
-        buf, count = which % 2, counts[first + which]
+        buf, count = which % 2, matches[total_outputs * slots + first + which]
         zero = jnp.zeros((size, size), jnp.float32)
         chunks = (count + CHUNK - 1) // CHUNK
 
@@ -134,25 +136,22 @@
         lax.fori_loop(count, chunks * CHUNK, clear, 0)
         return lax.fori_loop(0, chunks, one, zero)
 
-    share = outputs // len(out_refs)
     issue(0)
     for which in range(outputs):
         if which + 1 < outputs:
             issue(which + 1)
-        out_refs[which // share][which % share] = multiply(which)
-
-
-def products(name, parts, first, outputs, lists, left, panel):
+        out_ref[which] = multiply(which)
+
+
+def products(name, first, outputs, matches, slots, left, panel):
     size = left.shape[1]
-    slots = lists[1].shape[0] // lists[0].shape[0]
-    smem = pl.BlockSpec(memory_space=pltpu.SMEM)
     vmem = pl.BlockSpec(memory_space=pltpu.VMEM)
-    shape = jax.ShapeDtypeStruct((outputs // parts, size, size), jnp.float32)
     return pl.pallas_call(
-        functools.partial(product_kernel, first, outputs, slots),
-        out_shape=[shape] * parts,
-        in_specs=[smem] * 3 + [pl.BlockSpec(memory_space=pl.ANY)] * 2,
-        out_specs=[vmem] * parts,
+        functools.partial(product_kernel, first, outputs),
+        out_shape=jax.ShapeDtypeStruct((outputs, size, size), jnp.float32),
+        in_specs=[pl.BlockSpec(memory_space=pltpu.SMEM)]
+        + [pl.BlockSpec(memory_space=pl.ANY)] * 2,
+        out_specs=vmem,
         scratch_shapes=[
             pltpu.VMEM((2, slots, size, size), jnp.float32),
             pltpu.VMEM((2, slots, size, 2 * size), jnp.bfloat16),
@@ -161,11 +160,11 @@
         ],
         compiler_params=pltpu.CompilerParams(vmem_limit_bytes=52 * 1024 * 1024),
         cost_estimate=pl.CostEstimate(
-            flops=outputs * 16 * 8 * size**3, bytes_accessed=outputs * 16 * 4 * size**2,
+            flops=outputs * 16 * 8 * size**3, bytes_accessed=outputs * 16 * 8 * size**2,
             transcendentals=0,
         ),
         name=name,
-    )(*lists, left, panel)
+    )(matches, left, panel)
 
 
 def with_index(values, index):
@@ -209,30 +208,40 @@
     me = lax.axis_index("layer")
     rows_here, cols_here = out_rows[0, 0], out_cols[0, 0]
 
-    def quarter(array, away):
-        start = lax.rem(me + away, layer_count) * share
-        return lax.dynamic_slice_in_dim(array, start, share)
-
-    order = [2, 1, 3, 0]
-    rows = jnp.concatenate([quarter(rows_here, away) for away in order])
-    cols = jnp.concatenate([quarter(cols_here, away) for away in order])
-    lists = match_lists(rows, cols, left_keys, right_keys, right_base, block_rows)
+    def quarter(array, which):
+        return lax.dynamic_slice_in_dim(array, which * share, share)
+
+    def partners(layer, core):
+        near, far = layer ^ 1, layer_count - 1 - layer
+        return near + core * (far - near), far + core * (near - far)
+
+    def trade(value, step):
+        pairs = []
+        for col in range(lax.axis_size("col")):
+            for layer in range(layer_count):
+                to = partners(layer, col % 2)[step]
+                pairs.append((col * layer_count + layer, col * layer_count + to))
+        return lax.ppermute(value, ("col", "layer"), pairs)
+
+    core = lax.rem(lax.axis_index("col"), 2)
+    one, two = partners(me, core)
+    order = [partners(one, core)[1], one, two, me]
+    rows = jnp.concatenate([quarter(rows_here, which) for which in order])
+    cols = jnp.concatenate([quarter(cols_here, which) for which in order])
+    matches = match_lists(rows, cols, left_keys, right_keys, right_base, block_rows)
     panel = split_panel(pieces, half * block_cols, size)
 
-    far_low, far_high = products("far_blocks", 2, 0, share, lists, left, panel)
-    from_last = shift(far_low, "layer", 1)
-    from_next = shift(far_high, "layer", -1)
-    up_low, up_high, down_low, down_high = products(
-        "near_blocks", 4, share, 2 * share, lists, left, panel
-    )
-    up_high_in, down_low_in = shift(up_high, "layer", 1), shift(down_low, "layer", -1)
-    up_low_in = shift(up_low + from_last, "layer", 1)
-    down_high_in = shift(down_high + from_next, "layer", -1)
-    (own,) = products("own_blocks", 1, 3 * share, share, lists, left, panel)
-    mine = own + jnp.concatenate([up_low_in + down_low_in, up_high_in + down_high_in])
+    def blocks(name, number):
+        slots = right_base.shape[0]
+        return products(name, number * share, share, matches, slots, left, panel)
+
+    passed = trade(blocks("passed_blocks", 0), 0)
+    partner = trade(blocks("partner_blocks", 1), 0)
+    second = trade(blocks("second_blocks", 2) + passed, 1)
+    mine = blocks("own_blocks", 3) + partner + second
 
     squared = mine * mine
-    cols_mine = quarter(cols_here, 0)
+    cols_mine = quarter(cols_here, me)
     column_hot = (cols_mine[:, None] == jnp.arange(block_cols, dtype=jnp.int32)[None, :]).astype(
         jnp.float32
     )

time: 216 us -> 207 us (0.958)
  the two profiles are of different devices: /device:TPU:64 before, /device:TPU:32 now
where the time goes in v4:
time: 207 us
  waiting for transfers between devices  53.3 us (26%)
  blocking collectives  51 us (25%)
  starting transfers between devices  37.4 us (18%)
  Pallas kernels  33.4 us (16%)
  between operations  14.9 us (7%)
  local copies, waits for them, and re-layouts  11.9 us (6%)
  other arithmetic  4.93 us (2%)
    psum x2, blocking collectives, local(): colsum = lax.psum(lax.psum(local_sums, 'layer'), 'row')  33.4 us
    ppermute x6, waiting for transfers between devices, shift(): lax.ppermute(value, axis, [(i, (i + by) % count) for i in range(count)])  30.1 us
    pallas_call x4, Pallas kernels, products(): pl.pallas_call(functools.partial(product_kernel, first, outputs), out_sha...  22.8 us
    ppermute x6, starting transfers between devices, shift(): lax.ppermute(value, axis, [(i, (i + by) % count) for i in range(count)])  19.9 us
    all_gather x1, blocking collectives, local(): left_keys = lax.all_gather(left_index, 'col', axis=0, tiled=True)  17.6 us
    ppermute x3, starting transfers between devices, trade(): return lax.ppermute(value, ('col', 'layer'), pairs)  17.4 us
    all_gather x1, waiting for transfers between devices, local(): lax.all_gather(a_values.reshape(block_rows, size, lanes), 'col', axis=0,...  15.7 us
    ppermute x3, waiting for transfers between devices, trade(): return lax.ppermute(value, ('col', 'layer'), pairs)  6.73 us
  transfers between devices with their start and end apart: 10, of which 7 were waited for; matrix products, arithmetic and copies ran while one was open for 6% of the time, Pallas kernels for 14%

profile of v4, /device:TPU:32, one launch (start us, length us, event | category | flops | bytes accessed | tf_op | source)
XLA Modules:
  0.0 207.2 jit_solution(5953982554887232666)
XLA Ops:
  6.5 0.7 all-gather.4.cloned.1.call-update
  7.3 0.8 slice_convert_fusion
  8.1 0.1 copy.14
  8.2 0.1 convert_element_type.23
  8.3 2.7 %fusion.17 = (f32[1,4,4,128,128]{4,3,2,1,0:T(8,128)}, f32[1,4,4,128,128]{4,3,2,1,0:T(8,128)S(1)}) fusion(f32[1,8,4,128,128]{4,3,2,1,0:T(8,128)} %param.13), kind=kLoop, calls=%fused_computation.45 | loop fusion | bytes 4194304 | tf_op jit(solution)/shard_map/slice | solution.py:195
  11.0 3.4 %collective-permute-start = (f32[2056,128]{1,0:T(8,128)S(1)}, f32[2056,128]{1,0:T(8,128)S(1)}, u32[]{:S(2)}, u32[]{:S(2)}) collective-permute-start(f32[2056,128]{1,0:T(8,128)S(1)} %pad_maximum_fusion.refs_0_), channel_id=1, source_target_pairs={{0,128},{128,256},{256,384},{384,0},{1,129},{129,257},{257,385},{3... | collective-permute-start | bytes 3158024 | tf_op jit(solution)/shard_map/ppermute | solution.py:178
  14.4 0.1 copy.15
  14.5 0.1 convert_element_type.27
  14.7 1.3 pad_maximum_fusion.1.refs_1_
  16.0 3.7 %collective-permute-start.3 = (f32[2056,128]{1,0:T(8,128)S(1)}, f32[2056,128]{1,0:T(8,128)}, u32[]{:S(2)}, u32[]{:S(2)}) collective-permute-start(f32[2056,128]{1,0:T(8,128)S(1)} %pad_maximum_fusion.1.refs_1_), channel_id=1, source_target_pairs={{0,384},{128,0},{256,128},{384,256},{1,385},{129,1},{257,129},{385... | collective-permute-start | bytes 3158024 | tf_op jit(solution)/shard_map/ppermute | solution.py:178
  19.7 3.5 %collective-permute-start.2 = (f32[2056,128]{1,0:T(8,128)S(1)}, f32[2056,128]{1,0:T(8,128)}, u32[]{:S(2)}, u32[]{:S(2)}) collective-permute-start(f32[2056,128]{1,0:T(8,128)S(1)} %pad_maximum_fusion.refs_0_), channel_id=1, source_target_pairs={{0,384},{128,0},{256,128},{384,256},{1,385},{129,1},{257,129},{385... | collective-permute-start | bytes 3158024 | tf_op jit(solution)/shard_map/ppermute | solution.py:178
  23.1 2.4 %collective-permute-start.1 = (f32[2056,128]{1,0:T(8,128)S(1)}, f32[2056,128]{1,0:T(8,128)}, u32[]{:S(2)}, u32[]{:S(2)}) collective-permute-start(f32[2056,128]{1,0:T(8,128)S(1)} %pad_maximum_fusion.1.refs_1_), channel_id=1, source_target_pairs={{0,128},{128,256},{256,384},{384,0},{1,129},{129,257},{257,385},{3... | collective-permute-start | bytes 3158024 | tf_op jit(solution)/shard_map/ppermute | solution.py:178
  25.7 0.5 fusion.14.right_base
  26.4 1.3 dynamic-slice.22
  28.3 0.6 pad_add_fusion
  28.9 11.3 %collective-permute-done.refs_2_ = f32[2056,128]{1,0:T(8,128)S(1)} collective-permute-done((f32[2056,128]{1,0:T(8,128)S(1)}, f32[2056,128]{1,0:T(8,128)S(1)}, u32[]{:S(2)}, u32[]{:S(2)}) %collective-permute-start) | collective-permute-done | bytes 1052704 | tf_op jit(solution)/shard_map/ppermute | solution.py:178
  40.3 0.6 slice.70
  41.5 2.2 %collective-permute-start.4 = (f32[2056,128]{1,0:T(8,128)S(1)}, f32[2056,128]{1,0:T(8,128)}, u32[]{:S(2)}, u32[]{:S(2)}) collective-permute-start(f32[2056,128]{1,0:T(8,128)S(1)} %collective-permute-done.refs_2_), channel_id=1, source_target_pairs={{0,128},{128,256},{256,384},{384,0},{1,129},{129,257},{257,385},{3... | collective-permute-start | bytes 3158024 | tf_op jit(solution)/shard_map/ppermute | solution.py:178
  43.7 0.5 collective-permute-done.3.refs_5_
  44.2 4.9 %collective-permute-start.5 = (f32[2056,128]{1,0:T(8,128)}, f32[2056,128]{1,0:T(8,128)}, u32[]{:S(2)}, u32[]{:S(2)}) collective-permute-start(f32[2056,128]{1,0:T(8,128)} %collective-permute-done.3.refs_5_), channel_id=1, source_target_pairs={{0,384},{128,0},{256,128},{384,256},{1,385},{129,1},{257,129},{385... | collective-permute-start | bytes 3158024 | tf_op jit(solution)/shard_map/ppermute | solution.py:178
  49.1 0.1 bitcast_dynamic-update-slice_fusion
  49.2 17.6 %all-reduce.2.left_keys = s32[256]{0:T(256)} all-reduce(s32[256]{0:T(256)S(1)} %bitcast_dynamic-update-slice_fusion), channel_id=2, replica_groups=mesh['row'=4,'col'=32,'layer'=4] {'col'}, use_global_device_ids=true, to_apply=%add.2 | all-reduce | flops 256 | bytes 2048 | tf_op jit(solution)/shard_map/all_gather | solution.py:203
  66.8 0.7 slice_bitcast_fusion.2
  67.5 0.7 slice_bitcast_fusion.3
  68.1 0.7 slice_bitcast_fusion.4
  68.8 15.5 %collective-permute-done.4.refs_6_ = f32[2056,128]{1,0:T(8,128)} collective-permute-done((f32[2056,128]{1,0:T(8,128)S(1)}, f32[2056,128]{1,0:T(8,128)}, u32[]{:S(2)}, u32[]{:S(2)}) %collective-permute-start.4) | collective-permute-done | bytes 1052704 | tf_op jit(solution)/shard_map/ppermute | solution.py:178
  84.3 0.7 slice_bitcast_fusion.1
  85.0 2.8 %collective-permute-done.5.refs_7_ = f32[2056,128]{1,0:T(8,128)} collective-permute-done((f32[2056,128]{1,0:T(8,128)}, f32[2056,128]{1,0:T(8,128)}, u32[]{:S(2)}, u32[]{:S(2)}) %collective-permute-start.5) | collective-permute-done | bytes 1052704 | tf_op jit(solution)/shard_map/ppermute | solution.py:178
  87.8 0.7 slice_bitcast_fusion
  88.6 0.6 convert_element_type.28.right_keys
  89.2 6.1 %match_lists.1.matches = s32[528]{0:T(1024)} custom-call(s32[16]{0:T(128)} %get-tuple-element.41.rows_ref, s32[16]{0:T(128)} %get-tuple-element.42.cols_ref, s32[256]{0:T(256)} %all-reduce.2.left_keys, s32[128]{0:T(128)} %convert_element_type.28.right_keys, s32[32]{0:T(128)} %fusion.14.right_base), custom_call_target="tpu_custom_call" | custom-call | tf_op jit(solution)/shard_map/match_lists/pallas_call | solution.py:44
  95.3 4.5 %split_panel.1.panel = bf16[128,128,256]{2,1,0:T(8,128)(2,1)S(1)} custom-call(f32[2056,128]{1,0:T(8,128)S(1)} %pad_maximum_fusion.refs_0_, f32[2056,128]{1,0:T(8,128)S(1)} %pad_maximum_fusion.1.refs_1_, f32[2056,128]{1,0:T(8,128)S(1)} %collective-permute-done.refs_2_, f32[2056,128]{1,0:T(8,128)} %collective-permute-done.1.refs_3_, ...), custom_call_target="tpu_custom_call" | custom-call | tf_op jit(solution)/shard_map/split_panel/pallas_call | solution.py:72
  99.8 3.2 %copy-done = bf16[128,128,256]{2,1,0:T(8,128)(2,1)} copy-done((bf16[128,128,256]{2,1,0:T(8,128)(2,1)}, bf16[128,128,256]{2,1,0:T(8,128)(2,1)S(1)}, u32[]{:S(2)}) %copy-start) | copy-done | bytes 8388632
  103.0 15.7 %all-gather.4.cloned.1.call-done = f32[256,1,1,128,128]{4,3,2,1,0:T(8,128)} async-done(((f32[8,1,1,128,128]{4,3,2,1,0:T(8,128)}), f32[256,1,1,128,128]{4,3,2,1,0:T(8,128)}) %all-gather.4.cloned.1.call-update) | async-done | bytes 16777232 | tf_op jit(solution)/shard_map/all_gather | solution.py:193
  118.7 5.2 %passed_blocks.1 = f32[4,128,128]{2,1,0:T(8,128)S(1)} custom-call(s32[528]{0:T(1024)S(1)} %copy-done.1, f32[256,128,128]{2,1,0:T(8,128)} %bitcast.38, bf16[128,128,256]{2,1,0:T(8,128)(2,1)} %copy-done), custom_call_target="tpu_custom_call" | custom-call | flops 1073741824 | bytes 8388608 | tf_op jit(solution)/shard_map/passed_blocks/pallas_call | solution.py:149
  123.9 8.6 %collective-permute-start.7 = (f32[4,128,128]{2,1,0:T(8,128)S(1)}, f32[4,128,128]{2,1,0:T(8,128)S(1)}, u32[]{:S(2)}, u32[]{:S(2)}) collective-permute-start(f32[4,128,128]{2,1,0:T(8,128)S(1)} %passed_blocks.1), channel_id=1, source_target_pairs={{0,1},{1,0},{2,3},{3,2},{4,7},{5,6},{6,5},{7,4},{8,9},{9,8},{10,11... | collective-permute-start | bytes 786440 | tf_op jit(solution)/shard_map/ppermute | solution.py:224
  132.5 5.7 %partner_blocks.1 = f32[4,128,128]{2,1,0:T(8,128)S(1)} custom-call(s32[528]{0:T(1024)S(1)} %copy-done.1, f32[256,128,128]{2,1,0:T(8,128)} %bitcast.39, bf16[128,128,256]{2,1,0:T(8,128)(2,1)} %copy-done), custom_call_target="tpu_custom_call" | custom-call | flops 1073741824 | bytes 8388608 | tf_op jit(solution)/shard_map/partner_blocks/pallas_call | solution.py:149
  138.3 3.0 %collective-permute-start.6 = (f32[4,128,128]{2,1,0:T(8,128)S(1)}, f32[4,128,128]{2,1,0:T(8,128)S(1)}, u32[]{:S(2)}, u32[]{:S(2)}) collective-permute-start(f32[4,128,128]{2,1,0:T(8,128)S(1)} %partner_blocks.1), channel_id=1, source_target_pairs={{0,1},{1,0},{2,3},{3,2},{4,7},{5,6},{6,5},{7,4},{8,9},{9,8},{10,11... | collective-permute-start | bytes 786440 | tf_op jit(solution)/shard_map/ppermute | solution.py:224
  141.3 5.3 %second_blocks.1 = f32[4,128,128]{2,1,0:T(8,128)S(1)} custom-call(s32[528]{0:T(1024)S(1)} %copy-done.1, f32[256,128,128]{2,1,0:T(8,128)} %bitcast.40, bf16[128,128,256]{2,1,0:T(8,128)(2,1)} %copy-done), custom_call_target="tpu_custom_call" | custom-call | flops 1073741824 | bytes 8388608 | tf_op jit(solution)/shard_map/second_blocks/pallas_call | solution.py:149
  146.6 5.8 %collective-permute-start.8 = (f32[4,128,128]{2,1,0:T(8,128)S(1)}, f32[4,128,128]{2,1,0:T(8,128)S(1)}, u32[]{:S(2)}, u32[]{:S(2)}) collective-permute-start(f32[4,128,128]{2,1,0:T(8,128)S(1)} %add.92), channel_id=1, source_target_pairs={{0,3},{1,2},{2,1},{3,0},{4,5},{5,4},{6,7},{7,6},{8,11},{9,10},{10,... | collective-permute-start | bytes 786440 | tf_op jit(solution)/shard_map/ppermute | solution.py:224
  152.4 6.6 %own_blocks.1 = f32[4,128,128]{2,1,0:T(8,128)S(1)} custom-call(s32[528]{0:T(1024)S(1)} %copy-done.1, f32[256,128,128]{2,1,0:T(8,128)} %bitcast.41, bf16[128,128,256]{2,1,0:T(8,128)(2,1)} %copy-done), custom_call_target="tpu_custom_call" | custom-call | flops 1073741824 | bytes 8388608 | tf_op jit(solution)/shard_map/own_blocks/pallas_call | solution.py:149
  159.0 4.5 %collective-permute-done.6 = f32[4,128,128]{2,1,0:T(8,128)S(1)} collective-permute-done((f32[4,128,128]{2,1,0:T(8,128)S(1)}, f32[4,128,128]{2,1,0:T(8,128)S(1)}, u32[]{:S(2)}, u32[]{:S(2)}) %collective-permute-start.6) | collective-permute-done | bytes 262176 | tf_op jit(solution)/shard_map/ppermute | solution.py:224
  163.5 2.2 %collective-permute-done.8 = f32[4,128,128]{2,1,0:T(8,128)S(1)} collective-permute-done((f32[4,128,128]{2,1,0:T(8,128)S(1)}, f32[4,128,128]{2,1,0:T(8,128)S(1)}, u32[]{:S(2)}, u32[]{:S(2)}) %collective-permute-start.8) | collective-permute-done | bytes 262176 | tf_op jit(solution)/shard_map/ppermute | solution.py:224
  165.8 0.3 fusion.1
  166.1 14.8 %psum.14 = f32[4,128]{1,0:T(4,128)S(1)} all-reduce(f32[4,128]{1,0:T(4,128)S(1)} %fusion.1), channel_id=1, replica_groups=mesh['row'=4,'col'=32,'layer'=4] {'layer'}, use_global_device_ids=true, to_apply=%region_1.0 | all-reduce | flops 512 | bytes 4096 | tf_op jit(solution)/shard_map/psum | solution.py:251
  180.8 18.6 %psum.15 = f32[4,128]{1,0:T(4,128)S(1)} all-reduce(f32[4,128]{1,0:T(4,128)S(1)} %psum.14), channel_id=1, replica_groups=mesh['row'=4,'col'=32,'layer'=4] {'row'}, use_global_device_ids=true, to_apply=%region_2.0 | all-reduce | flops 512 | bytes 4096 | tf_op jit(solution)/shard_map/psum | solution.py:251
  199.4 0.2 convolution_divide_fusion
  199.6 0.8 multiply_bitcast_fusion
  (30 shorter events, 0.6 us)
Async XLA Ops:
  6.5 112.2 %all-gather.4.cloned.1.call-start = ((), (), s32[]{:S(2)}) async-start(), calls=%async_computation | async-start | bytes 17301504 | tf_op jit(solution)/shard_map/all_gather | solution.py:193
  11.0 29.2 %collective-permute-start = (f32[2056,128]{1,0:T(8,128)S(1)}, f32[2056,128]{1,0:T(8,128)S(1)}, u32[]{:S(2)}, u32[]{:S(2)}) collective-permute-start(f32[2056,128]{1,0:T(8,128)S(1)} %pad_maximum_fusion.refs_0_), channel_id=1, source_target_pairs={{0,128},{128,256},{256,384},{384,0},{1,129},{129,257},{257,385},{3... | collective-permute-start | bytes 3158024 | tf_op jit(solution)/shard_map/ppermute | solution.py:178
  14.6 10.9 %copy-start.5 = (s32[8]{0:T(128)S(1)}, s32[8]{0:T(128)}, u32[]{:S(2)}) copy-start(s32[8]{0:T(128)} %constant.92.clone) | copy-start | bytes 100
  14.6 11.6 %copy-start.2 = (s32[1,1,16]{2,1,0:T(1,128)S(1)}, s32[1,1,16]{2,1,0:T(1,128)}, u32[]{:S(2)}) copy-start(s32[1,1,16]{2,1,0:T(1,128)} %param.16) | copy-start | bytes 196
  14.6 11.7 %copy-start.3 = (s32[1,1,16]{2,1,0:T(1,128)S(1)}, s32[1,1,16]{2,1,0:T(1,128)}, u32[]{:S(2)}) copy-start(s32[1,1,16]{2,1,0:T(1,128)} %param.15) | copy-start | bytes 196
  14.7 34.4 %copy-start.4 = (s32[8,1,1]{0,2,1:T(1,128)S(1)}, s32[8,1,1]{0,2,1:T(1,128)}, u32[]{:S(2)}) copy-start(s32[8,1,1]{0,2,1:T(1,128)} %param.12) | copy-start | bytes 100
  16.0 28.2 %collective-permute-start.3 = (f32[2056,128]{1,0:T(8,128)S(1)}, f32[2056,128]{1,0:T(8,128)}, u32[]{:S(2)}, u32[]{:S(2)}) collective-permute-start(f32[2056,128]{1,0:T(8,128)S(1)} %pad_maximum_fusion.1.refs_1_), channel_id=1, source_target_pairs={{0,384},{128,0},{256,128},{384,256},{1,385},{129,1},{257,129},{385... | collective-permute-start | bytes 3158024 | tf_op jit(solution)/shard_map/ppermute | solution.py:178
  19.7 47.8 %collective-permute-start.2 = (f32[2056,128]{1,0:T(8,128)S(1)}, f32[2056,128]{1,0:T(8,128)}, u32[]{:S(2)}, u32[]{:S(2)}) collective-permute-start(f32[2056,128]{1,0:T(8,128)S(1)} %pad_maximum_fusion.refs_0_), channel_id=1, source_target_pairs={{0,384},{128,0},{256,128},{384,256},{1,385},{129,1},{257,129},{385... | collective-permute-start | bytes 3158024 | tf_op jit(solution)/shard_map/ppermute | solution.py:178
  23.1 45.0 %collective-permute-start.1 = (f32[2056,128]{1,0:T(8,128)S(1)}, f32[2056,128]{1,0:T(8,128)}, u32[]{:S(2)}, u32[]{:S(2)}) collective-permute-start(f32[2056,128]{1,0:T(8,128)S(1)} %pad_maximum_fusion.1.refs_1_), channel_id=1, source_target_pairs={{0,128},{128,256},{256,384},{384,0},{1,129},{129,257},{257,385},{3... | collective-permute-start | bytes 3158024 | tf_op jit(solution)/shard_map/ppermute | solution.py:178
  41.5 42.8 %collective-permute-start.4 = (f32[2056,128]{1,0:T(8,128)S(1)}, f32[2056,128]{1,0:T(8,128)}, u32[]{:S(2)}, u32[]{:S(2)}) collective-permute-start(f32[2056,128]{1,0:T(8,128)S(1)} %collective-permute-done.refs_2_), channel_id=1, source_target_pairs={{0,128},{128,256},{256,384},{384,0},{1,129},{129,257},{257,385},{3... | collective-permute-start | bytes 3158024 | tf_op jit(solution)/shard_map/ppermute | solution.py:178
  44.2 43.7 %collective-permute-start.5 = (f32[2056,128]{1,0:T(8,128)}, f32[2056,128]{1,0:T(8,128)}, u32[]{:S(2)}, u32[]{:S(2)}) collective-permute-start(f32[2056,128]{1,0:T(8,128)} %collective-permute-done.3.refs_5_), channel_id=1, source_target_pairs={{0,384},{128,0},{256,128},{384,256},{1,385},{129,1},{257,129},{385... | collective-permute-start | bytes 3158024 | tf_op jit(solution)/shard_map/ppermute | solution.py:178
  95.3 23.4 %copy-start.1 = (s32[528]{0:T(1024)S(1)}, s32[528]{0:T(1024)}, u32[]{:S(2)}) copy-start(s32[528]{0:T(1024)} %match_lists.1.matches) | copy-start | bytes 6340
  99.8 3.2 %copy-start = (bf16[128,128,256]{2,1,0:T(8,128)(2,1)}, bf16[128,128,256]{2,1,0:T(8,128)(2,1)S(1)}, u32[]{:S(2)}) copy-start(bf16[128,128,256]{2,1,0:T(8,128)(2,1)S(1)} %split_panel.1.panel) | copy-start | bytes 25165828
  123.9 22.7 %collective-permute-start.7 = (f32[4,128,128]{2,1,0:T(8,128)S(1)}, f32[4,128,128]{2,1,0:T(8,128)S(1)}, u32[]{:S(2)}, u32[]{:S(2)}) collective-permute-start(f32[4,128,128]{2,1,0:T(8,128)S(1)} %passed_blocks.1), channel_id=1, source_target_pairs={{0,1},{1,0},{2,3},{3,2},{4,7},{5,6},{6,5},{7,4},{8,9},{9,8},{10,11... | collective-permute-start | bytes 786440 | tf_op jit(solution)/shard_map/ppermute | solution.py:224
  138.3 25.2 %collective-permute-start.6 = (f32[4,128,128]{2,1,0:T(8,128)S(1)}, f32[4,128,128]{2,1,0:T(8,128)S(1)}, u32[]{:S(2)}, u32[]{:S(2)}) collective-permute-start(f32[4,128,128]{2,1,0:T(8,128)S(1)} %partner_blocks.1), channel_id=1, source_target_pairs={{0,1},{1,0},{2,3},{3,2},{4,7},{5,6},{6,5},{7,4},{8,9},{9,8},{10,11... | collective-permute-start | bytes 786440 | tf_op jit(solution)/shard_map/ppermute | solution.py:224
  146.6 19.2 %collective-permute-start.8 = (f32[4,128,128]{2,1,0:T(8,128)S(1)}, f32[4,128,128]{2,1,0:T(8,128)S(1)}, u32[]{:S(2)}, u32[]{:S(2)}) collective-permute-start(f32[4,128,128]{2,1,0:T(8,128)S(1)} %add.92), channel_id=1, source_target_pairs={{0,3},{1,2},{2,1},{3,0},{4,5},{5,4},{6,7},{7,6},{8,11},{9,10},{10,... | collective-permute-start | bytes 786440 | tf_op jit(solution)/shard_map/ppermute | solution.py:224
Sparse Core Ops, SparseCore 0:
  9.5 109.1 all-gather.3

commit v5 on v4

--- a/solution.py
+++ b/solution.py
@@ -9,6 +9,7 @@
 
 KB_C = 2
 CHUNK = 8
+VMEM_GRANT = 42 * 1024 * 1024
 
 
 def halves(value):
@@ -79,28 +80,32 @@
     )(*pieces)
 
 
-def product_kernel(first, outputs, matches, left_ref, panel, out_ref, left_buf, right_buf,
-                   left_sem, right_sem):
+def product_kernel(first, outputs, keep, *refs):
+    if keep:
+        (matches, left_ref, panel, out_ref, panel_out, left_buf, left_sem, right_buf, right_sem,
+         panel_sem) = refs
+    else:
+        matches, left_ref, panel, out_ref, left_buf, left_sem = refs
     size = left_ref.shape[1]
     blocks = panel.shape[0]
     slots = left_buf.shape[1]
     total_outputs = matches.shape[0] // (slots + 1)
 
-    def copies(which, spot, left_place, right_place):
+    def copies(which, spot, match):
         buf = which % 2
-        return (
-            pltpu.make_async_copy(
-                left_ref.at[left_place], left_buf.at[buf, spot], left_sem.at[buf, spot]
-            ),
-            pltpu.make_async_copy(
-                panel.at[right_place], right_buf.at[buf, spot], right_sem.at[buf, spot]
-            ),
+        left = pltpu.make_async_copy(
+            left_ref.at[lax.div(match, blocks)], left_buf.at[buf, spot], left_sem.at[buf, spot]
         )
+        if not keep:
+            return [left]
+        right = pltpu.make_async_copy(
+            panel.at[lax.rem(match, blocks)], right_buf.at[buf, spot], right_sem.at[buf, spot]
+        )
+        return [left, right]
 
     def issue(which):
         def one(spot, carry):
-            match = matches[(first + which) * slots + spot]
-            for copy in copies(which, spot, lax.div(match, blocks), lax.rem(match, blocks)):
+            for copy in copies(which, spot, matches[(first + which) * slots + spot]):
                 copy.start()
             return carry
 
@@ -112,19 +117,26 @@
         chunks = (count + CHUNK - 1) // CHUNK
 
         def arrive(spot, carry):
-            for copy in copies(which, spot, 0, 0):
+            for copy in copies(which, spot, 0):
                 copy.wait()
             return carry
 
         def clear(spot, carry):
             left_buf[buf, spot] = zero
-            right_buf[buf, spot] = jnp.zeros((size, 2 * size), jnp.bfloat16)
-            return carry
+            if keep:
+                right_buf[buf, spot] = jnp.zeros((size, 2 * size), jnp.bfloat16)
+            return carry
+
+        def right_block(spot):
+            if keep:
+                return right_buf[buf, spot]
+            match = matches[(first + which) * slots + spot]
+            return panel[jnp.where(spot < count, lax.rem(match, blocks), 0)]
 
         def one(chunk, total):
             base = chunk * CHUNK
             left = [left_buf[buf, base + part] for part in range(CHUNK)]
-            right = [right_buf[buf, base + part] for part in range(CHUNK)]
+            right = [right_block(base + part) for part in range(CHUNK)]
             high, low = halves(jnp.concatenate(left, axis=1))
             both = jnp.dot(
                 jnp.concatenate([high, low], axis=0), jnp.concatenate(right, axis=0),
@@ -137,28 +149,41 @@
         return lax.fori_loop(0, chunks, one, zero)
 
     issue(0)
+    if keep:
+        whole = pltpu.make_async_copy(panel, panel_out, panel_sem.at[0])
+        whole.start()
     for which in range(outputs):
         if which + 1 < outputs:
             issue(which + 1)
         out_ref[which] = multiply(which)
-
-
-def products(name, first, outputs, matches, slots, left, panel):
+    if keep:
+        whole.wait()
+
+
+def products(name, first, outputs, keep, matches, slots, left, panel):
     size = left.shape[1]
+    smem = pl.BlockSpec(memory_space=pltpu.SMEM)
     vmem = pl.BlockSpec(memory_space=pltpu.VMEM)
-    return pl.pallas_call(
-        functools.partial(product_kernel, first, outputs),
-        out_shape=jax.ShapeDtypeStruct((outputs, size, size), jnp.float32),
-        in_specs=[pl.BlockSpec(memory_space=pltpu.SMEM)]
-        + [pl.BlockSpec(memory_space=pl.ANY)] * 2,
-        out_specs=vmem,
-        scratch_shapes=[
-            pltpu.VMEM((2, slots, size, size), jnp.float32),
+    hbm = pl.BlockSpec(memory_space=pl.ANY)
+    out_shape = [jax.ShapeDtypeStruct((outputs, size, size), jnp.float32)]
+    scratch = [
+        pltpu.VMEM((2, slots, size, size), jnp.float32),
+        pltpu.SemaphoreType.DMA((2, slots)),
+    ]
+    if keep:
+        out_shape.append(jax.ShapeDtypeStruct(panel.shape, panel.dtype))
+        scratch += [
             pltpu.VMEM((2, slots, size, 2 * size), jnp.bfloat16),
             pltpu.SemaphoreType.DMA((2, slots)),
-            pltpu.SemaphoreType.DMA((2, slots)),
-        ],
-        compiler_params=pltpu.CompilerParams(vmem_limit_bytes=52 * 1024 * 1024),
+            pltpu.SemaphoreType.DMA((1,)),
+        ]
+    return pl.pallas_call(
+        functools.partial(product_kernel, first, outputs, keep),
+        out_shape=out_shape,
+        in_specs=[smem, hbm, hbm if keep else vmem],
+        out_specs=[vmem] * len(out_shape),
+        scratch_shapes=scratch,
+        compiler_params=pltpu.CompilerParams(vmem_limit_bytes=VMEM_GRANT),
         cost_estimate=pl.CostEstimate(
             flops=outputs * 16 * 8 * size**3, bytes_accessed=outputs * 16 * 8 * size**2,
             transcendentals=0,
@@ -231,14 +256,15 @@
     matches = match_lists(rows, cols, left_keys, right_keys, right_base, block_rows)
     panel = split_panel(pieces, half * block_cols, size)
 
-    def blocks(name, number):
+    def blocks(name, number, keep, panel):
         slots = right_base.shape[0]
-        return products(name, number * share, share, matches, slots, left, panel)
-
-    passed = trade(blocks("passed_blocks", 0), 0)
-    partner = trade(blocks("partner_blocks", 1), 0)
-    second = trade(blocks("second_blocks", 2) + passed, 1)
-    mine = blocks("own_blocks", 3) + partner + second
+        return products(name, number * share, share, keep, matches, slots, left, panel)
+
+    first, panel = blocks("passed_blocks", 0, True, panel)
+    passed = trade(first, 0)
+    partner = trade(blocks("partner_blocks", 1, False, panel)[0], 0)
+    second = trade(blocks("second_blocks", 2, False, panel)[0] + passed, 1)
+    mine = blocks("own_blocks", 3, False, panel)[0] + partner + second
 
     squared = mine * mine
     cols_mine = quarter(cols_here, me)

time: 207 us -> 209 us (level)
  transfers between devices with their start and end apart: 10 -> 10, of which waited for: 7 -> 7; matrix products, arithmetic and copies ran while one was open for 6% -> 6% of each run, Pallas kernels for 14% -> 13%
where the time goes in v5:
time: 209 us; the launch traced here: 208 us
  waiting for transfers between devices  53.6 us (26%)
  blocking collectives  50.7 us (24%)
  starting transfers between devices  35.9 us (17%)
  Pallas kernels  35 us (17%)
  between operations  15 us (7%)
  local copies, waits for them, and re-layouts  12 us (6%)
  other arithmetic  4.93 us (2%)
    psum x2, blocking collectives, local(): colsum = lax.psum(lax.psum(local_sums, 'layer'), 'row')  33.2 us
    ppermute x6, waiting for transfers between devices, shift(): lax.ppermute(value, axis, [(i, (i + by) % count) for i in range(count)])  30 us
    pallas_call x4, Pallas kernels, products(): pl.pallas_call(functools.partial(product_kernel, first, outputs, keep), o...  24.4 us
    ppermute x6, starting transfers between devices, shift(): lax.ppermute(value, axis, [(i, (i + by) % count) for i in range(count)])  19.9 us
    all_gather x1, blocking collectives, local(): left_keys = lax.all_gather(left_index, 'col', axis=0, tiled=True)  17.6 us
    ppermute x3, starting transfers between devices, trade(): return lax.ppermute(value, ('col', 'layer'), pairs)  16 us
    all_gather x1, waiting for transfers between devices, local(): lax.all_gather(a_values.reshape(block_rows, size, lanes), 'col', axis=0,...  15.7 us
    ppermute x3, waiting for transfers between devices, trade(): return lax.ppermute(value, ('col', 'layer'), pairs)  7.14 us
  transfers between devices with their start and end apart: 10, of which 7 were waited for; matrix products, arithmetic and copies ran while one was open for 6% of the time, Pallas kernels for 13%

profile of v5, /device:TPU:32, one launch (start us, length us, event | category | flops | bytes accessed | tf_op | source)
XLA Modules:
  0.0 207.5 jit_solution(14262531082467017301)
XLA Ops:
  6.5 0.7 all-gather.4.cloned.1.call-update
  7.3 0.8 slice_convert_fusion
  8.1 0.1 copy.14
  8.2 0.1 convert_element_type.23
  8.3 2.7 %fusion.17 = (f32[1,4,4,128,128]{4,3,2,1,0:T(8,128)}, f32[1,4,4,128,128]{4,3,2,1,0:T(8,128)S(1)}) fusion(f32[1,8,4,128,128]{4,3,2,1,0:T(8,128)} %param.13), kind=kLoop, calls=%fused_computation.45 | loop fusion | bytes 4194304 | tf_op jit(solution)/shard_map/slice | solution.py:220
  11.0 3.4 %collective-permute-start = (f32[2056,128]{1,0:T(8,128)S(1)}, f32[2056,128]{1,0:T(8,128)S(1)}, u32[]{:S(2)}, u32[]{:S(2)}) collective-permute-start(f32[2056,128]{1,0:T(8,128)S(1)} %pad_maximum_fusion.refs_0_), channel_id=1, source_target_pairs={{0,128},{128,256},{256,384},{384,0},{1,129},{129,257},{257,385},{3... | collective-permute-start | bytes 3158024 | tf_op jit(solution)/shard_map/ppermute | solution.py:203
  14.4 0.1 copy.15
  14.5 0.1 convert_element_type.27
  14.7 1.3 pad_maximum_fusion.1.refs_1_
  16.0 3.7 %collective-permute-start.3 = (f32[2056,128]{1,0:T(8,128)S(1)}, f32[2056,128]{1,0:T(8,128)}, u32[]{:S(2)}, u32[]{:S(2)}) collective-permute-start(f32[2056,128]{1,0:T(8,128)S(1)} %pad_maximum_fusion.1.refs_1_), channel_id=1, source_target_pairs={{0,384},{128,0},{256,128},{384,256},{1,385},{129,1},{257,129},{385... | collective-permute-start | bytes 3158024 | tf_op jit(solution)/shard_map/ppermute | solution.py:203
  19.7 3.5 %collective-permute-start.2 = (f32[2056,128]{1,0:T(8,128)S(1)}, f32[2056,128]{1,0:T(8,128)}, u32[]{:S(2)}, u32[]{:S(2)}) collective-permute-start(f32[2056,128]{1,0:T(8,128)S(1)} %pad_maximum_fusion.refs_0_), channel_id=1, source_target_pairs={{0,384},{128,0},{256,128},{384,256},{1,385},{129,1},{257,129},{385... | collective-permute-start | bytes 3158024 | tf_op jit(solution)/shard_map/ppermute | solution.py:203
  23.1 2.4 %collective-permute-start.1 = (f32[2056,128]{1,0:T(8,128)S(1)}, f32[2056,128]{1,0:T(8,128)}, u32[]{:S(2)}, u32[]{:S(2)}) collective-permute-start(f32[2056,128]{1,0:T(8,128)S(1)} %pad_maximum_fusion.1.refs_1_), channel_id=1, source_target_pairs={{0,128},{128,256},{256,384},{384,0},{1,129},{129,257},{257,385},{3... | collective-permute-start | bytes 3158024 | tf_op jit(solution)/shard_map/ppermute | solution.py:203
  25.7 0.6 fusion.14.right_base
  26.5 1.3 dynamic-slice.22
  28.4 0.6 pad_add_fusion
  29.0 11.3 %collective-permute-done.refs_2_ = f32[2056,128]{1,0:T(8,128)S(1)} collective-permute-done((f32[2056,128]{1,0:T(8,128)S(1)}, f32[2056,128]{1,0:T(8,128)S(1)}, u32[]{:S(2)}, u32[]{:S(2)}) %collective-permute-start) | collective-permute-done | bytes 1052704 | tf_op jit(solution)/shard_map/ppermute | solution.py:203
  40.3 0.7 slice.70
  41.6 2.2 %collective-permute-start.4 = (f32[2056,128]{1,0:T(8,128)S(1)}, f32[2056,128]{1,0:T(8,128)}, u32[]{:S(2)}, u32[]{:S(2)}) collective-permute-start(f32[2056,128]{1,0:T(8,128)S(1)} %collective-permute-done.refs_2_), channel_id=1, source_target_pairs={{0,128},{128,256},{256,384},{384,0},{1,129},{129,257},{257,385},{3... | collective-permute-start | bytes 3158024 | tf_op jit(solution)/shard_map/ppermute | solution.py:203
  43.8 0.3 collective-permute-done.3.refs_5_
  44.2 4.9 %collective-permute-start.5 = (f32[2056,128]{1,0:T(8,128)}, f32[2056,128]{1,0:T(8,128)}, u32[]{:S(2)}, u32[]{:S(2)}) collective-permute-start(f32[2056,128]{1,0:T(8,128)} %collective-permute-done.3.refs_5_), channel_id=1, source_target_pairs={{0,384},{128,0},{256,128},{384,256},{1,385},{129,1},{257,129},{385... | collective-permute-start | bytes 3158024 | tf_op jit(solution)/shard_map/ppermute | solution.py:203
  49.0 0.1 bitcast_dynamic-update-slice_fusion
  49.2 17.6 %all-reduce.2.left_keys = s32[256]{0:T(256)} all-reduce(s32[256]{0:T(256)S(1)} %bitcast_dynamic-update-slice_fusion), channel_id=2, replica_groups=mesh['row'=4,'col'=32,'layer'=4] {'col'}, use_global_device_ids=true, to_apply=%add.2 | all-reduce | flops 256 | bytes 2048 | tf_op jit(solution)/shard_map/all_gather | solution.py:228
  66.7 0.7 slice_bitcast_fusion.2
  67.4 0.7 slice_bitcast_fusion.3
  68.1 0.7 slice_bitcast_fusion.4
  68.8 15.6 %collective-permute-done.4.refs_6_ = f32[2056,128]{1,0:T(8,128)} collective-permute-done((f32[2056,128]{1,0:T(8,128)S(1)}, f32[2056,128]{1,0:T(8,128)}, u32[]{:S(2)}, u32[]{:S(2)}) %collective-permute-start.4) | collective-permute-done | bytes 1052704 | tf_op jit(solution)/shard_map/ppermute | solution.py:203
  84.3 0.7 slice_bitcast_fusion.1
  85.0 2.8 %collective-permute-done.5.refs_7_ = f32[2056,128]{1,0:T(8,128)} collective-permute-done((f32[2056,128]{1,0:T(8,128)}, f32[2056,128]{1,0:T(8,128)}, u32[]{:S(2)}, u32[]{:S(2)}) %collective-permute-start.5) | collective-permute-done | bytes 1052704 | tf_op jit(solution)/shard_map/ppermute | solution.py:203
  87.8 0.7 slice_bitcast_fusion
  88.6 0.5 convert_element_type.28.right_keys
  89.1 6.1 %match_lists.1.refs_0_ = s32[528]{0:T(1024)} custom-call(s32[16]{0:T(128)} %get-tuple-element.45.rows_ref, s32[16]{0:T(128)} %get-tuple-element.46.cols_ref, s32[256]{0:T(256)} %all-reduce.2.left_keys, s32[128]{0:T(128)} %convert_element_type.28.right_keys, s32[32]{0:T(128)} %fusion.14.right_base), custom_call_target="tpu_custom_call" | custom-call | tf_op jit(solution)/shard_map/match_lists/pallas_call | solution.py:45
  95.3 4.5 %split_panel.1.refs_2_ = bf16[128,128,256]{2,1,0:T(8,128)(2,1)S(1)} custom-call(f32[2056,128]{1,0:T(8,128)S(1)} %pad_maximum_fusion.refs_0_, f32[2056,128]{1,0:T(8,128)S(1)} %pad_maximum_fusion.1.refs_1_, f32[2056,128]{1,0:T(8,128)S(1)} %collective-permute-done.refs_2_, f32[2056,128]{1,0:T(8,128)} %collective-permute-done.1.refs_3_, ...), custom_call_target="tpu_custom_call" | custom-call | tf_op jit(solution)/shard_map/split_panel/pallas_call | solution.py:73
  99.8 3.2 %copy-done = bf16[128,128,256]{2,1,0:T(8,128)(2,1)} copy-done((bf16[128,128,256]{2,1,0:T(8,128)(2,1)}, bf16[128,128,256]{2,1,0:T(8,128)(2,1)S(1)}, u32[]{:S(2)}) %copy-start) | copy-done | bytes 8388632
  103.0 15.7 %all-gather.4.cloned.1.call-done = f32[256,1,1,128,128]{4,3,2,1,0:T(8,128)} async-done(((f32[8,1,1,128,128]{4,3,2,1,0:T(8,128)}), f32[256,1,1,128,128]{4,3,2,1,0:T(8,128)}) %all-gather.4.cloned.1.call-update) | async-done | bytes 16777232 | tf_op jit(solution)/shard_map/all_gather | solution.py:218
  118.7 8.3 %passed_blocks.1 = (f32[4,128,128]{2,1,0:T(8,128)S(1)}, bf16[128,128,256]{2,1,0:T(8,128)(2,1)S(1)}) custom-call(s32[528]{0:T(1024)S(1)} %copy-done.1, f32[256,128,128]{2,1,0:T(8,128)} %bitcast.38, bf16[128,128,256]{2,1,0:T(8,128)(2,1)} %copy-done), custom_call_target="tpu_custom_call" | custom-call | flops 1073741824 | bytes 8388608 | tf_op jit(solution)/shard_map/passed_blocks/pallas_call | solution.py:180
  127.0 7.6 %collective-permute-start.7 = (f32[4,128,128]{2,1,0:T(8,128)S(1)}, f32[4,128,128]{2,1,0:T(8,128)S(1)}, u32[]{:S(2)}, u32[]{:S(2)}) collective-permute-start(f32[4,128,128]{2,1,0:T(8,128)S(1)} %get-tuple-element.32), channel_id=1, source_target_pairs={{0,1},{1,0},{2,3},{3,2},{4,7},{5,6},{6,5},{7,4},{8,9},{9,8},{10,11... | collective-permute-start | bytes 786440 | tf_op jit(solution)/shard_map/ppermute | solution.py:249
  134.7 5.7 %partner_blocks.1 = f32[4,128,128]{2,1,0:T(8,128)S(1)} custom-call(s32[528]{0:T(1024)S(1)} %copy-done.1, f32[256,128,128]{2,1,0:T(8,128)} %bitcast.39, bf16[128,128,256]{2,1,0:T(8,128)(2,1)S(1)} %get-tuple-element.31.refs_2_), custom_call_target="tpu_custom_call" | custom-call | flops 1073741824 | bytes 8388608 | tf_op jit(solution)/shard_map/partner_blocks/pallas_call | solution.py:180
  140.4 2.0 collective-permute-start.6
  142.4 4.8 %second_blocks.1 = f32[4,128,128]{2,1,0:T(8,128)S(1)} custom-call(s32[528]{0:T(1024)S(1)} %copy-done.1, f32[256,128,128]{2,1,0:T(8,128)} %bitcast.40, bf16[128,128,256]{2,1,0:T(8,128)(2,1)S(1)} %get-tuple-element.31.refs_2_), custom_call_target="tpu_custom_call" | custom-call | flops 1073741824 | bytes 8388608 | tf_op jit(solution)/shard_map/second_blocks/pallas_call | solution.py:180
  147.2 0.7 collective-permute-done.7
  147.9 6.3 %collective-permute-start.8 = (f32[4,128,128]{2,1,0:T(8,128)S(1)}, f32[4,128,128]{2,1,0:T(8,128)S(1)}, u32[]{:S(2)}, u32[]{:S(2)}) collective-permute-start(f32[4,128,128]{2,1,0:T(8,128)S(1)} %add.92), channel_id=1, source_target_pairs={{0,3},{1,2},{2,1},{3,0},{4,5},{5,4},{6,7},{7,6},{8,11},{9,10},{10,... | collective-permute-start | bytes 786440 | tf_op jit(solution)/shard_map/ppermute | solution.py:249
  154.2 5.6 %own_blocks.1 = f32[4,128,128]{2,1,0:T(8,128)S(1)} custom-call(s32[528]{0:T(1024)S(1)} %copy-done.1, f32[256,128,128]{2,1,0:T(8,128)} %bitcast.41, bf16[128,128,256]{2,1,0:T(8,128)(2,1)S(1)} %get-tuple-element.31.refs_2_), custom_call_target="tpu_custom_call" | custom-call | flops 1073741824 | bytes 8388608 | tf_op jit(solution)/shard_map/own_blocks/pallas_call | solution.py:180
  159.8 6.5 %collective-permute-done.8 = f32[4,128,128]{2,1,0:T(8,128)S(1)} collective-permute-done((f32[4,128,128]{2,1,0:T(8,128)S(1)}, f32[4,128,128]{2,1,0:T(8,128)S(1)}, u32[]{:S(2)}, u32[]{:S(2)}) %collective-permute-start.8) | collective-permute-done | bytes 262176 | tf_op jit(solution)/shard_map/ppermute | solution.py:249
  166.3 0.3 fusion.1
  166.6 15.4 %psum.14 = f32[4,128]{1,0:T(4,128)S(1)} all-reduce(f32[4,128]{1,0:T(4,128)S(1)} %fusion.1), channel_id=1, replica_groups=mesh['row'=4,'col'=32,'layer'=4] {'layer'}, use_global_device_ids=true, to_apply=%region_1.0 | all-reduce | flops 512 | bytes 4096 | tf_op jit(solution)/shard_map/psum | solution.py:277
  182.0 17.7 %psum.15 = f32[4,128]{1,0:T(4,128)S(1)} all-reduce(f32[4,128]{1,0:T(4,128)S(1)} %psum.14), channel_id=1, replica_groups=mesh['row'=4,'col'=32,'layer'=4] {'row'}, use_global_device_ids=true, to_apply=%region_2.0 | all-reduce | flops 512 | bytes 4096 | tf_op jit(solution)/shard_map/psum | solution.py:277
  199.7 0.2 convolution_divide_fusion
  199.9 0.8 multiply_bitcast_fusion
  (30 shorter events, 0.6 us)
Async XLA Ops:
  6.5 112.2 %all-gather.4.cloned.1.call-start = ((), (), s32[]{:S(2)}) async-start(), calls=%async_computation | async-start | bytes 17301504 | tf_op jit(solution)/shard_map/all_gather | solution.py:218
  11.0 29.2 %collective-permute-start = (f32[2056,128]{1,0:T(8,128)S(1)}, f32[2056,128]{1,0:T(8,128)S(1)}, u32[]{:S(2)}, u32[]{:S(2)}) collective-permute-start(f32[2056,128]{1,0:T(8,128)S(1)} %pad_maximum_fusion.refs_0_), channel_id=1, source_target_pairs={{0,128},{128,256},{256,384},{384,0},{1,129},{129,257},{257,385},{3... | collective-permute-start | bytes 3158024 | tf_op jit(solution)/shard_map/ppermute | solution.py:203
  14.6 10.9 %copy-start.5 = (s32[8]{0:T(128)S(1)}, s32[8]{0:T(128)}, u32[]{:S(2)}) copy-start(s32[8]{0:T(128)} %constant.92.clone) | copy-start | bytes 100
  14.6 11.7 %copy-start.2 = (s32[1,1,16]{2,1,0:T(1,128)S(1)}, s32[1,1,16]{2,1,0:T(1,128)}, u32[]{:S(2)}) copy-start(s32[1,1,16]{2,1,0:T(1,128)} %param.15) | copy-start | bytes 196
  14.6 11.7 %copy-start.3 = (s32[1,1,16]{2,1,0:T(1,128)S(1)}, s32[1,1,16]{2,1,0:T(1,128)}, u32[]{:S(2)}) copy-start(s32[1,1,16]{2,1,0:T(1,128)} %param.16) | copy-start | bytes 196
  14.7 34.4 %copy-start.4 = (s32[8,1,1]{0,2,1:T(1,128)S(1)}, s32[8,1,1]{0,2,1:T(1,128)}, u32[]{:S(2)}) copy-start(s32[8,1,1]{0,2,1:T(1,128)} %param.12) | copy-start | bytes 100
  16.0 28.2 %collective-permute-start.3 = (f32[2056,128]{1,0:T(8,128)S(1)}, f32[2056,128]{1,0:T(8,128)}, u32[]{:S(2)}, u32[]{:S(2)}) collective-permute-start(f32[2056,128]{1,0:T(8,128)S(1)} %pad_maximum_fusion.1.refs_1_), channel_id=1, source_target_pairs={{0,384},{128,0},{256,128},{384,256},{1,385},{129,1},{257,129},{385... | collective-permute-start | bytes 3158024 | tf_op jit(solution)/shard_map/ppermute | solution.py:203
  19.7 47.7 %collective-permute-start.2 = (f32[2056,128]{1,0:T(8,128)S(1)}, f32[2056,128]{1,0:T(8,128)}, u32[]{:S(2)}, u32[]{:S(2)}) collective-permute-start(f32[2056,128]{1,0:T(8,128)S(1)} %pad_maximum_fusion.refs_0_), channel_id=1, source_target_pairs={{0,384},{128,0},{256,128},{384,256},{1,385},{129,1},{257,129},{385... | collective-permute-start | bytes 3158024 | tf_op jit(solution)/shard_map/ppermute | solution.py:203
  23.1 45.0 %collective-permute-start.1 = (f32[2056,128]{1,0:T(8,128)S(1)}, f32[2056,128]{1,0:T(8,128)}, u32[]{:S(2)}, u32[]{:S(2)}) collective-permute-start(f32[2056,128]{1,0:T(8,128)S(1)} %pad_maximum_fusion.1.refs_1_), channel_id=1, source_target_pairs={{0,128},{128,256},{256,384},{384,0},{1,129},{129,257},{257,385},{3... | collective-permute-start | bytes 3158024 | tf_op jit(solution)/shard_map/ppermute | solution.py:203
  41.6 42.7 %collective-permute-start.4 = (f32[2056,128]{1,0:T(8,128)S(1)}, f32[2056,128]{1,0:T(8,128)}, u32[]{:S(2)}, u32[]{:S(2)}) collective-permute-start(f32[2056,128]{1,0:T(8,128)S(1)} %collective-permute-done.refs_2_), channel_id=1, source_target_pairs={{0,128},{128,256},{256,384},{384,0},{1,129},{129,257},{257,385},{3... | collective-permute-start | bytes 3158024 | tf_op jit(solution)/shard_map/ppermute | solution.py:203
  44.2 43.7 %collective-permute-start.5 = (f32[2056,128]{1,0:T(8,128)}, f32[2056,128]{1,0:T(8,128)}, u32[]{:S(2)}, u32[]{:S(2)}) collective-permute-start(f32[2056,128]{1,0:T(8,128)} %collective-permute-done.3.refs_5_), channel_id=1, source_target_pairs={{0,384},{128,0},{256,128},{384,256},{1,385},{129,1},{257,129},{385... | collective-permute-start | bytes 3158024 | tf_op jit(solution)/shard_map/ppermute | solution.py:203
  95.3 23.4 %copy-start.1 = (s32[528]{0:T(1024)S(1)}, s32[528]{0:T(1024)}, u32[]{:S(2)}) copy-start(s32[528]{0:T(1024)} %match_lists.1.refs_0_) | copy-start | bytes 6340
  99.8 3.2 %copy-start = (bf16[128,128,256]{2,1,0:T(8,128)(2,1)}, bf16[128,128,256]{2,1,0:T(8,128)(2,1)S(1)}, u32[]{:S(2)}) copy-start(bf16[128,128,256]{2,1,0:T(8,128)(2,1)S(1)} %split_panel.1.refs_2_) | copy-start | bytes 25165828
  127.0 20.8 %collective-permute-start.7 = (f32[4,128,128]{2,1,0:T(8,128)S(1)}, f32[4,128,128]{2,1,0:T(8,128)S(1)}, u32[]{:S(2)}, u32[]{:S(2)}) collective-permute-start(f32[4,128,128]{2,1,0:T(8,128)S(1)} %get-tuple-element.32), channel_id=1, source_target_pairs={{0,1},{1,0},{2,3},{3,2},{4,7},{5,6},{6,5},{7,4},{8,9},{9,8},{10,11... | collective-permute-start | bytes 786440 | tf_op jit(solution)/shard_map/ppermute | solution.py:249
  140.4 19.4 %collective-permute-start.6 = (f32[4,128,128]{2,1,0:T(8,128)S(1)}, f32[4,128,128]{2,1,0:T(8,128)S(1)}, u32[]{:S(2)}, u32[]{:S(2)}) collective-permute-start(f32[4,128,128]{2,1,0:T(8,128)S(1)} %partner_blocks.1), channel_id=1, source_target_pairs={{0,1},{1,0},{2,3},{3,2},{4,7},{5,6},{6,5},{7,4},{8,9},{9,8},{10,11... | collective-permute-start | bytes 786440 | tf_op jit(solution)/shard_map/ppermute | solution.py:249
  147.9 18.4 %collective-permute-start.8 = (f32[4,128,128]{2,1,0:T(8,128)S(1)}, f32[4,128,128]{2,1,0:T(8,128)S(1)}, u32[]{:S(2)}, u32[]{:S(2)}) collective-permute-start(f32[4,128,128]{2,1,0:T(8,128)S(1)} %add.92), channel_id=1, source_target_pairs={{0,3},{1,2},{2,1},{3,0},{4,5},{5,4},{6,7},{7,6},{8,11},{9,10},{10,... | collective-permute-start | bytes 786440 | tf_op jit(solution)/shard_map/ppermute | solution.py:249
Sparse Core Ops, SparseCore 0:
  9.5 109.1 all-gather.3

commit v6 on v5

--- a/solution.py
+++ b/solution.py
@@ -80,12 +80,13 @@
     )(*pieces)
 
 
-def product_kernel(first, outputs, keep, *refs):
-    if keep:
-        (matches, left_ref, panel, out_ref, panel_out, left_buf, left_sem, right_buf, right_sem,
-         panel_sem) = refs
-    else:
-        matches, left_ref, panel, out_ref, left_buf, left_sem = refs
+def product_kernel(first, outputs, fetch, keep, *refs):
+    refs = list(refs)
+    matches, left_ref, panel, out_ref = refs[:4]
+    panel_out, panel_sem = (refs.pop(4), refs.pop()) if keep else (None, None)
+    left_buf, left_sem = refs[4:6]
+    if fetch:
+        right_buf, right_sem = refs[6:]
     size = left_ref.shape[1]
     blocks = panel.shape[0]
     slots = left_buf.shape[1]
@@ -96,7 +97,7 @@
         left = pltpu.make_async_copy(
             left_ref.at[lax.div(match, blocks)], left_buf.at[buf, spot], left_sem.at[buf, spot]
         )
-        if not keep:
+        if not fetch:
             return [left]
         right = pltpu.make_async_copy(
             panel.at[lax.rem(match, blocks)], right_buf.at[buf, spot], right_sem.at[buf, spot]
@@ -123,12 +124,12 @@
 
         def clear(spot, carry):
             left_buf[buf, spot] = zero
-            if keep:
+            if fetch:
                 right_buf[buf, spot] = jnp.zeros((size, 2 * size), jnp.bfloat16)
             return carry
 
         def right_block(spot):
-            if keep:
+            if fetch:
                 return right_buf[buf, spot]
             match = matches[(first + which) * slots + spot]
             return panel[jnp.where(spot < count, lax.rem(match, blocks), 0)]
@@ -160,7 +161,7 @@
         whole.wait()
 
 
-def products(name, first, outputs, keep, matches, slots, left, panel):
+def products(name, first, outputs, fetch, keep, matches, slots, left, panel):
     size = left.shape[1]
     smem = pl.BlockSpec(memory_space=pltpu.SMEM)
     vmem = pl.BlockSpec(memory_space=pltpu.VMEM)
@@ -170,17 +171,18 @@
         pltpu.VMEM((2, slots, size, size), jnp.float32),
         pltpu.SemaphoreType.DMA((2, slots)),
     ]
-    if keep:
-        out_shape.append(jax.ShapeDtypeStruct(panel.shape, panel.dtype))
+    if fetch:
         scratch += [
             pltpu.VMEM((2, slots, size, 2 * size), jnp.bfloat16),
             pltpu.SemaphoreType.DMA((2, slots)),
-            pltpu.SemaphoreType.DMA((1,)),
         ]
+    if keep:
+        out_shape.append(jax.ShapeDtypeStruct(panel.shape, panel.dtype))
+        scratch.append(pltpu.SemaphoreType.DMA((1,)))
     return pl.pallas_call(
-        functools.partial(product_kernel, first, outputs, keep),
+        functools.partial(product_kernel, first, outputs, fetch, keep),
         out_shape=out_shape,
-        in_specs=[smem, hbm, hbm if keep else vmem],
+        in_specs=[smem, hbm, hbm if fetch else vmem],
         out_specs=[vmem] * len(out_shape),
         scratch_shapes=scratch,
         compiler_params=pltpu.CompilerParams(vmem_limit_bytes=VMEM_GRANT),
@@ -256,15 +258,17 @@
     matches = match_lists(rows, cols, left_keys, right_keys, right_base, block_rows)
     panel = split_panel(pieces, half * block_cols, size)
 
-    def blocks(name, number, keep, panel):
+    def blocks(name, number, panel, fetch=False, keep=False):
         slots = right_base.shape[0]
-        return products(name, number * share, share, keep, matches, slots, left, panel)
-
-    first, panel = blocks("passed_blocks", 0, True, panel)
-    passed = trade(first, 0)
-    partner = trade(blocks("partner_blocks", 1, False, panel)[0], 0)
-    second = trade(blocks("second_blocks", 2, False, panel)[0] + passed, 1)
-    mine = blocks("own_blocks", 3, False, panel)[0] + partner + second
+        return products(
+            name, number * share, share, fetch, keep, matches, slots, left, panel
+        )
+
+    passed = trade(blocks("passed_blocks", 0, panel, True)[0], 0)
+    partner, kept = blocks("partner_blocks", 1, panel, True, True)
+    partner = trade(partner, 0)
+    second = trade(blocks("second_blocks", 2, kept)[0] + passed, 1)
+    mine = blocks("own_blocks", 3, kept)[0] + partner + second
 
     squared = mine * mine
     cols_mine = quarter(cols_here, me)
@@ -274,7 +278,8 @@
     local_sums = jnp.einsum(
         "oc,ox->cx", column_hot, jnp.sum(squared, axis=1), precision=lax.Precision.HIGHEST
     )
-    colsum = lax.psum(lax.psum(local_sums, "layer"), "row")
+    row_sums = lax.all_gather(lax.psum(local_sums, "layer"), "row", axis=1, tiled=True)
+    colsum = jnp.sum(row_sums.reshape(block_cols, row_count, lanes), axis=1)
     denom = colsum + 1e-06
     picked_denom = jnp.einsum("oc,cx->ox", column_hot, denom, precision=lax.Precision.HIGHEST)
     scale_rows = float(row_count * block_rows * size)

time: 209 us -> 213 us (1.019)
  the two profiles are of different devices: /device:TPU:32 before, /device:TPU:80 now
where the time goes in v6:
time: 213 us; the launch traced here: 212 us
  waiting for transfers between devices  54 us (25%)
  blocking collectives  52.4 us (25%)
  Pallas kernels  35.3 us (17%)
  starting transfers between devices  34.7 us (16%)
  local copies, waits for them, and re-layouts  15.3 us (7%)
  between operations  14.8 us (7%)
  other arithmetic  4.97 us (2%)
    ppermute x6, waiting for transfers between devices, shift(): lax.ppermute(value, axis, [(i, (i + by) % count) for i in range(count)])  34 us
    psum x1, blocking collectives, local(): lax.psum(local_sums, 'layer')  25.7 us
    pallas_call x4, Pallas kernels, products(): pl.pallas_call(functools.partial(product_kernel, first, outputs, fetch, k...  24.8 us
    ppermute x6, starting transfers between devices, shift(): lax.ppermute(value, axis, [(i, (i + by) % count) for i in range(count)])  19.9 us
    all_gather x1, waiting for transfers between devices, local(): lax.all_gather(a_values.reshape(block_rows, size, lanes), 'col', axis=0,...  14.7 us
    ppermute x3, starting transfers between devices, trade(): return lax.ppermute(value, ('col', 'layer'), pairs)  14.7 us
    all_gather x1, blocking collectives, local(): left_keys = lax.all_gather(left_index, 'col', axis=0, tiled=True)  13.7 us
    all_gather x1, blocking collectives, local(): lax.all_gather(lax.psum(local_sums, 'layer'), 'row', axis=1, tiled=True)  13 us
  transfers between devices with their start and end apart: 10, of which 9 were waited for; matrix products, arithmetic and copies ran while one was open for 6% of the time, Pallas kernels for 13%

profile of v6, /device:TPU:80, one launch (start us, length us, event | category | flops | bytes accessed | tf_op | source)
XLA Modules:
  0.0 212.0 jit_solution(15957659911665199459)
XLA Ops:
  6.5 0.7 all-gather.4.cloned.1.call-update
  7.3 0.8 slice_convert_fusion
  8.3 2.7 %fusion.17 = (f32[1,4,4,128,128]{4,3,2,1,0:T(8,128)}, f32[1,4,4,128,128]{4,3,2,1,0:T(8,128)S(1)}) fusion(f32[1,8,4,128,128]{4,3,2,1,0:T(8,128)} %param.13), kind=kLoop, calls=%fused_computation.45 | loop fusion | bytes 4194304 | tf_op jit(solution)/shard_map/slice | solution.py:222
  11.0 3.4 %collective-permute-start = (f32[2056,128]{1,0:T(8,128)S(1)}, f32[2056,128]{1,0:T(8,128)S(1)}, u32[]{:S(2)}, u32[]{:S(2)}) collective-permute-start(f32[2056,128]{1,0:T(8,128)S(1)} %pad_maximum_fusion.refs_0_), channel_id=1, source_target_pairs={{0,128},{128,256},{256,384},{384,0},{1,129},{129,257},{257,385},{3... | collective-permute-start | bytes 3158024 | tf_op jit(solution)/shard_map/ppermute | solution.py:205
  14.4 0.1 copy.15
  14.7 1.3 pad_maximum_fusion.1.refs_1_
  16.0 3.7 %collective-permute-start.3 = (f32[2056,128]{1,0:T(8,128)S(1)}, f32[2056,128]{1,0:T(8,128)}, u32[]{:S(2)}, u32[]{:S(2)}) collective-permute-start(f32[2056,128]{1,0:T(8,128)S(1)} %pad_maximum_fusion.1.refs_1_), channel_id=1, source_target_pairs={{0,384},{128,0},{256,128},{384,256},{1,385},{129,1},{257,129},{385... | collective-permute-start | bytes 3158024 | tf_op jit(solution)/shard_map/ppermute | solution.py:205
  19.7 3.5 %collective-permute-start.2 = (f32[2056,128]{1,0:T(8,128)S(1)}, f32[2056,128]{1,0:T(8,128)}, u32[]{:S(2)}, u32[]{:S(2)}) collective-permute-start(f32[2056,128]{1,0:T(8,128)S(1)} %pad_maximum_fusion.refs_0_), channel_id=1, source_target_pairs={{0,384},{128,0},{256,128},{384,256},{1,385},{129,1},{257,129},{385... | collective-permute-start | bytes 3158024 | tf_op jit(solution)/shard_map/ppermute | solution.py:205
  23.1 2.4 %collective-permute-start.1 = (f32[2056,128]{1,0:T(8,128)S(1)}, f32[2056,128]{1,0:T(8,128)}, u32[]{:S(2)}, u32[]{:S(2)}) collective-permute-start(f32[2056,128]{1,0:T(8,128)S(1)} %pad_maximum_fusion.1.refs_1_), channel_id=1, source_target_pairs={{0,128},{128,256},{256,384},{384,0},{1,129},{129,257},{257,385},{3... | collective-permute-start | bytes 3158024 | tf_op jit(solution)/shard_map/ppermute | solution.py:205
  25.7 0.5 fusion.14.right_base
  26.4 1.3 dynamic-slice.22
  28.3 0.7 pad_add_fusion
  29.0 11.3 %collective-permute-done.refs_2_ = f32[2056,128]{1,0:T(8,128)S(1)} collective-permute-done((f32[2056,128]{1,0:T(8,128)S(1)}, f32[2056,128]{1,0:T(8,128)S(1)}, u32[]{:S(2)}, u32[]{:S(2)}) %collective-permute-start) | collective-permute-done | bytes 1052704 | tf_op jit(solution)/shard_map/ppermute | solution.py:205
  40.3 0.6 slice.70
  41.4 2.2 %collective-permute-start.4 = (f32[2056,128]{1,0:T(8,128)S(1)}, f32[2056,128]{1,0:T(8,128)}, u32[]{:S(2)}, u32[]{:S(2)}) collective-permute-start(f32[2056,128]{1,0:T(8,128)S(1)} %collective-permute-done.refs_2_), channel_id=1, source_target_pairs={{0,128},{128,256},{256,384},{384,0},{1,129},{129,257},{257,385},{3... | collective-permute-start | bytes 3158024 | tf_op jit(solution)/shard_map/ppermute | solution.py:205
  43.6 0.5 collective-permute-done.3.refs_5_
  44.2 4.9 %collective-permute-start.5 = (f32[2056,128]{1,0:T(8,128)}, f32[2056,128]{1,0:T(8,128)}, u32[]{:S(2)}, u32[]{:S(2)}) collective-permute-start(f32[2056,128]{1,0:T(8,128)} %collective-permute-done.3.refs_5_), channel_id=1, source_target_pairs={{0,384},{128,0},{256,128},{384,256},{1,385},{129,1},{257,129},{385... | collective-permute-start | bytes 3158024 | tf_op jit(solution)/shard_map/ppermute | solution.py:205
  49.0 0.1 bitcast_dynamic-update-slice_fusion
  49.1 13.7 %all-reduce.2.left_keys = s32[256]{0:T(256)} all-reduce(s32[256]{0:T(256)S(1)} %bitcast_dynamic-update-slice_fusion), channel_id=2, replica_groups=mesh['row'=4,'col'=32,'layer'=4] {'col'}, use_global_device_ids=true, to_apply=%add.2 | all-reduce | flops 256 | bytes 2048 | tf_op jit(solution)/shard_map/all_gather | solution.py:230
  62.9 0.7 slice_bitcast_fusion.2
  63.5 3.2 %collective-permute-done.2.refs_4_ = f32[2056,128]{1,0:T(8,128)} collective-permute-done((f32[2056,128]{1,0:T(8,128)S(1)}, f32[2056,128]{1,0:T(8,128)}, u32[]{:S(2)}, u32[]{:S(2)}) %collective-permute-start.2) | collective-permute-done | bytes 1052704 | tf_op jit(solution)/shard_map/ppermute | solution.py:205
  66.7 0.7 slice_bitcast_fusion.3
  67.4 0.7 slice_bitcast_fusion.4
  68.1 16.2 %collective-permute-done.4.refs_6_ = f32[2056,128]{1,0:T(8,128)} collective-permute-done((f32[2056,128]{1,0:T(8,128)S(1)}, f32[2056,128]{1,0:T(8,128)}, u32[]{:S(2)}, u32[]{:S(2)}) %collective-permute-start.4) | collective-permute-done | bytes 1052704 | tf_op jit(solution)/shard_map/ppermute | solution.py:205
  84.3 0.7 slice_bitcast_fusion.1
  85.0 2.8 %collective-permute-done.5.refs_7_ = f32[2056,128]{1,0:T(8,128)} collective-permute-done((f32[2056,128]{1,0:T(8,128)}, f32[2056,128]{1,0:T(8,128)}, u32[]{:S(2)}, u32[]{:S(2)}) %collective-permute-start.5) | collective-permute-done | bytes 1052704 | tf_op jit(solution)/shard_map/ppermute | solution.py:205
  87.8 0.7 slice_bitcast_fusion
  88.6 0.6 convert_element_type.28.right_keys
  89.1 6.1 %match_lists.1.refs_0_ = s32[528]{0:T(1024)} custom-call(s32[16]{0:T(128)} %get-tuple-element.45.rows_ref, s32[16]{0:T(128)} %get-tuple-element.46.cols_ref, s32[256]{0:T(256)} %all-reduce.2.left_keys, s32[128]{0:T(128)} %convert_element_type.28.right_keys, s32[32]{0:T(128)} %fusion.14.right_base), custom_call_target="tpu_custom_call" | custom-call | tf_op jit(solution)/shard_map/match_lists/pallas_call | solution.py:45
  95.3 4.5 %split_panel.1.refs_2_ = bf16[128,128,256]{2,1,0:T(8,128)(2,1)S(1)} custom-call(f32[2056,128]{1,0:T(8,128)S(1)} %pad_maximum_fusion.refs_0_, f32[2056,128]{1,0:T(8,128)S(1)} %pad_maximum_fusion.1.refs_1_, f32[2056,128]{1,0:T(8,128)S(1)} %collective-permute-done.refs_2_, f32[2056,128]{1,0:T(8,128)} %collective-permute-done.1.refs_3_, ...), custom_call_target="tpu_custom_call" | custom-call | tf_op jit(solution)/shard_map/split_panel/pallas_call | solution.py:73
  99.8 3.2 %copy-done = bf16[128,128,256]{2,1,0:T(8,128)(2,1)} copy-done((bf16[128,128,256]{2,1,0:T(8,128)(2,1)}, bf16[128,128,256]{2,1,0:T(8,128)(2,1)S(1)}, u32[]{:S(2)}) %copy-start) | copy-done | bytes 8388632
  103.0 14.7 %all-gather.4.cloned.1.call-done = f32[256,1,1,128,128]{4,3,2,1,0:T(8,128)} async-done(((f32[8,1,1,128,128]{4,3,2,1,0:T(8,128)}), f32[256,1,1,128,128]{4,3,2,1,0:T(8,128)}) %all-gather.4.cloned.1.call-update) | async-done | bytes 16777232 | tf_op jit(solution)/shard_map/all_gather | solution.py:220
  117.7 3.4 %copy-done.1 = bf16[128,128,256]{2,1,0:T(8,128)(2,1)S(1)} copy-done((bf16[128,128,256]{2,1,0:T(8,128)(2,1)S(1)}, bf16[128,128,256]{2,1,0:T(8,128)(2,1)}, u32[]{:S(2)}) %copy-start.1) | copy-done | bytes 8388632
  121.1 6.9 %passed_blocks.1 = f32[4,128,128]{2,1,0:T(8,128)S(1)} custom-call(s32[528]{0:T(1024)S(1)} %copy-done.2, f32[256,128,128]{2,1,0:T(8,128)} %bitcast.38, bf16[128,128,256]{2,1,0:T(8,128)(2,1)S(1)} %copy-done.1), custom_call_target="tpu_custom_call" | custom-call | flops 1073741824 | bytes 8388608 | tf_op jit(solution)/shard_map/passed_blocks/pallas_call | solution.py:182
  128.0 7.8 %collective-permute-start.7 = (f32[4,128,128]{2,1,0:T(8,128)S(1)}, f32[4,128,128]{2,1,0:T(8,128)S(1)}, u32[]{:S(2)}, u32[]{:S(2)}) collective-permute-start(f32[4,128,128]{2,1,0:T(8,128)S(1)} %passed_blocks.1), channel_id=1, source_target_pairs={{0,1},{1,0},{2,3},{3,2},{4,7},{5,6},{6,5},{7,4},{8,9},{9,8},{10,11... | collective-permute-start | bytes 786440 | tf_op jit(solution)/shard_map/ppermute | solution.py:251
  135.9 7.9 %partner_blocks.1 = (f32[4,128,128]{2,1,0:T(8,128)S(1)}, bf16[128,128,256]{2,1,0:T(8,128)(2,1)S(1)}) custom-call(s32[528]{0:T(1024)S(1)} %copy-done.2, f32[256,128,128]{2,1,0:T(8,128)} %bitcast.39, bf16[128,128,256]{2,1,0:T(8,128)(2,1)} %copy-done), custom_call_target="tpu_custom_call" | custom-call | flops 1073741824 | bytes 8388608 | tf_op jit(solution)/shard_map/partner_blocks/pallas_call | solution.py:182
  143.7 2.4 %collective-permute-start.6 = (f32[4,128,128]{2,1,0:T(8,128)S(1)}, f32[4,128,128]{2,1,0:T(8,128)S(1)}, u32[]{:S(2)}, u32[]{:S(2)}) collective-permute-start(f32[4,128,128]{2,1,0:T(8,128)S(1)} %get-tuple-element.32), channel_id=1, source_target_pairs={{0,1},{1,0},{2,3},{3,2},{4,7},{5,6},{6,5},{7,4},{8,9},{9,8},{10,11... | collective-permute-start | bytes 786440 | tf_op jit(solution)/shard_map/ppermute | solution.py:251
  146.1 4.7 %second_blocks.1 = f32[4,128,128]{2,1,0:T(8,128)S(1)} custom-call(s32[528]{0:T(1024)S(1)} %copy-done.2, f32[256,128,128]{2,1,0:T(8,128)} %bitcast.40, bf16[128,128,256]{2,1,0:T(8,128)(2,1)S(1)} %get-tuple-element.31.refs_2_), custom_call_target="tpu_custom_call" | custom-call | flops 1073741824 | bytes 8388608 | tf_op jit(solution)/shard_map/second_blocks/pallas_call | solution.py:182
  150.8 0.7 collective-permute-done.7
  151.5 4.5 %collective-permute-start.8 = (f32[4,128,128]{2,1,0:T(8,128)S(1)}, f32[4,128,128]{2,1,0:T(8,128)S(1)}, u32[]{:S(2)}, u32[]{:S(2)}) collective-permute-start(f32[4,128,128]{2,1,0:T(8,128)S(1)} %add.90), channel_id=1, source_target_pairs={{0,3},{1,2},{2,1},{3,0},{4,5},{5,4},{6,7},{7,6},{8,11},{9,10},{10,... | collective-permute-start | bytes 786440 | tf_op jit(solution)/shard_map/ppermute | solution.py:251
  156.0 5.3 %own_blocks.1 = f32[4,128,128]{2,1,0:T(8,128)S(1)} custom-call(s32[528]{0:T(1024)S(1)} %copy-done.2, f32[256,128,128]{2,1,0:T(8,128)} %bitcast.41, bf16[128,128,256]{2,1,0:T(8,128)(2,1)S(1)} %get-tuple-element.31.refs_2_), custom_call_target="tpu_custom_call" | custom-call | flops 1073741824 | bytes 8388608 | tf_op jit(solution)/shard_map/own_blocks/pallas_call | solution.py:182
  161.3 2.9 %collective-permute-done.6 = f32[4,128,128]{2,1,0:T(8,128)S(1)} collective-permute-done((f32[4,128,128]{2,1,0:T(8,128)S(1)}, f32[4,128,128]{2,1,0:T(8,128)S(1)}, u32[]{:S(2)}, u32[]{:S(2)}) %collective-permute-start.6) | collective-permute-done | bytes 262176 | tf_op jit(solution)/shard_map/ppermute | solution.py:251
  164.2 1.0 collective-permute-done.8
  165.2 0.3 fusion.1
  165.5 25.7 %psum.7 = f32[4,128]{1,0:T(4,128)S(1)} all-reduce(f32[4,128]{1,0:T(4,128)S(1)} %fusion.1), channel_id=1, replica_groups=mesh['row'=4,'col'=32,'layer'=4] {'layer'}, use_global_device_ids=true, to_apply=%region_1.0 | all-reduce | flops 512 | bytes 4096 | tf_op jit(solution)/shard_map/psum | solution.py:281
  191.2 13.0 %all_gather.11 = f32[4,512]{1,0:T(4,128)S(1)} all-gather(f32[4,128]{1,0:T(4,128)S(1)} %psum.7), channel_id=1, replica_groups=mesh['row'=4,'col'=32,'layer'=4] {'row'}, dimensions={1}, use_global_device_ids=true | all-gather | bytes 10240 | tf_op jit(solution)/shard_map/all_gather | solution.py:281
  204.3 0.2 convolution_divide_fusion
  204.4 0.8 multiply_bitcast_fusion
  (34 shorter events, 0.9 us)
Async XLA Ops:
  6.5 111.2 %all-gather.4.cloned.1.call-start = ((), (), s32[]{:S(2)}) async-start(), calls=%async_computation | async-start | bytes 17301504 | tf_op jit(solution)/shard_map/all_gather | solution.py:220
  11.0 29.2 %collective-permute-start = (f32[2056,128]{1,0:T(8,128)S(1)}, f32[2056,128]{1,0:T(8,128)S(1)}, u32[]{:S(2)}, u32[]{:S(2)}) collective-permute-start(f32[2056,128]{1,0:T(8,128)S(1)} %pad_maximum_fusion.refs_0_), channel_id=1, source_target_pairs={{0,128},{128,256},{256,384},{384,0},{1,129},{129,257},{257,385},{3... | collective-permute-start | bytes 3158024 | tf_op jit(solution)/shard_map/ppermute | solution.py:205
  14.6 10.9 %copy-start.6 = (s32[8]{0:T(128)S(1)}, s32[8]{0:T(128)}, u32[]{:S(2)}) copy-start(s32[8]{0:T(128)} %constant.92.clone) | copy-start | bytes 100
  14.6 11.6 %copy-start.3 = (s32[1,1,16]{2,1,0:T(1,128)S(1)}, s32[1,1,16]{2,1,0:T(1,128)}, u32[]{:S(2)}) copy-start(s32[1,1,16]{2,1,0:T(1,128)} %param.15) | copy-start | bytes 196
  14.6 11.7 %copy-start.4 = (s32[1,1,16]{2,1,0:T(1,128)S(1)}, s32[1,1,16]{2,1,0:T(1,128)}, u32[]{:S(2)}) copy-start(s32[1,1,16]{2,1,0:T(1,128)} %param.16) | copy-start | bytes 196
  14.7 34.4 %copy-start.5 = (s32[8,1,1]{0,2,1:T(1,128)S(1)}, s32[8,1,1]{0,2,1:T(1,128)}, u32[]{:S(2)}) copy-start(s32[8,1,1]{0,2,1:T(1,128)} %param.12) | copy-start | bytes 100
  16.0 28.2 %collective-permute-start.3 = (f32[2056,128]{1,0:T(8,128)S(1)}, f32[2056,128]{1,0:T(8,128)}, u32[]{:S(2)}, u32[]{:S(2)}) collective-permute-start(f32[2056,128]{1,0:T(8,128)S(1)} %pad_maximum_fusion.1.refs_1_), channel_id=1, source_target_pairs={{0,384},{128,0},{256,128},{384,256},{1,385},{129,1},{257,129},{385... | collective-permute-start | bytes 3158024 | tf_op jit(solution)/shard_map/ppermute | solution.py:205
  19.7 47.1 %collective-permute-start.2 = (f32[2056,128]{1,0:T(8,128)S(1)}, f32[2056,128]{1,0:T(8,128)}, u32[]{:S(2)}, u32[]{:S(2)}) collective-permute-start(f32[2056,128]{1,0:T(8,128)S(1)} %pad_maximum_fusion.refs_0_), channel_id=1, source_target_pairs={{0,384},{128,0},{256,128},{384,256},{1,385},{129,1},{257,129},{385... | collective-permute-start | bytes 3158024 | tf_op jit(solution)/shard_map/ppermute | solution.py:205
  23.1 44.3 %collective-permute-start.1 = (f32[2056,128]{1,0:T(8,128)S(1)}, f32[2056,128]{1,0:T(8,128)}, u32[]{:S(2)}, u32[]{:S(2)}) collective-permute-start(f32[2056,128]{1,0:T(8,128)S(1)} %pad_maximum_fusion.1.refs_1_), channel_id=1, source_target_pairs={{0,128},{128,256},{256,384},{384,0},{1,129},{129,257},{257,385},{3... | collective-permute-start | bytes 3158024 | tf_op jit(solution)/shard_map/ppermute | solution.py:205
  41.4 42.9 %collective-permute-start.4 = (f32[2056,128]{1,0:T(8,128)S(1)}, f32[2056,128]{1,0:T(8,128)}, u32[]{:S(2)}, u32[]{:S(2)}) collective-permute-start(f32[2056,128]{1,0:T(8,128)S(1)} %collective-permute-done.refs_2_), channel_id=1, source_target_pairs={{0,128},{128,256},{256,384},{384,0},{1,129},{129,257},{257,385},{3... | collective-permute-start | bytes 3158024 | tf_op jit(solution)/shard_map/ppermute | solution.py:205
  44.2 43.7 %collective-permute-start.5 = (f32[2056,128]{1,0:T(8,128)}, f32[2056,128]{1,0:T(8,128)}, u32[]{:S(2)}, u32[]{:S(2)}) collective-permute-start(f32[2056,128]{1,0:T(8,128)} %collective-permute-done.3.refs_5_), channel_id=1, source_target_pairs={{0,384},{128,0},{256,128},{384,256},{1,385},{129,1},{257,129},{385... | collective-permute-start | bytes 3158024 | tf_op jit(solution)/shard_map/ppermute | solution.py:205
  95.3 22.5 %copy-start.2 = (s32[528]{0:T(1024)S(1)}, s32[528]{0:T(1024)}, u32[]{:S(2)}) copy-start(s32[528]{0:T(1024)} %match_lists.1.refs_0_) | copy-start | bytes 6340
  99.7 3.2 %copy-start = (bf16[128,128,256]{2,1,0:T(8,128)(2,1)}, bf16[128,128,256]{2,1,0:T(8,128)(2,1)S(1)}, u32[]{:S(2)}) copy-start(bf16[128,128,256]{2,1,0:T(8,128)(2,1)S(1)} %split_panel.1.refs_2_) | copy-start | bytes 25165828
  117.7 3.4 %copy-start.1 = (bf16[128,128,256]{2,1,0:T(8,128)(2,1)S(1)}, bf16[128,128,256]{2,1,0:T(8,128)(2,1)}, u32[]{:S(2)}) copy-start(bf16[128,128,256]{2,1,0:T(8,128)(2,1)} %copy-done) | copy-start | bytes 25165828
  128.0 23.5 %collective-permute-start.7 = (f32[4,128,128]{2,1,0:T(8,128)S(1)}, f32[4,128,128]{2,1,0:T(8,128)S(1)}, u32[]{:S(2)}, u32[]{:S(2)}) collective-permute-start(f32[4,128,128]{2,1,0:T(8,128)S(1)} %passed_blocks.1), channel_id=1, source_target_pairs={{0,1},{1,0},{2,3},{3,2},{4,7},{5,6},{6,5},{7,4},{8,9},{9,8},{10,11... | collective-permute-start | bytes 786440 | tf_op jit(solution)/shard_map/ppermute | solution.py:251
  143.7 20.5 %collective-permute-start.6 = (f32[4,128,128]{2,1,0:T(8,128)S(1)}, f32[4,128,128]{2,1,0:T(8,128)S(1)}, u32[]{:S(2)}, u32[]{:S(2)}) collective-permute-start(f32[4,128,128]{2,1,0:T(8,128)S(1)} %get-tuple-element.32), channel_id=1, source_target_pairs={{0,1},{1,0},{2,3},{3,2},{4,7},{5,6},{6,5},{7,4},{8,9},{9,8},{10,11... | collective-permute-start | bytes 786440 | tf_op jit(solution)/shard_map/ppermute | solution.py:251
  151.5 13.7 %collective-permute-start.8 = (f32[4,128,128]{2,1,0:T(8,128)S(1)}, f32[4,128,128]{2,1,0:T(8,128)S(1)}, u32[]{:S(2)}, u32[]{:S(2)}) collective-permute-start(f32[4,128,128]{2,1,0:T(8,128)S(1)} %add.90), channel_id=1, source_target_pairs={{0,3},{1,2},{2,1},{3,0},{4,5},{5,4},{6,7},{7,6},{8,11},{9,10},{10,... | collective-permute-start | bytes 786440 | tf_op jit(solution)/shard_map/ppermute | solution.py:251
Sparse Core Ops, SparseCore 0:
  9.5 108.1 all-gather.3

commit v7 on v6

--- a/solution.py
+++ b/solution.py
@@ -10,6 +10,7 @@
 KB_C = 2
 CHUNK = 8
 VMEM_GRANT = 42 * 1024 * 1024
+FULL_GRANT = 52 * 1024 * 1024
 
 
 def halves(value):
@@ -185,7 +186,9 @@
         in_specs=[smem, hbm, hbm if fetch else vmem],
         out_specs=[vmem] * len(out_shape),
         scratch_shapes=scratch,
-        compiler_params=pltpu.CompilerParams(vmem_limit_bytes=VMEM_GRANT),
+        compiler_params=pltpu.CompilerParams(
+            vmem_limit_bytes=FULL_GRANT if fetch and not keep else VMEM_GRANT
+        ),
         cost_estimate=pl.CostEstimate(
             flops=outputs * 16 * 8 * size**3, bytes_accessed=outputs * 16 * 8 * size**2,
             transcendentals=0,
@@ -278,8 +281,7 @@
     local_sums = jnp.einsum(
         "oc,ox->cx", column_hot, jnp.sum(squared, axis=1), precision=lax.Precision.HIGHEST
     )
-    row_sums = lax.all_gather(lax.psum(local_sums, "layer"), "row", axis=1, tiled=True)
-    colsum = jnp.sum(row_sums.reshape(block_cols, row_count, lanes), axis=1)
+    colsum = lax.psum(lax.psum(local_sums, "layer"), "row")
     denom = colsum + 1e-06
     picked_denom = jnp.einsum("oc,cx->ox", column_hot, denom, precision=lax.Precision.HIGHEST)
     scale_rows = float(row_count * block_rows * size)

time: 213 us -> 207 us (0.972)
  the two profiles are of different devices: /device:TPU:80 before, /device:TPU:72 now
where the time goes in v7:
time: 207 us; the launch traced here: 205 us
  waiting for transfers between devices  58.4 us (28%)
  blocking collectives  44.6 us (22%)
  starting transfers between devices  36.3 us (18%)
  Pallas kernels  33.8 us (16%)
  between operations  15 us (7%)
  local copies, waits for them, and re-layouts  12 us (6%)
  other arithmetic  4.93 us (2%)
    ppermute x6, waiting for transfers between devices, shift(): lax.ppermute(value, axis, [(i, (i + by) % count) for i in range(count)])  32.6 us
    psum x2, blocking collectives, local(): colsum = lax.psum(lax.psum(local_sums, 'layer'), 'row')  29.6 us
    pallas_call x4, Pallas kernels, products(): pl.pallas_call(functools.partial(product_kernel, first, outputs, fetch, k...  23.2 us
    ppermute x6, starting transfers between devices, shift(): lax.ppermute(value, axis, [(i, (i + by) % count) for i in range(count)])  19.9 us
    ppermute x3, starting transfers between devices, trade(): return lax.ppermute(value, ('col', 'layer'), pairs)  16.3 us
    all_gather x1, waiting for transfers between devices, local(): lax.all_gather(a_values.reshape(block_rows, size, lanes), 'col', axis=0,...  15.1 us
    all_gather x1, blocking collectives, local(): left_keys = lax.all_gather(left_index, 'col', axis=0, tiled=True)  15 us
    ppermute x3, waiting for transfers between devices, trade(): return lax.ppermute(value, ('col', 'layer'), pairs)  10 us
  transfers between devices with their start and end apart: 10, of which 8 were waited for; matrix products, arithmetic and copies ran while one was open for 6% of the time, Pallas kernels for 13%

profile of v7, /device:TPU:72, one launch (start us, length us, event | category | flops | bytes accessed | tf_op | source)
XLA Modules:
  0.0 205.3 jit_solution(9705599550525719515)
XLA Ops:
  6.5 0.7 all-gather.4.cloned.1.call-update
  7.3 0.8 slice_convert_fusion
  8.1 0.1 copy.14
  8.2 0.1 convert_element_type.23
  8.3 2.7 %fusion.17 = (f32[1,4,4,128,128]{4,3,2,1,0:T(8,128)}, f32[1,4,4,128,128]{4,3,2,1,0:T(8,128)S(1)}) fusion(f32[1,8,4,128,128]{4,3,2,1,0:T(8,128)} %param.13), kind=kLoop, calls=%fused_computation.45 | loop fusion | bytes 4194304 | tf_op jit(solution)/shard_map/slice | solution.py:225
  11.0 3.4 %collective-permute-start = (f32[2056,128]{1,0:T(8,128)S(1)}, f32[2056,128]{1,0:T(8,128)S(1)}, u32[]{:S(2)}, u32[]{:S(2)}) collective-permute-start(f32[2056,128]{1,0:T(8,128)S(1)} %pad_maximum_fusion.refs_0_), channel_id=1, source_target_pairs={{0,128},{128,256},{256,384},{384,0},{1,129},{129,257},{257,385},{3... | collective-permute-start | bytes 3158024 | tf_op jit(solution)/shard_map/ppermute | solution.py:208
  14.4 0.1 copy.15
  14.7 1.3 pad_maximum_fusion.1.refs_1_
  16.0 3.7 %collective-permute-start.3 = (f32[2056,128]{1,0:T(8,128)S(1)}, f32[2056,128]{1,0:T(8,128)}, u32[]{:S(2)}, u32[]{:S(2)}) collective-permute-start(f32[2056,128]{1,0:T(8,128)S(1)} %pad_maximum_fusion.1.refs_1_), channel_id=1, source_target_pairs={{0,384},{128,0},{256,128},{384,256},{1,385},{129,1},{257,129},{385... | collective-permute-start | bytes 3158024 | tf_op jit(solution)/shard_map/ppermute | solution.py:208
  19.7 3.5 %collective-permute-start.2 = (f32[2056,128]{1,0:T(8,128)S(1)}, f32[2056,128]{1,0:T(8,128)}, u32[]{:S(2)}, u32[]{:S(2)}) collective-permute-start(f32[2056,128]{1,0:T(8,128)S(1)} %pad_maximum_fusion.refs_0_), channel_id=1, source_target_pairs={{0,384},{128,0},{256,128},{384,256},{1,385},{129,1},{257,129},{385... | collective-permute-start | bytes 3158024 | tf_op jit(solution)/shard_map/ppermute | solution.py:208
  23.1 2.4 %collective-permute-start.1 = (f32[2056,128]{1,0:T(8,128)S(1)}, f32[2056,128]{1,0:T(8,128)}, u32[]{:S(2)}, u32[]{:S(2)}) collective-permute-start(f32[2056,128]{1,0:T(8,128)S(1)} %pad_maximum_fusion.1.refs_1_), channel_id=1, source_target_pairs={{0,128},{128,256},{256,384},{384,0},{1,129},{129,257},{257,385},{3... | collective-permute-start | bytes 3158024 | tf_op jit(solution)/shard_map/ppermute | solution.py:208
  25.7 0.6 fusion.14.right_base
  26.5 1.3 dynamic-slice.22
  28.4 0.6 pad_add_fusion
  29.0 11.3 %collective-permute-done.refs_2_ = f32[2056,128]{1,0:T(8,128)S(1)} collective-permute-done((f32[2056,128]{1,0:T(8,128)S(1)}, f32[2056,128]{1,0:T(8,128)S(1)}, u32[]{:S(2)}, u32[]{:S(2)}) %collective-permute-start) | collective-permute-done | bytes 1052704 | tf_op jit(solution)/shard_map/ppermute | solution.py:208
  40.3 0.7 slice.70
  41.6 2.2 %collective-permute-start.4 = (f32[2056,128]{1,0:T(8,128)S(1)}, f32[2056,128]{1,0:T(8,128)}, u32[]{:S(2)}, u32[]{:S(2)}) collective-permute-start(f32[2056,128]{1,0:T(8,128)S(1)} %collective-permute-done.refs_2_), channel_id=1, source_target_pairs={{0,128},{128,256},{256,384},{384,0},{1,129},{129,257},{257,385},{3... | collective-permute-start | bytes 3158024 | tf_op jit(solution)/shard_map/ppermute | solution.py:208
  43.8 0.3 collective-permute-done.3.refs_5_
  44.2 4.9 %collective-permute-start.5 = (f32[2056,128]{1,0:T(8,128)}, f32[2056,128]{1,0:T(8,128)}, u32[]{:S(2)}, u32[]{:S(2)}) collective-permute-start(f32[2056,128]{1,0:T(8,128)} %collective-permute-done.3.refs_5_), channel_id=1, source_target_pairs={{0,384},{128,0},{256,128},{384,256},{1,385},{129,1},{257,129},{385... | collective-permute-start | bytes 3158024 | tf_op jit(solution)/shard_map/ppermute | solution.py:208
  49.0 0.1 bitcast_dynamic-update-slice_fusion
  49.2 15.0 %all-reduce.2.left_keys = s32[256]{0:T(256)} all-reduce(s32[256]{0:T(256)S(1)} %bitcast_dynamic-update-slice_fusion), channel_id=2, replica_groups=mesh['row'=4,'col'=32,'layer'=4] {'col'}, use_global_device_ids=true, to_apply=%add.2 | all-reduce | flops 256 | bytes 2048 | tf_op jit(solution)/shard_map/all_gather | solution.py:233
  64.1 0.7 slice_bitcast_fusion.2
  64.8 1.9 collective-permute-done.2.refs_4_
  66.7 0.7 slice_bitcast_fusion.3
  67.4 0.7 slice_bitcast_fusion.4
  68.1 16.2 %collective-permute-done.4.refs_6_ = f32[2056,128]{1,0:T(8,128)} collective-permute-done((f32[2056,128]{1,0:T(8,128)S(1)}, f32[2056,128]{1,0:T(8,128)}, u32[]{:S(2)}, u32[]{:S(2)}) %collective-permute-start.4) | collective-permute-done | bytes 1052704 | tf_op jit(solution)/shard_map/ppermute | solution.py:208
  84.3 0.7 slice_bitcast_fusion.1
  85.0 2.8 %collective-permute-done.5.refs_7_ = f32[2056,128]{1,0:T(8,128)} collective-permute-done((f32[2056,128]{1,0:T(8,128)}, f32[2056,128]{1,0:T(8,128)}, u32[]{:S(2)}, u32[]{:S(2)}) %collective-permute-start.5) | collective-permute-done | bytes 1052704 | tf_op jit(solution)/shard_map/ppermute | solution.py:208
  87.8 0.7 slice_bitcast_fusion
  88.6 0.5 convert_element_type.28.right_keys
  89.1 6.1 %match_lists.1.refs_0_ = s32[528]{0:T(1024)} custom-call(s32[16]{0:T(128)} %get-tuple-element.45.rows_ref, s32[16]{0:T(128)} %get-tuple-element.46.cols_ref, s32[256]{0:T(256)} %all-reduce.2.left_keys, s32[128]{0:T(128)} %convert_element_type.28.right_keys, s32[32]{0:T(128)} %fusion.14.right_base), custom_call_target="tpu_custom_call" | custom-call | tf_op jit(solution)/shard_map/match_lists/pallas_call | solution.py:46
  95.3 4.5 %split_panel.1.refs_2_ = bf16[128,128,256]{2,1,0:T(8,128)(2,1)S(1)} custom-call(f32[2056,128]{1,0:T(8,128)S(1)} %pad_maximum_fusion.refs_0_, f32[2056,128]{1,0:T(8,128)S(1)} %pad_maximum_fusion.1.refs_1_, f32[2056,128]{1,0:T(8,128)S(1)} %collective-permute-done.refs_2_, f32[2056,128]{1,0:T(8,128)} %collective-permute-done.1.refs_3_, ...), custom_call_target="tpu_custom_call" | custom-call | tf_op jit(solution)/shard_map/split_panel/pallas_call | solution.py:74
  99.8 3.2 %copy-done = bf16[128,128,256]{2,1,0:T(8,128)(2,1)} copy-done((bf16[128,128,256]{2,1,0:T(8,128)(2,1)}, bf16[128,128,256]{2,1,0:T(8,128)(2,1)S(1)}, u32[]{:S(2)}) %copy-start) | copy-done | bytes 8388632
  103.0 15.1 %all-gather.4.cloned.1.call-done = f32[256,1,1,128,128]{4,3,2,1,0:T(8,128)} async-done(((f32[8,1,1,128,128]{4,3,2,1,0:T(8,128)}), f32[256,1,1,128,128]{4,3,2,1,0:T(8,128)}) %all-gather.4.cloned.1.call-update) | async-done | bytes 16777232 | tf_op jit(solution)/shard_map/all_gather | solution.py:223
  118.0 6.1 %passed_blocks.1 = f32[4,128,128]{2,1,0:T(8,128)S(1)} custom-call(s32[528]{0:T(1024)S(1)} %copy-done.1, f32[256,128,128]{2,1,0:T(8,128)} %bitcast.38, bf16[128,128,256]{2,1,0:T(8,128)(2,1)} %copy-done), custom_call_target="tpu_custom_call" | custom-call | flops 1073741824 | bytes 8388608 | tf_op jit(solution)/shard_map/passed_blocks/pallas_call | solution.py:183
  124.1 7.8 %collective-permute-start.7 = (f32[4,128,128]{2,1,0:T(8,128)S(1)}, f32[4,128,128]{2,1,0:T(8,128)S(1)}, u32[]{:S(2)}, u32[]{:S(2)}) collective-permute-start(f32[4,128,128]{2,1,0:T(8,128)S(1)} %passed_blocks.1), channel_id=1, source_target_pairs={{0,1},{1,0},{2,3},{3,2},{4,7},{5,6},{6,5},{7,4},{8,9},{9,8},{10,11... | collective-permute-start | bytes 786440 | tf_op jit(solution)/shard_map/ppermute | solution.py:254
  131.9 7.8 %partner_blocks.1 = (f32[4,128,128]{2,1,0:T(8,128)S(1)}, bf16[128,128,256]{2,1,0:T(8,128)(2,1)S(1)}) custom-call(s32[528]{0:T(1024)S(1)} %copy-done.1, f32[256,128,128]{2,1,0:T(8,128)} %bitcast.39, bf16[128,128,256]{2,1,0:T(8,128)(2,1)} %copy-done), custom_call_target="tpu_custom_call" | custom-call | flops 1073741824 | bytes 8388608 | tf_op jit(solution)/shard_map/partner_blocks/pallas_call | solution.py:183
  139.7 2.3 %collective-permute-start.6 = (f32[4,128,128]{2,1,0:T(8,128)S(1)}, f32[4,128,128]{2,1,0:T(8,128)S(1)}, u32[]{:S(2)}, u32[]{:S(2)}) collective-permute-start(f32[4,128,128]{2,1,0:T(8,128)S(1)} %get-tuple-element.32), channel_id=1, source_target_pairs={{0,1},{1,0},{2,3},{3,2},{4,7},{5,6},{6,5},{7,4},{8,9},{9,8},{10,11... | collective-permute-start | bytes 786440 | tf_op jit(solution)/shard_map/ppermute | solution.py:254
  142.0 4.2 %second_blocks.1 = f32[4,128,128]{2,1,0:T(8,128)S(1)} custom-call(s32[528]{0:T(1024)S(1)} %copy-done.1, f32[256,128,128]{2,1,0:T(8,128)} %bitcast.40, bf16[128,128,256]{2,1,0:T(8,128)(2,1)S(1)} %get-tuple-element.31.refs_2_), custom_call_target="tpu_custom_call" | custom-call | flops 1073741824 | bytes 8388608 | tf_op jit(solution)/shard_map/second_blocks/pallas_call | solution.py:183
  146.2 6.3 %collective-permute-start.8 = (f32[4,128,128]{2,1,0:T(8,128)S(1)}, f32[4,128,128]{2,1,0:T(8,128)S(1)}, u32[]{:S(2)}, u32[]{:S(2)}) collective-permute-start(f32[4,128,128]{2,1,0:T(8,128)S(1)} %add.92), channel_id=1, source_target_pairs={{0,3},{1,2},{2,1},{3,0},{4,5},{5,4},{6,7},{7,6},{8,11},{9,10},{10,... | collective-permute-start | bytes 786440 | tf_op jit(solution)/shard_map/ppermute | solution.py:254
  152.5 5.1 %own_blocks.1 = f32[4,128,128]{2,1,0:T(8,128)S(1)} custom-call(s32[528]{0:T(1024)S(1)} %copy-done.1, f32[256,128,128]{2,1,0:T(8,128)} %bitcast.41, bf16[128,128,256]{2,1,0:T(8,128)(2,1)S(1)} %get-tuple-element.31.refs_2_), custom_call_target="tpu_custom_call" | custom-call | flops 1073741824 | bytes 8388608 | tf_op jit(solution)/shard_map/own_blocks/pallas_call | solution.py:183
  157.6 8.0 %collective-permute-done.6 = f32[4,128,128]{2,1,0:T(8,128)S(1)} collective-permute-done((f32[4,128,128]{2,1,0:T(8,128)S(1)}, f32[4,128,128]{2,1,0:T(8,128)S(1)}, u32[]{:S(2)}, u32[]{:S(2)}) %collective-permute-start.6) | collective-permute-done | bytes 262176 | tf_op jit(solution)/shard_map/ppermute | solution.py:254
  165.6 2.0 collective-permute-done.8
  167.7 0.3 fusion.1
  168.0 17.1 %psum.14 = f32[4,128]{1,0:T(4,128)S(1)} all-reduce(f32[4,128]{1,0:T(4,128)S(1)} %fusion.1), channel_id=1, replica_groups=mesh['row'=4,'col'=32,'layer'=4] {'layer'}, use_global_device_ids=true, to_apply=%region_1.0 | all-reduce | flops 512 | bytes 4096 | tf_op jit(solution)/shard_map/psum | solution.py:284
  185.0 12.5 %psum.15 = f32[4,128]{1,0:T(4,128)S(1)} all-reduce(f32[4,128]{1,0:T(4,128)S(1)} %psum.14), channel_id=1, replica_groups=mesh['row'=4,'col'=32,'layer'=4] {'row'}, use_global_device_ids=true, to_apply=%region_2.0 | all-reduce | flops 512 | bytes 4096 | tf_op jit(solution)/shard_map/psum | solution.py:284
  197.5 0.2 convolution_divide_fusion
  197.7 0.8 multiply_bitcast_fusion
  (30 shorter events, 0.7 us)
Async XLA Ops:
  6.5 111.5 %all-gather.4.cloned.1.call-start = ((), (), s32[]{:S(2)}) async-start(), calls=%async_computation | async-start | bytes 17301504 | tf_op jit(solution)/shard_map/all_gather | solution.py:223
  11.0 29.2 %collective-permute-start = (f32[2056,128]{1,0:T(8,128)S(1)}, f32[2056,128]{1,0:T(8,128)S(1)}, u32[]{:S(2)}, u32[]{:S(2)}) collective-permute-start(f32[2056,128]{1,0:T(8,128)S(1)} %pad_maximum_fusion.refs_0_), channel_id=1, source_target_pairs={{0,128},{128,256},{256,384},{384,0},{1,129},{129,257},{257,385},{3... | collective-permute-start | bytes 3158024 | tf_op jit(solution)/shard_map/ppermute | solution.py:208
  14.6 10.9 %copy-start.5 = (s32[8]{0:T(128)S(1)}, s32[8]{0:T(128)}, u32[]{:S(2)}) copy-start(s32[8]{0:T(128)} %constant.92.clone) | copy-start | bytes 100
  14.6 11.7 %copy-start.2 = (s32[1,1,16]{2,1,0:T(1,128)S(1)}, s32[1,1,16]{2,1,0:T(1,128)}, u32[]{:S(2)}) copy-start(s32[1,1,16]{2,1,0:T(1,128)} %param.15) | copy-start | bytes 196
  14.6 11.7 %copy-start.3 = (s32[1,1,16]{2,1,0:T(1,128)S(1)}, s32[1,1,16]{2,1,0:T(1,128)}, u32[]{:S(2)}) copy-start(s32[1,1,16]{2,1,0:T(1,128)} %param.16) | copy-start | bytes 196
  14.7 34.4 %copy-start.4 = (s32[8,1,1]{0,2,1:T(1,128)S(1)}, s32[8,1,1]{0,2,1:T(1,128)}, u32[]{:S(2)}) copy-start(s32[8,1,1]{0,2,1:T(1,128)} %param.12) | copy-start | bytes 100
  16.0 28.2 %collective-permute-start.3 = (f32[2056,128]{1,0:T(8,128)S(1)}, f32[2056,128]{1,0:T(8,128)}, u32[]{:S(2)}, u32[]{:S(2)}) collective-permute-start(f32[2056,128]{1,0:T(8,128)S(1)} %pad_maximum_fusion.1.refs_1_), channel_id=1, source_target_pairs={{0,384},{128,0},{256,128},{384,256},{1,385},{129,1},{257,129},{385... | collective-permute-start | bytes 3158024 | tf_op jit(solution)/shard_map/ppermute | solution.py:208
  19.7 47.1 %collective-permute-start.2 = (f32[2056,128]{1,0:T(8,128)S(1)}, f32[2056,128]{1,0:T(8,128)}, u32[]{:S(2)}, u32[]{:S(2)}) collective-permute-start(f32[2056,128]{1,0:T(8,128)S(1)} %pad_maximum_fusion.refs_0_), channel_id=1, source_target_pairs={{0,384},{128,0},{256,128},{384,256},{1,385},{129,1},{257,129},{385... | collective-permute-start | bytes 3158024 | tf_op jit(solution)/shard_map/ppermute | solution.py:208
  23.1 44.3 %collective-permute-start.1 = (f32[2056,128]{1,0:T(8,128)S(1)}, f32[2056,128]{1,0:T(8,128)}, u32[]{:S(2)}, u32[]{:S(2)}) collective-permute-start(f32[2056,128]{1,0:T(8,128)S(1)} %pad_maximum_fusion.1.refs_1_), channel_id=1, source_target_pairs={{0,128},{128,256},{256,384},{384,0},{1,129},{129,257},{257,385},{3... | collective-permute-start | bytes 3158024 | tf_op jit(solution)/shard_map/ppermute | solution.py:208
  41.6 42.7 %collective-permute-start.4 = (f32[2056,128]{1,0:T(8,128)S(1)}, f32[2056,128]{1,0:T(8,128)}, u32[]{:S(2)}, u32[]{:S(2)}) collective-permute-start(f32[2056,128]{1,0:T(8,128)S(1)} %collective-permute-done.refs_2_), channel_id=1, source_target_pairs={{0,128},{128,256},{256,384},{384,0},{1,129},{129,257},{257,385},{3... | collective-permute-start | bytes 3158024 | tf_op jit(solution)/shard_map/ppermute | solution.py:208
  44.2 43.7 %collective-permute-start.5 = (f32[2056,128]{1,0:T(8,128)}, f32[2056,128]{1,0:T(8,128)}, u32[]{:S(2)}, u32[]{:S(2)}) collective-permute-start(f32[2056,128]{1,0:T(8,128)} %collective-permute-done.3.refs_5_), channel_id=1, source_target_pairs={{0,384},{128,0},{256,128},{384,256},{1,385},{129,1},{257,129},{385... | collective-permute-start | bytes 3158024 | tf_op jit(solution)/shard_map/ppermute | solution.py:208
  95.3 22.8 %copy-start.1 = (s32[528]{0:T(1024)S(1)}, s32[528]{0:T(1024)}, u32[]{:S(2)}) copy-start(s32[528]{0:T(1024)} %match_lists.1.refs_0_) | copy-start | bytes 6340
  99.7 3.2 %copy-start = (bf16[128,128,256]{2,1,0:T(8,128)(2,1)}, bf16[128,128,256]{2,1,0:T(8,128)(2,1)S(1)}, u32[]{:S(2)}) copy-start(bf16[128,128,256]{2,1,0:T(8,128)(2,1)S(1)} %split_panel.1.refs_2_) | copy-start | bytes 25165828
  124.1 22.0 %collective-permute-start.7 = (f32[4,128,128]{2,1,0:T(8,128)S(1)}, f32[4,128,128]{2,1,0:T(8,128)S(1)}, u32[]{:S(2)}, u32[]{:S(2)}) collective-permute-start(f32[4,128,128]{2,1,0:T(8,128)S(1)} %passed_blocks.1), channel_id=1, source_target_pairs={{0,1},{1,0},{2,3},{3,2},{4,7},{5,6},{6,5},{7,4},{8,9},{9,8},{10,11... | collective-permute-start | bytes 786440 | tf_op jit(solution)/shard_map/ppermute | solution.py:254
  139.7 25.9 %collective-permute-start.6 = (f32[4,128,128]{2,1,0:T(8,128)S(1)}, f32[4,128,128]{2,1,0:T(8,128)S(1)}, u32[]{:S(2)}, u32[]{:S(2)}) collective-permute-start(f32[4,128,128]{2,1,0:T(8,128)S(1)} %get-tuple-element.32), channel_id=1, source_target_pairs={{0,1},{1,0},{2,3},{3,2},{4,7},{5,6},{6,5},{7,4},{8,9},{9,8},{10,11... | collective-permute-start | bytes 786440 | tf_op jit(solution)/shard_map/ppermute | solution.py:254
  146.2 21.4 %collective-permute-start.8 = (f32[4,128,128]{2,1,0:T(8,128)S(1)}, f32[4,128,128]{2,1,0:T(8,128)S(1)}, u32[]{:S(2)}, u32[]{:S(2)}) collective-permute-start(f32[4,128,128]{2,1,0:T(8,128)S(1)} %add.92), channel_id=1, source_target_pairs={{0,3},{1,2},{2,1},{3,0},{4,5},{5,4},{6,7},{7,6},{8,11},{9,10},{10,... | collective-permute-start | bytes 786440 | tf_op jit(solution)/shard_map/ppermute | solution.py:254
Sparse Core Ops, SparseCore 0:
  9.5 108.4 all-gather.3

commit v8 on v4

--- a/solution.py
+++ b/solution.py
@@ -248,7 +248,9 @@
     local_sums = jnp.einsum(
         "oc,ox->cx", column_hot, jnp.sum(squared, axis=1), precision=lax.Precision.HIGHEST
     )
-    colsum = lax.psum(lax.psum(local_sums, "layer"), "row")
+    local_sums = local_sums + trade(local_sums, 0)
+    local_sums = local_sums + trade(local_sums, 1)
+    colsum = lax.psum(local_sums, "row")
     denom = colsum + 1e-06
     picked_denom = jnp.einsum("oc,cx->ox", column_hot, denom, precision=lax.Precision.HIGHEST)
     scale_rows = float(row_count * block_rows * size)

time: 207 us -> 209 us (level)
  the two profiles are of different devices: /device:TPU:32 before, /device:TPU:8 now
where the time goes in v8:
time: 209 us; the launch traced here: 207 us
  waiting for transfers between devices  59.3 us (28%)
  starting transfers between devices  53.6 us (26%)
  Pallas kernels  34.9 us (17%)
  blocking collectives  26.8 us (13%)
  between operations  15 us (7%)
  local copies, waits for them, and re-layouts  12 us (6%)
  other arithmetic  4.93 us (2%)
    ppermute x5, starting transfers between devices, trade(): return lax.ppermute(value, ('col', 'layer'), pairs)  33.6 us
    ppermute x6, waiting for transfers between devices, shift(): lax.ppermute(value, axis, [(i, (i + by) % count) for i in range(count)])  30.4 us
    pallas_call x4, Pallas kernels, products(): pl.pallas_call(functools.partial(product_kernel, first, outputs), out_sha...  24.3 us
    ppermute x6, starting transfers between devices, shift(): lax.ppermute(value, axis, [(i, (i + by) % count) for i in range(count)])  19.9 us
    all_gather x1, blocking collectives, local(): left_keys = lax.all_gather(left_index, 'col', axis=0, tiled=True)  17.1 us
    all_gather x1, waiting for transfers between devices, local(): lax.all_gather(a_values.reshape(block_rows, size, lanes), 'col', axis=0,...  15.8 us
    ppermute x5, waiting for transfers between devices, trade(): return lax.ppermute(value, ('col', 'layer'), pairs)  12.4 us
    psum x1, blocking collectives, local(): colsum = lax.psum(local_sums, 'row')  9.64 us
  transfers between devices with their start and end apart: 12, of which 8 were waited for; matrix products, arithmetic and copies ran while one was open for 6% of the time, Pallas kernels for 14%

profile of v8, /device:TPU:8, one launch (start us, length us, event | category | flops | bytes accessed | tf_op | source)
XLA Modules:
  0.0 206.9 jit_solution(1244206701021724763)
XLA Ops:
  6.5 0.7 all-gather.4.cloned.1.call-update
  7.3 0.8 slice_convert_fusion
  8.1 0.1 copy.14
  8.3 2.7 %fusion.17 = (f32[1,4,4,128,128]{4,3,2,1,0:T(8,128)}, f32[1,4,4,128,128]{4,3,2,1,0:T(8,128)S(1)}) fusion(f32[1,8,4,128,128]{4,3,2,1,0:T(8,128)} %param.13), kind=kLoop, calls=%fused_computation.45 | loop fusion | bytes 4194304 | tf_op jit(solution)/shard_map/slice | solution.py:195
  11.0 3.4 %collective-permute-start = (f32[2056,128]{1,0:T(8,128)S(1)}, f32[2056,128]{1,0:T(8,128)S(1)}, u32[]{:S(2)}, u32[]{:S(2)}) collective-permute-start(f32[2056,128]{1,0:T(8,128)S(1)} %pad_maximum_fusion.refs_0_), channel_id=1, source_target_pairs={{0,128},{128,256},{256,384},{384,0},{1,129},{129,257},{257,385},{3... | collective-permute-start | bytes 3158024 | tf_op jit(solution)/shard_map/ppermute | solution.py:178
  14.4 0.1 copy.15
  14.7 1.3 pad_maximum_fusion.1.refs_1_
  16.0 3.7 %collective-permute-start.3 = (f32[2056,128]{1,0:T(8,128)S(1)}, f32[2056,128]{1,0:T(8,128)}, u32[]{:S(2)}, u32[]{:S(2)}) collective-permute-start(f32[2056,128]{1,0:T(8,128)S(1)} %pad_maximum_fusion.1.refs_1_), channel_id=1, source_target_pairs={{0,384},{128,0},{256,128},{384,256},{1,385},{129,1},{257,129},{385... | collective-permute-start | bytes 3158024 | tf_op jit(solution)/shard_map/ppermute | solution.py:178
  19.7 3.5 %collective-permute-start.2 = (f32[2056,128]{1,0:T(8,128)S(1)}, f32[2056,128]{1,0:T(8,128)}, u32[]{:S(2)}, u32[]{:S(2)}) collective-permute-start(f32[2056,128]{1,0:T(8,128)S(1)} %pad_maximum_fusion.refs_0_), channel_id=1, source_target_pairs={{0,384},{128,0},{256,128},{384,256},{1,385},{129,1},{257,129},{385... | collective-permute-start | bytes 3158024 | tf_op jit(solution)/shard_map/ppermute | solution.py:178
  23.1 2.4 %collective-permute-start.1 = (f32[2056,128]{1,0:T(8,128)S(1)}, f32[2056,128]{1,0:T(8,128)}, u32[]{:S(2)}, u32[]{:S(2)}) collective-permute-start(f32[2056,128]{1,0:T(8,128)S(1)} %pad_maximum_fusion.1.refs_1_), channel_id=1, source_target_pairs={{0,128},{128,256},{256,384},{384,0},{1,129},{129,257},{257,385},{3... | collective-permute-start | bytes 3158024 | tf_op jit(solution)/shard_map/ppermute | solution.py:178
  25.7 0.6 fusion.14.right_base
  26.5 1.3 dynamic-slice.22
  28.4 0.6 pad_add_fusion
  29.0 11.3 %collective-permute-done.refs_2_ = f32[2056,128]{1,0:T(8,128)S(1)} collective-permute-done((f32[2056,128]{1,0:T(8,128)S(1)}, f32[2056,128]{1,0:T(8,128)S(1)}, u32[]{:S(2)}, u32[]{:S(2)}) %collective-permute-start) | collective-permute-done | bytes 1052704 | tf_op jit(solution)/shard_map/ppermute | solution.py:178
  40.3 0.7 slice.70
  41.6 2.2 %collective-permute-start.4 = (f32[2056,128]{1,0:T(8,128)S(1)}, f32[2056,128]{1,0:T(8,128)}, u32[]{:S(2)}, u32[]{:S(2)}) collective-permute-start(f32[2056,128]{1,0:T(8,128)S(1)} %collective-permute-done.refs_2_), channel_id=1, source_target_pairs={{0,128},{128,256},{256,384},{384,0},{1,129},{129,257},{257,385},{3... | collective-permute-start | bytes 3158024 | tf_op jit(solution)/shard_map/ppermute | solution.py:178
  43.8 0.3 collective-permute-done.3.refs_5_
  44.2 4.9 %collective-permute-start.5 = (f32[2056,128]{1,0:T(8,128)}, f32[2056,128]{1,0:T(8,128)}, u32[]{:S(2)}, u32[]{:S(2)}) collective-permute-start(f32[2056,128]{1,0:T(8,128)} %collective-permute-done.3.refs_5_), channel_id=1, source_target_pairs={{0,384},{128,0},{256,128},{384,256},{1,385},{129,1},{257,129},{385... | collective-permute-start | bytes 3158024 | tf_op jit(solution)/shard_map/ppermute | solution.py:178
  49.0 0.1 bitcast_dynamic-update-slice_fusion
  49.1 17.1 %all-reduce.2.left_keys = s32[256]{0:T(256)} all-reduce(s32[256]{0:T(256)S(1)} %bitcast_dynamic-update-slice_fusion), channel_id=2, replica_groups=mesh['row'=4,'col'=32,'layer'=4] {'col'}, use_global_device_ids=true, to_apply=%add.2 | all-reduce | flops 256 | bytes 2048 | tf_op jit(solution)/shard_map/all_gather | solution.py:203
  66.3 0.7 slice_bitcast_fusion.2
  67.0 0.7 slice_bitcast_fusion.3
  67.7 0.7 slice_bitcast_fusion.4
  68.3 16.0 %collective-permute-done.4.refs_6_ = f32[2056,128]{1,0:T(8,128)} collective-permute-done((f32[2056,128]{1,0:T(8,128)S(1)}, f32[2056,128]{1,0:T(8,128)}, u32[]{:S(2)}, u32[]{:S(2)}) %collective-permute-start.4) | collective-permute-done | bytes 1052704 | tf_op jit(solution)/shard_map/ppermute | solution.py:178
  84.3 0.7 slice_bitcast_fusion.1
  85.0 2.8 %collective-permute-done.5.refs_7_ = f32[2056,128]{1,0:T(8,128)} collective-permute-done((f32[2056,128]{1,0:T(8,128)}, f32[2056,128]{1,0:T(8,128)}, u32[]{:S(2)}, u32[]{:S(2)}) %collective-permute-start.5) | collective-permute-done | bytes 1052704 | tf_op jit(solution)/shard_map/ppermute | solution.py:178
  87.8 0.7 slice_bitcast_fusion
  88.6 0.5 convert_element_type.28.right_keys
  89.1 6.1 %match_lists.1.matches = s32[528]{0:T(1024)} custom-call(s32[16]{0:T(128)} %get-tuple-element.41.rows_ref, s32[16]{0:T(128)} %get-tuple-element.42.cols_ref, s32[256]{0:T(256)} %all-reduce.2.left_keys, s32[128]{0:T(128)} %convert_element_type.28.right_keys, s32[32]{0:T(128)} %fusion.14.right_base), custom_call_target="tpu_custom_call" | custom-call | tf_op jit(solution)/shard_map/match_lists/pallas_call | solution.py:44
  95.2 4.5 %split_panel.1.panel = bf16[128,128,256]{2,1,0:T(8,128)(2,1)S(1)} custom-call(f32[2056,128]{1,0:T(8,128)S(1)} %pad_maximum_fusion.refs_0_, f32[2056,128]{1,0:T(8,128)S(1)} %pad_maximum_fusion.1.refs_1_, f32[2056,128]{1,0:T(8,128)S(1)} %collective-permute-done.refs_2_, f32[2056,128]{1,0:T(8,128)} %collective-permute-done.1.refs_3_, ...), custom_call_target="tpu_custom_call" | custom-call | tf_op jit(solution)/shard_map/split_panel/pallas_call | solution.py:72
  99.8 3.2 %copy-done = bf16[128,128,256]{2,1,0:T(8,128)(2,1)} copy-done((bf16[128,128,256]{2,1,0:T(8,128)(2,1)}, bf16[128,128,256]{2,1,0:T(8,128)(2,1)S(1)}, u32[]{:S(2)}) %copy-start) | copy-done | bytes 8388632
  103.0 15.8 %all-gather.4.cloned.1.call-done = f32[256,1,1,128,128]{4,3,2,1,0:T(8,128)} async-done(((f32[8,1,1,128,128]{4,3,2,1,0:T(8,128)}), f32[256,1,1,128,128]{4,3,2,1,0:T(8,128)}) %all-gather.4.cloned.1.call-update) | async-done | bytes 16777232 | tf_op jit(solution)/shard_map/all_gather | solution.py:193
  118.7 6.3 %passed_blocks.1 = f32[4,128,128]{2,1,0:T(8,128)S(1)} custom-call(s32[528]{0:T(1024)S(1)} %copy-done.1, f32[256,128,128]{2,1,0:T(8,128)} %bitcast.38, bf16[128,128,256]{2,1,0:T(8,128)(2,1)} %copy-done), custom_call_target="tpu_custom_call" | custom-call | flops 1073741824 | bytes 8388608 | tf_op jit(solution)/shard_map/passed_blocks/pallas_call | solution.py:149
  125.1 6.4 %collective-permute-start.7 = (f32[4,128,128]{2,1,0:T(8,128)S(1)}, f32[4,128,128]{2,1,0:T(8,128)S(1)}, u32[]{:S(2)}, u32[]{:S(2)}) collective-permute-start(f32[4,128,128]{2,1,0:T(8,128)S(1)} %passed_blocks.1), channel_id=1, source_target_pairs={{0,1},{1,0},{2,3},{3,2},{4,7},{5,6},{6,5},{7,4},{8,9},{9,8},{10,11... | collective-permute-start | bytes 786440 | tf_op jit(solution)/shard_map/ppermute | solution.py:224
  131.4 5.5 %partner_blocks.1 = f32[4,128,128]{2,1,0:T(8,128)S(1)} custom-call(s32[528]{0:T(1024)S(1)} %copy-done.1, f32[256,128,128]{2,1,0:T(8,128)} %bitcast.39, bf16[128,128,256]{2,1,0:T(8,128)(2,1)} %copy-done), custom_call_target="tpu_custom_call" | custom-call | flops 1073741824 | bytes 8388608 | tf_op jit(solution)/shard_map/partner_blocks/pallas_call | solution.py:149
  137.0 3.1 %collective-permute-start.6 = (f32[4,128,128]{2,1,0:T(8,128)S(1)}, f32[4,128,128]{2,1,0:T(8,128)S(1)}, u32[]{:S(2)}, u32[]{:S(2)}) collective-permute-start(f32[4,128,128]{2,1,0:T(8,128)S(1)} %partner_blocks.1), channel_id=1, source_target_pairs={{0,1},{1,0},{2,3},{3,2},{4,7},{5,6},{6,5},{7,4},{8,9},{9,8},{10,11... | collective-permute-start | bytes 786440 | tf_op jit(solution)/shard_map/ppermute | solution.py:224
  140.1 5.9 %second_blocks.1 = f32[4,128,128]{2,1,0:T(8,128)S(1)} custom-call(s32[528]{0:T(1024)S(1)} %copy-done.1, f32[256,128,128]{2,1,0:T(8,128)} %bitcast.40, bf16[128,128,256]{2,1,0:T(8,128)(2,1)} %copy-done), custom_call_target="tpu_custom_call" | custom-call | flops 1073741824 | bytes 8388608 | tf_op jit(solution)/shard_map/second_blocks/pallas_call | solution.py:149
  146.0 8.0 %collective-permute-start.8 = (f32[4,128,128]{2,1,0:T(8,128)S(1)}, f32[4,128,128]{2,1,0:T(8,128)S(1)}, u32[]{:S(2)}, u32[]{:S(2)}) collective-permute-start(f32[4,128,128]{2,1,0:T(8,128)S(1)} %add.96), channel_id=1, source_target_pairs={{0,3},{1,2},{2,1},{3,0},{4,5},{5,4},{6,7},{7,6},{8,11},{9,10},{10,... | collective-permute-start | bytes 786440 | tf_op jit(solution)/shard_map/ppermute | solution.py:224
  154.0 6.6 %own_blocks.1 = f32[4,128,128]{2,1,0:T(8,128)S(1)} custom-call(s32[528]{0:T(1024)S(1)} %copy-done.1, f32[256,128,128]{2,1,0:T(8,128)} %bitcast.41, bf16[128,128,256]{2,1,0:T(8,128)(2,1)} %copy-done), custom_call_target="tpu_custom_call" | custom-call | flops 1073741824 | bytes 8388608 | tf_op jit(solution)/shard_map/own_blocks/pallas_call | solution.py:149
  160.6 6.9 %collective-permute-done.8 = f32[4,128,128]{2,1,0:T(8,128)S(1)} collective-permute-done((f32[4,128,128]{2,1,0:T(8,128)S(1)}, f32[4,128,128]{2,1,0:T(8,128)S(1)}, u32[]{:S(2)}, u32[]{:S(2)}) %collective-permute-start.8) | collective-permute-done | bytes 262176 | tf_op jit(solution)/shard_map/ppermute | solution.py:224
  167.5 0.3 fusion.1
  167.8 10.8 %collective-permute-start.9 = (f32[4,128]{1,0:T(4,128)S(1)}, f32[4,128]{1,0:T(4,128)S(1)}, u32[]{:S(2)}, u32[]{:S(2)}) collective-permute-start(f32[4,128]{1,0:T(4,128)S(1)} %fusion.1), channel_id=1, source_target_pairs={{0,1},{1,0},{2,3},{3,2},{4,7},{5,6},{6,5},{7,4},{8,9},{9,8},{10,11... | collective-permute-start | bytes 6152 | tf_op jit(solution)/shard_map/ppermute | solution.py:224
  178.6 1.6 collective-permute-done.9
  180.1 5.4 %collective-permute-start.10 = (f32[4,128]{1,0:T(4,128)S(1)}, f32[4,128]{1,0:T(4,128)S(1)}, u32[]{:S(2)}, u32[]{:S(2)}) collective-permute-start(f32[4,128]{1,0:T(4,128)S(1)} %add.98), channel_id=1, source_target_pairs={{0,3},{1,2},{2,1},{3,0},{4,5},{5,4},{6,7},{7,6},{8,11},{9,10},{10,... | collective-permute-start | bytes 6152 | tf_op jit(solution)/shard_map/ppermute | solution.py:224
  185.5 4.0 %collective-permute-done.10 = f32[4,128]{1,0:T(4,128)S(1)} collective-permute-done((f32[4,128]{1,0:T(4,128)S(1)}, f32[4,128]{1,0:T(4,128)S(1)}, u32[]{:S(2)}, u32[]{:S(2)}) %collective-permute-start.10) | collective-permute-done | bytes 2080 | tf_op jit(solution)/shard_map/ppermute | solution.py:224
  189.5 9.6 %psum.7 = f32[4,128]{1,0:T(4,128)S(1)} all-reduce(f32[4,128]{1,0:T(4,128)S(1)} %add.99), channel_id=1, replica_groups=mesh['row'=4,'col'=32,'layer'=4] {'row'}, use_global_device_ids=true, to_apply=%region_1.0 | all-reduce | flops 512 | bytes 4096 | tf_op jit(solution)/shard_map/psum | solution.py:253
  199.1 0.2 convolution_divide_fusion
  199.3 0.8 multiply_bitcast_fusion
  (35 shorter events, 0.8 us)
Async XLA Ops:
  6.5 112.2 %all-gather.4.cloned.1.call-start = ((), (), s32[]{:S(2)}) async-start(), calls=%async_computation | async-start | bytes 17301504 | tf_op jit(solution)/shard_map/all_gather | solution.py:193
  11.0 29.2 %collective-permute-start = (f32[2056,128]{1,0:T(8,128)S(1)}, f32[2056,128]{1,0:T(8,128)S(1)}, u32[]{:S(2)}, u32[]{:S(2)}) collective-permute-start(f32[2056,128]{1,0:T(8,128)S(1)} %pad_maximum_fusion.refs_0_), channel_id=1, source_target_pairs={{0,128},{128,256},{256,384},{384,0},{1,129},{129,257},{257,385},{3... | collective-permute-start | bytes 3158024 | tf_op jit(solution)/shard_map/ppermute | solution.py:178
  14.6 10.9 %copy-start.5 = (s32[8]{0:T(128)S(1)}, s32[8]{0:T(128)}, u32[]{:S(2)}) copy-start(s32[8]{0:T(128)} %constant.92.clone) | copy-start | bytes 100
  14.6 11.7 %copy-start.2 = (s32[1,1,16]{2,1,0:T(1,128)S(1)}, s32[1,1,16]{2,1,0:T(1,128)}, u32[]{:S(2)}) copy-start(s32[1,1,16]{2,1,0:T(1,128)} %param.16) | copy-start | bytes 196
  14.6 11.7 %copy-start.3 = (s32[1,1,16]{2,1,0:T(1,128)S(1)}, s32[1,1,16]{2,1,0:T(1,128)}, u32[]{:S(2)}) copy-start(s32[1,1,16]{2,1,0:T(1,128)} %param.15) | copy-start | bytes 196
  14.7 34.4 %copy-start.4 = (s32[8,1,1]{0,2,1:T(1,128)S(1)}, s32[8,1,1]{0,2,1:T(1,128)}, u32[]{:S(2)}) copy-start(s32[8,1,1]{0,2,1:T(1,128)} %param.12) | copy-start | bytes 100
  16.0 28.2 %collective-permute-start.3 = (f32[2056,128]{1,0:T(8,128)S(1)}, f32[2056,128]{1,0:T(8,128)}, u32[]{:S(2)}, u32[]{:S(2)}) collective-permute-start(f32[2056,128]{1,0:T(8,128)S(1)} %pad_maximum_fusion.1.refs_1_), channel_id=1, source_target_pairs={{0,384},{128,0},{256,128},{384,256},{1,385},{129,1},{257,129},{385... | collective-permute-start | bytes 3158024 | tf_op jit(solution)/shard_map/ppermute | solution.py:178
  19.7 47.3 %collective-permute-start.2 = (f32[2056,128]{1,0:T(8,128)S(1)}, f32[2056,128]{1,0:T(8,128)}, u32[]{:S(2)}, u32[]{:S(2)}) collective-permute-start(f32[2056,128]{1,0:T(8,128)S(1)} %pad_maximum_fusion.refs_0_), channel_id=1, source_target_pairs={{0,384},{128,0},{256,128},{384,256},{1,385},{129,1},{257,129},{385... | collective-permute-start | bytes 3158024 | tf_op jit(solution)/shard_map/ppermute | solution.py:178
  23.1 44.5 %collective-permute-start.1 = (f32[2056,128]{1,0:T(8,128)S(1)}, f32[2056,128]{1,0:T(8,128)}, u32[]{:S(2)}, u32[]{:S(2)}) collective-permute-start(f32[2056,128]{1,0:T(8,128)S(1)} %pad_maximum_fusion.1.refs_1_), channel_id=1, source_target_pairs={{0,128},{128,256},{256,384},{384,0},{1,129},{129,257},{257,385},{3... | collective-permute-start | bytes 3158024 | tf_op jit(solution)/shard_map/ppermute | solution.py:178
  41.6 42.7 %collective-permute-start.4 = (f32[2056,128]{1,0:T(8,128)S(1)}, f32[2056,128]{1,0:T(8,128)}, u32[]{:S(2)}, u32[]{:S(2)}) collective-permute-start(f32[2056,128]{1,0:T(8,128)S(1)} %collective-permute-done.refs_2_), channel_id=1, source_target_pairs={{0,128},{128,256},{256,384},{384,0},{1,129},{129,257},{257,385},{3... | collective-permute-start | bytes 3158024 | tf_op jit(solution)/shard_map/ppermute | solution.py:178
  44.2 43.7 %collective-permute-start.5 = (f32[2056,128]{1,0:T(8,128)}, f32[2056,128]{1,0:T(8,128)}, u32[]{:S(2)}, u32[]{:S(2)}) collective-permute-start(f32[2056,128]{1,0:T(8,128)} %collective-permute-done.3.refs_5_), channel_id=1, source_target_pairs={{0,384},{128,0},{256,128},{384,256},{1,385},{129,1},{257,129},{385... | collective-permute-start | bytes 3158024 | tf_op jit(solution)/shard_map/ppermute | solution.py:178
  95.2 23.5 %copy-start.1 = (s32[528]{0:T(1024)S(1)}, s32[528]{0:T(1024)}, u32[]{:S(2)}) copy-start(s32[528]{0:T(1024)} %match_lists.1.matches) | copy-start | bytes 6340
  99.7 3.2 %copy-start = (bf16[128,128,256]{2,1,0:T(8,128)(2,1)}, bf16[128,128,256]{2,1,0:T(8,128)(2,1)S(1)}, u32[]{:S(2)}) copy-start(bf16[128,128,256]{2,1,0:T(8,128)(2,1)S(1)} %split_panel.1.panel) | copy-start | bytes 25165828
  125.1 20.9 %collective-permute-start.7 = (f32[4,128,128]{2,1,0:T(8,128)S(1)}, f32[4,128,128]{2,1,0:T(8,128)S(1)}, u32[]{:S(2)}, u32[]{:S(2)}) collective-permute-start(f32[4,128,128]{2,1,0:T(8,128)S(1)} %passed_blocks.1), channel_id=1, source_target_pairs={{0,1},{1,0},{2,3},{3,2},{4,7},{5,6},{6,5},{7,4},{8,9},{9,8},{10,11... | collective-permute-start | bytes 786440 | tf_op jit(solution)/shard_map/ppermute | solution.py:224
  137.0 23.6 %collective-permute-start.6 = (f32[4,128,128]{2,1,0:T(8,128)S(1)}, f32[4,128,128]{2,1,0:T(8,128)S(1)}, u32[]{:S(2)}, u32[]{:S(2)}) collective-permute-start(f32[4,128,128]{2,1,0:T(8,128)S(1)} %partner_blocks.1), channel_id=1, source_target_pairs={{0,1},{1,0},{2,3},{3,2},{4,7},{5,6},{6,5},{7,4},{8,9},{9,8},{10,11... | collective-permute-start | bytes 786440 | tf_op jit(solution)/shard_map/ppermute | solution.py:224
  146.0 21.5 %collective-permute-start.8 = (f32[4,128,128]{2,1,0:T(8,128)S(1)}, f32[4,128,128]{2,1,0:T(8,128)S(1)}, u32[]{:S(2)}, u32[]{:S(2)}) collective-permute-start(f32[4,128,128]{2,1,0:T(8,128)S(1)} %add.96), channel_id=1, source_target_pairs={{0,3},{1,2},{2,1},{3,0},{4,5},{5,4},{6,7},{7,6},{8,11},{9,10},{10,... | collective-permute-start | bytes 786440 | tf_op jit(solution)/shard_map/ppermute | solution.py:224
  167.8 12.4 %collective-permute-start.9 = (f32[4,128]{1,0:T(4,128)S(1)}, f32[4,128]{1,0:T(4,128)S(1)}, u32[]{:S(2)}, u32[]{:S(2)}) collective-permute-start(f32[4,128]{1,0:T(4,128)S(1)} %fusion.1), channel_id=1, source_target_pairs={{0,1},{1,0},{2,3},{3,2},{4,7},{5,6},{6,5},{7,4},{8,9},{9,8},{10,11... | collective-permute-start | bytes 6152 | tf_op jit(solution)/shard_map/ppermute | solution.py:224
  180.1 9.4 %collective-permute-start.10 = (f32[4,128]{1,0:T(4,128)S(1)}, f32[4,128]{1,0:T(4,128)S(1)}, u32[]{:S(2)}, u32[]{:S(2)}) collective-permute-start(f32[4,128]{1,0:T(4,128)S(1)} %add.98), channel_id=1, source_target_pairs={{0,3},{1,2},{2,1},{3,0},{4,5},{5,4},{6,7},{7,6},{8,11},{9,10},{10,... | collective-permute-start | bytes 6152 | tf_op jit(solution)/shard_map/ppermute | solution.py:224
Sparse Core Ops, SparseCore 0:
  9.5 109.1 all-gather.3
